TPU v7x, 32 devices: a whole 2x2x4 slice. The times are simulated.
32 devices in a mesh: dp: 4 (over y, x), mp: 8 (over z, core).
Axes of the slice: x: 2, y: 2, z: 4, core: 2. Of those that a mesh axis runs over, the one named last changes fastest.
Arguments:
- tokens: bfloat16 [8192, 2048], P(('dp', 'mp')), may hold values from -6 to 6
- seg_len: int32 [4], P('dp'), may hold values from 1024 to 1998, as said below
- cotangent: bfloat16 [8192, 2048], P(('dp', 'mp')), may hold values from -6 to 6
- ln_gain: float32 [2, 2048], replicated, may hold values from 0.5 to 1.5
- qkv_weight: float32 [2048, 6144], P('dp', 'mp'), may hold values from -0.125 to 0.125
- out_weight: float32 [2048, 2048], P('dp', 'mp'), may hold values from -1 to 1
- up_weight: float32 [2048, 8192], P('dp', 'mp'), may hold values from -0.125 to 0.125
- down_weight: float32 [8192, 2048], P('mp', 'dp'), may hold values from -0.0625 to 0.0625
- left_qkv: float32 [2, 4, 32, 512, 512], P(None, 'dp', 'mp'), as said below
- right_qkv: float32 [2, 4, 32, 192, 192], P(None, 'dp', 'mp'), as said below
- left_out: float32 [2, 4, 32, 512, 512], P(None, 'dp', 'mp'), as said below
- right_out: float32 [2, 4, 32, 64, 64], P(None, 'dp', 'mp'), as said below
- left_up: float32 [2, 4, 32, 512, 512], P(None, 'dp', 'mp'), as said below
- right_up: float32 [2, 4, 32, 256, 256], P(None, 'dp', 'mp'), as said below
- left_down: float32 [2, 32, 4, 256, 256], P(None, 'mp', 'dp'), as said below
- right_down: float32 [2, 32, 4, 512, 512], P(None, 'mp', 'dp'), as said below
Outputs:
- block_out: bfloat16 [8192, 2048], P(('dp', 'mp'))
- input_grad: float32 [8192, 2048], P(('dp', 'mp'))
- summaries: float32 [4, 50, 2048], P('dp', None, 'mp')
- gain_grads: float32 [2, 2048], replicated
- new_gains: float32 [2, 2048], replicated
- grad_qkv: float32 [2048, 6144], P('dp', 'mp')
- grad_out: float32 [2048, 2048], P('dp', 'mp')
- grad_up: float32 [2048, 8192], P('dp', 'mp')
- grad_down: float32 [8192, 2048], P('mp', 'dp')
- new_qkv: float32 [2048, 6144], P('dp', 'mp')
- new_out: float32 [2048, 2048], P('dp', 'mp')
- new_up: float32 [2048, 8192], P('dp', 'mp')
- new_down: float32 [8192, 2048], P('mp', 'dp')
- new_left_qkv: float32 [4, 32, 512, 512], P('dp', 'mp')
- new_right_qkv: float32 [4, 32, 192, 192], P('dp', 'mp')
- new_left_out: float32 [4, 32, 512, 512], P('dp', 'mp')
- new_right_out: float32 [4, 32, 64, 64], P('dp', 'mp')
- new_left_up: float32 [4, 32, 512, 512], P('dp', 'mp')
- new_right_up: float32 [4, 32, 256, 256], P('dp', 'mp')
- new_left_down: float32 [32, 4, 256, 256], P('mp', 'dp')
- new_right_down: float32 [32, 4, 512, 512], P('mp', 'dp')
Inputs may be any that keep to these rules, and one draw needn't show every extreme that they name: Segment s holds seg_len[s] real tokens in its first slots and its 50 summary slots right after them; the remaining slots are padding. One segment has exactly 1998 tokens and another exactly 1024. `left_qkv`: index 0 holds each tile's statistics, index 1 a given inverse fourth root; both are symmetric. `right_qkv`: as left_qkv. `left_out`: as left_qkv. `right_out`: as left_qkv. `left_up`: as left_qkv. `right_up`: as left_qkv. `left_down`: as left_qkv. `right_down`: as left_qkv.
All inputs are finite; a program needn't handle non-finite values.
Results may differ from a plain program's by a relative error of at most 0.017.
Values may be sent and summed in bfloat16 or wider, within the bound.
A program may use at most 384 MiB of HBM per device.

v0:
```python
import math

import jax
import jax.numpy as jnp
from jax import lax
from jax.sharding import PartitionSpec as P

HD = 64
SLOT = 2048
NSUM = 50
BLOCK = 512
FBLK = 256


NORM_EPSILON = 1e-05
SHAMPOO_RATE = 0.5
GAIN_RATE = 0.1
DECAY = 0.5
HIGHEST = lax.Precision.HIGHEST
MASKED_SCORE = -1e30


def layer_norm(value, gain):
    mean = jnp.mean(value, axis=-1, keepdims=True)
    centred = value - mean
    spread = jnp.mean(centred * centred, axis=-1, keepdims=True)
    return centred * lax.rsqrt(spread + NORM_EPSILON) * gain


def gelu_tanh(value):
    return jax.nn.gelu(value, approximate=True)


def masked_scores(queries, key_rows, key_limit):
    scale = 1.0 / math.sqrt(queries.shape[-1])
    scores = jnp.einsum("qd,kd->qk", queries, key_rows, preferred_element_type=jnp.float32) * scale
    positions = jnp.arange(queries.shape[0])
    allowed = (positions[None, :] <= positions[:, None]) & (positions[None, :] < key_limit)
    return jnp.where(allowed, scores, MASKED_SCORE)


def attend_forward(bundle):
    queries, key_rows, values, key_limit = bundle
    scores = masked_scores(queries, key_rows, key_limit)
    row_top = jnp.max(scores, axis=-1, keepdims=True)
    exponent = jnp.exp(scores - row_top)
    row_total = jnp.sum(exponent, axis=-1, keepdims=True)
    attn_probs = (exponent / row_total).astype(jnp.bfloat16)
    context = jnp.dot(attn_probs, values, preferred_element_type=jnp.float32).astype(jnp.bfloat16)
    return (context, (row_top + jnp.log(row_total))[:, 0])


def attend_backward(bundle):
    queries, key_rows, values, key_limit, incoming, log_sums = bundle
    scale = 1.0 / math.sqrt(queries.shape[-1])
    scores = masked_scores(queries, key_rows, key_limit)
    attn_probs = jnp.exp(scores - log_sums[:, None])
    probs_low = attn_probs.astype(jnp.bfloat16)
    d_values = jnp.einsum("qk,qd->kd", probs_low, incoming, preferred_element_type=jnp.float32)
    d_probs = jnp.einsum("qd,kd->qk", incoming, values, preferred_element_type=jnp.float32)
    inner = jnp.sum(attn_probs * d_probs, axis=-1, keepdims=True)
    d_scores = (attn_probs * (d_probs - inner)).astype(jnp.bfloat16)
    d_queries = jnp.dot(d_scores, key_rows, preferred_element_type=jnp.float32) * scale
    d_keys = jnp.einsum("qk,qd->kd", d_scores, queries, preferred_element_type=jnp.float32) * scale
    return (
        d_queries.astype(jnp.bfloat16),
        d_keys.astype(jnp.bfloat16),
        d_values.astype(jnp.bfloat16),
    )


def precondition(weight, grad, stats_left, stats_right, tile_rows, tile_cols):
    rows_all, cols_all = grad.shape
    tiles = grad.reshape(
        rows_all // tile_rows, tile_rows, cols_all // tile_cols, tile_cols
    ).transpose(0, 2, 1, 3)
    left_new = DECAY * stats_left[0] + (1.0 - DECAY) * jnp.einsum(
        "abik,abjk->abij", tiles, tiles, precision=HIGHEST
    )
    right_new = DECAY * stats_right[0] + (1.0 - DECAY) * jnp.einsum(
        "abki,abkj->abij", tiles, tiles, precision=HIGHEST
    )
    stepped = jnp.einsum("abij,abjk->abik", stats_left[1], tiles, precision=HIGHEST)
    stepped = jnp.einsum("abik,abkl->abil", stepped, stats_right[1], precision=HIGHEST)
    stepped = stepped.transpose(0, 2, 1, 3).reshape(rows_all, cols_all)
    return (weight - SHAMPOO_RATE * stepped, left_new, right_new)


def body(
    tokens,
    seg_len,
    cotangent,
    ln_gain,
    qkv_weight,
    out_weight,
    up_weight,
    down_weight,
    left_qkv,
    right_qkv,
    left_out,
    right_out,
    left_up,
    right_up,
    left_down,
    right_down,
):
    row_count, features = tokens.shape
    mp_count = lax.axis_size("mp")
    mp_index = lax.axis_index("mp")
    seg_count = seg_len.shape[0]
    group_rows = row_count * mp_count
    inputs = tokens.astype(jnp.float32)
    qkv_part, out_part, up_part, down_part = (
        lax.all_gather(qkv_weight.astype(jnp.bfloat16), "dp", axis=0, tiled=True),
        lax.all_gather(out_weight.astype(jnp.bfloat16), "dp", axis=0, tiled=True),
        lax.all_gather(up_weight.astype(jnp.bfloat16), "dp", axis=0, tiled=True),
        lax.all_gather(down_weight.astype(jnp.bfloat16), "dp", axis=1, tiled=True),
    )
    positions = mp_index * row_count + jnp.arange(row_count)
    owner_seg = positions // SLOT
    own_length = jnp.sum(
        jnp.where(owner_seg[:, None] == jnp.arange(seg_count)[None, :], seg_len[None, :], 0), axis=1
    )
    valid = positions % SLOT < own_length + NSUM
    normed_one = layer_norm(inputs, ln_gain[0]).astype(jnp.bfloat16)
    gathered = lax.all_gather(normed_one, "mp", axis=0, tiled=True)
    qkv_rows = jnp.dot(gathered, qkv_part, preferred_element_type=jnp.float32).astype(jnp.bfloat16)
    head_count = qkv_part.shape[1] // (3 * HD)
    parted = (
        qkv_rows.reshape(seg_count, SLOT, head_count, 3, HD)
        .transpose(3, 0, 2, 1, 4)
        .reshape(3, seg_count * head_count, SLOT, HD)
    )
    key_limits = jnp.repeat(seg_len + NSUM, head_count)
    context, log_sums = lax.map(attend_forward, (parted[0], parted[1], parted[2], key_limits))
    ctx_heads = (
        context.reshape(seg_count, head_count, SLOT, HD)
        .transpose(0, 2, 1, 3)
        .reshape(group_rows, head_count * HD)
    )
    ctx_rows = lax.all_to_all(ctx_heads, "mp", split_axis=0, concat_axis=1, tiled=True)
    out_full, up_full, down_full = (
        lax.all_gather(out_part, "mp", axis=1, tiled=True),
        lax.all_gather(up_part, "mp", axis=1, tiled=True),
        lax.all_gather(down_part, "mp", axis=0, tiled=True),
    )
    resid = inputs + jnp.dot(ctx_rows, out_full, preferred_element_type=jnp.float32)
    normed_two = layer_norm(resid, ln_gain[1]).astype(jnp.bfloat16)
    upstream = jnp.where(valid[:, None], cotangent, jnp.zeros_like(cotangent))
    pre_act = jnp.dot(normed_two, up_full, preferred_element_type=jnp.float32)
    hidden = gelu_tanh(pre_act).astype(jnp.bfloat16)
    ffn_out = jnp.dot(hidden, down_full, preferred_element_type=jnp.float32)
    d_hidden = jnp.einsum("rd,fd->rf", upstream, down_full, preferred_element_type=jnp.float32)
    d_pre = jax.vjp(gelu_tanh, pre_act)[1](d_hidden)[0].astype(jnp.bfloat16)
    grad_down_part = jnp.einsum("rf,rd->fd", hidden, upstream, preferred_element_type=jnp.float32)
    grad_up_part = jnp.einsum("rd,rf->df", normed_two, d_pre, preferred_element_type=jnp.float32)
    d_normed_two = jnp.einsum("rf,df->rd", d_pre, up_full, preferred_element_type=jnp.float32)
    block_out = (resid + ffn_out).astype(jnp.bfloat16)
    norm_back_two = jax.vjp(layer_norm, resid, ln_gain[1])[1]
    d_resid_ln, d_gain_two = norm_back_two(d_normed_two)
    d_resid = upstream.astype(jnp.float32) + d_resid_ln
    d_resid_low = d_resid.astype(jnp.bfloat16)
    grad_out_part = jnp.einsum(
        "rd,re->de", ctx_rows, d_resid_low, preferred_element_type=jnp.float32
    )
    d_context = jnp.einsum(
        "re,de->rd", d_resid_low, out_full, preferred_element_type=jnp.float32
    ).astype(jnp.bfloat16)
    d_ctx_heads = lax.all_to_all(d_context, "mp", split_axis=1, concat_axis=0, tiled=True)
    d_ctx_items = (
        d_ctx_heads.reshape(seg_count, SLOT, head_count, HD)
        .transpose(0, 2, 1, 3)
        .reshape(seg_count * head_count, SLOT, HD)
    )
    d_queries, d_keys, d_values = lax.map(
        attend_backward, (parted[0], parted[1], parted[2], key_limits, d_ctx_items, log_sums)
    )
    d_qkv = (
        jnp.stack([d_queries, d_keys, d_values])
        .reshape(3, seg_count, head_count, SLOT, HD)
        .transpose(1, 3, 2, 0, 4)
        .reshape(group_rows, head_count * 3 * HD)
    )
    grad_qkv_part = jnp.einsum("gd,gc->dc", gathered, d_qkv, preferred_element_type=jnp.float32)
    d_normed_one = lax.psum_scatter(
        jnp.einsum("gc,dc->gd", d_qkv, qkv_part, preferred_element_type=jnp.float32).astype(
            jnp.bfloat16
        ),
        "mp",
        scatter_dimension=0,
        tiled=True,
    ).astype(jnp.float32)
    norm_back_one = jax.vjp(layer_norm, inputs, ln_gain[0])[1]
    d_input_ln, d_gain_one = norm_back_one(d_normed_one)
    input_grad = d_resid + d_input_ln
    grad_out_cols, grad_up_cols, grad_down_rows = (
        lax.psum_scatter(
            grad_out_part.astype(jnp.bfloat16), "mp", scatter_dimension=1, tiled=True
        ).astype(jnp.float32),
        lax.psum_scatter(
            grad_up_part.astype(jnp.bfloat16), "mp", scatter_dimension=1, tiled=True
        ).astype(jnp.float32),
        lax.psum_scatter(
            grad_down_part.astype(jnp.bfloat16), "mp", scatter_dimension=0, tiled=True
        ).astype(jnp.float32),
    )
    grad_qkv, grad_out, grad_up, grad_down = (
        lax.psum_scatter(
            grad_qkv_part.astype(jnp.bfloat16), "dp", scatter_dimension=0, tiled=True
        ).astype(jnp.float32),
        lax.psum_scatter(
            grad_out_cols.astype(jnp.bfloat16), "dp", scatter_dimension=0, tiled=True
        ).astype(jnp.float32),
        lax.psum_scatter(
            grad_up_cols.astype(jnp.bfloat16), "dp", scatter_dimension=0, tiled=True
        ).astype(jnp.float32),
        lax.psum_scatter(
            grad_down_rows.astype(jnp.bfloat16), "dp", scatter_dimension=1, tiled=True
        ).astype(jnp.float32),
    )
    slot_index = (jnp.arange(seg_count) * SLOT + seg_len)[:, None] + jnp.arange(NSUM)[None, :]
    selector = (slot_index.reshape(-1)[:, None] == positions[None, :]).astype(jnp.bfloat16)
    picked = jnp.dot(selector, block_out, preferred_element_type=jnp.float32).reshape(
        seg_count, NSUM, features
    )
    owned_vectors = lax.psum_scatter(
        picked.astype(jnp.bfloat16), "mp", scatter_dimension=2, tiled=True
    ).astype(jnp.float32)
    owned_width = owned_vectors.shape[2]
    col_sums = jnp.sum(owned_vectors, axis=(0, 1))
    spread_sums = (
        (jnp.arange(mp_count) == mp_index).astype(jnp.float32)[:, None] * col_sums[None, :]
    ).reshape(features)
    gain_parts = jnp.stack([d_gain_one, d_gain_two])
    gain_grads, total_cols, total_squares = lax.psum(
        (gain_parts, spread_sums, jnp.sum(owned_vectors * owned_vectors)), ("dp", "mp")
    )
    vector_count = seg_count * lax.axis_size("dp") * NSUM
    centre_all = total_cols / vector_count
    centre = lax.dynamic_slice_in_dim(centre_all, mp_index * owned_width, owned_width, 0)
    variance = total_squares / (vector_count * features) - jnp.mean(centre_all * centre_all)
    summaries = (owned_vectors - centre) * lax.rsqrt(variance + NORM_EPSILON)
    new_gains = ln_gain - GAIN_RATE * gain_grads * lax.rsqrt(
        jnp.mean(gain_grads * gain_grads, axis=-1, keepdims=True) + 1e-06
    )
    new_qkv, new_left_qkv, new_right_qkv = precondition(
        qkv_weight, grad_qkv, left_qkv, right_qkv, BLOCK, 3 * HD
    )
    new_out, new_left_out, new_right_out = precondition(
        out_weight, grad_out, left_out, right_out, BLOCK, HD
    )
    new_up, new_left_up, new_right_up = precondition(
        up_weight, grad_up, left_up, right_up, BLOCK, FBLK
    )
    new_down, new_left_down, new_right_down = precondition(
        down_weight, grad_down, left_down, right_down, FBLK, BLOCK
    )
    return (
        block_out,
        input_grad,
        summaries,
        gain_grads,
        new_gains,
        grad_qkv,
        grad_out,
        grad_up,
        grad_down,
        new_qkv,
        new_out,
        new_up,
        new_down,
        new_left_qkv,
        new_right_qkv,
        new_left_out,
        new_right_out,
        new_left_up,
        new_right_up,
        new_left_down,
        new_right_down,
    )


def solution(mesh):
    in_specs = (
        P(("dp", "mp"), None),
        P("dp"),
        P(("dp", "mp"), None),
        P(),
        P("dp", "mp"),
        P("dp", "mp"),
        P("dp", "mp"),
        P("mp", "dp"),
        P(None, "dp", "mp", None, None),
        P(None, "dp", "mp", None, None),
        P(None, "dp", "mp", None, None),
        P(None, "dp", "mp", None, None),
        P(None, "dp", "mp", None, None),
        P(None, "dp", "mp", None, None),
        P(None, "mp", "dp", None, None),
        P(None, "mp", "dp", None, None),
    )
    out_specs = (
        P(("dp", "mp"), None),
        P(("dp", "mp"), None),
        P("dp", None, "mp"),
        P(),
        P(),
        P("dp", "mp"),
        P("dp", "mp"),
        P("dp", "mp"),
        P("mp", "dp"),
        P("dp", "mp"),
        P("dp", "mp"),
        P("dp", "mp"),
        P("mp", "dp"),
        P("dp", "mp", None, None),
        P("dp", "mp", None, None),
        P("dp", "mp", None, None),
        P("dp", "mp", None, None),
        P("dp", "mp", None, None),
        P("dp", "mp", None, None),
        P("mp", "dp", None, None),
        P("mp", "dp", None, None),
    )
    return jax.shard_map(body, mesh=mesh, in_specs=in_specs, out_specs=out_specs, check_vma=False)
```

profile of v0, /device:TPU:0, one launch (start us, length us, event | category | flops | bytes accessed | tf_op | source)
XLA Modules:
  0.0 2159.2 jit_solution(2445036093157223368)
XLA Ops:
  16.5 23.4 %all-gather.13.cloned.1.call-done = bf16[2048,256]{1,0:T(8,128)(2,1)} async-done(((bf16[512,256]{1,0:T(8,128)(2,1)}), bf16[2048,256]{1,0:T(8,128)(2,1)}) %all-gather.13.cloned.1.call-update) | async-done | bytes 1048592 | tf_op jit(solution)/shard_map/all_gather | solution.py:115
  39.9 55.1 %all-gather.17.cloned.1.call-done = bf16[2048,1024]{1,0:T(8,128)(2,1)} async-done(((bf16[512,1024]{1,0:T(8,128)(2,1)}), bf16[2048,1024]{1,0:T(8,128)(2,1)}) %all-gather.17.cloned.1.call-update) | async-done | bytes 4194320 | tf_op jit(solution)/shard_map/all_gather | solution.py:116
  95.7 45.7 %all-gather.11.cloned.1.call-done = bf16[2048,768]{1,0:T(8,128)(2,1)} async-done(((bf16[512,768]{1,0:T(8,128)(2,1)}), bf16[2048,768]{1,0:T(8,128)(2,1)}) %all-gather.11.cloned.1.call-update) | async-done | bytes 3145744 | tf_op jit(solution)/shard_map/all_gather | solution.py:114
  141.4 84.1 %all-gather.9.cloned.1.call-done = bf16[2048,2048]{1,0:T(8,128)(2,1)} async-done(((bf16[256,2048]{1,0:T(8,128)(2,1)}), bf16[2048,2048]{1,0:T(8,128)(2,1)}) %all-gather.9.cloned.1.call-update) | async-done | bytes 8388624 | tf_op jit(solution)/shard_map/all_gather | solution.py:126
  225.5 10.1 convolution_convert_fusion.4
  235.7 4.5 copy.105
  240.2 5.7 slice_bitcast_fusion.3
  246.5 87.9 %while.26 = (s32[]{:T(128)}, bf16[4,2048,64]{1,2,0:T(8,128)(2,1)S(1)}, f32[4,2048]{1,0:T(4,128)}, s32[4]{0:T(128)}, bf16[4,2048,64]{2,1,0:T(8,128)(2,1)}, /*inde...) while((s32[]{:T(128)}, bf16[4,2048,64]{1,2,0:T(8,128)(2,1)S(1)}, ...), condition=%wide.region_5.6_spmd, body=%wide.region_2.5_spmd.sunk | while | flops 1149370368 | bytes 52258936 | solution.py:135
  248.4 6.5 fusion.188
  254.9 8.1 fusion.189
  270.3 6.5 fusion.188
  276.8 8.1 fusion.189
  292.2 6.5 fusion.188
  298.6 8.1 fusion.189
  306.7 4.0 fusion.190
  314.0 6.6 fusion.188
  320.6 8.1 fusion.189
  335.9 4.2 all-to-all-start
  340.3 60.6 %all-to-all-done = bf16[8,256,256]{1,2,0:T(8,128)(2,1)} async-done(((bf16[8,256,256]{1,2,0:T(8,128)(2,1)}), bf16[8,256,256]{1,2,0:T(8,128)(2,1)}, u32[]{:S(2)}, u32[]{:S(2)}) %all-to-all-start) | async-done | bytes 1048608 | tf_op jit(solution)/shard_map/all_to_all | solution.py:141
  400.9 6.5 fusion.125
  407.8 211.0 %all-gather.19.cloned.1.call-done = bf16[2048,8192]{1,0:T(8,128)(2,1)} async-done(((bf16[2048,1024]{1,0:T(8,128)(2,1)}), bf16[2048,8192]{1,0:T(8,128)(2,1)}) %all-gather.19.cloned.1.call-update) | async-done | bytes 33554448 | tf_op jit(solution)/shard_map/all_gather | solution.py:144
  618.8 17.2 fusion.122
  636.0 21.0 convolution_convert_fusion
  657.1 323.8 %reduce-scatter.24.cloned.1.call-done = bf16[1024,2048]{1,0:T(8,128)(2,1)} async-done(((bf16[8192,2048]{1,0:T(8,128)(2,1)}), bf16[1024,2048]{1,0:T(8,128)(2,1)}) %reduce-scatter.24.cloned.1.call-update) | async-done | bytes 4194320 | tf_op jit(solution)/shard_map/reduce_scatter | solution.py:203
  981.0 54.2 %reduce-scatter.26.cloned.1.call-done = bf16[1024,512]{1,0:T(8,128)(2,1)} async-done(((bf16[1024,2048]{1,0:T(8,128)(2,1)}), bf16[1024,512]{1,0:T(8,128)(2,1)}) %reduce-scatter.26.cloned.1.call-update) | async-done | bytes 1048592 | tf_op jit(solution)/shard_map/reduce_scatter | solution.py:217
  1037.7 5.7 fusion.94
  1045.6 52.7 %all-gather.21.cloned.1.call-done = bf16[1024,2048]{1,0:T(8,128)(2,1)} async-done(((bf16[1024,512]{1,0:T(8,128)(2,1)}), bf16[1024,2048]{1,0:T(8,128)(2,1)}) %all-gather.21.cloned.1.call-update) | async-done | bytes 4194320 | tf_op jit(solution)/shard_map/all_gather | solution.py:117
  1098.4 290.0 %all-gather.23.cloned.1.call-done = bf16[8192,2048]{1,0:T(8,128)(2,1)} async-done(((bf16[1024,2048]{1,0:T(8,128)(2,1)}), bf16[8192,2048]{1,0:T(8,128)(2,1)}) %all-gather.23.cloned.1.call-update) | async-done | bytes 33554448 | tf_op jit(solution)/shard_map/all_gather | solution.py:145
  1388.4 20.7 fusion.62
  1409.1 18.0 multiply_reduce_fusion.1
  1432.1 6.9 convolution_convert_fusion.2
  1439.1 16.5 convolution_convert_fusion.1
  1456.8 6.8 convolution_convert_fusion.6
  1469.5 19.7 fusion.86
  1491.6 21.6 %all-to-all-done.1 = bf16[256,8,256]{0,2,1:T(8,128)(2,1)S(1)} async-done(((bf16[256,8,256]{0,2,1:T(8,128)(2,1)}), bf16[256,8,256]{0,2,1:T(8,128)(2,1)S(1)}, u32[]{:S(2)}, u32[]{:S(2)}) %all-to-all-start.1) | async-done | bytes 1048608 | tf_op jit(solution)/shard_map/all_to_all | solution.py:169
  1515.6 164.7 %while.27 = (s32[]{:T(128)}, bf16[4,2048,64]{1,2,0:T(8,128)(2,1)S(1)}, bf16[4,2048,64]{1,2,0:T(8,128)(2,1)S(1)}, bf16[4,2048,64]{1,2,0:T(8,128)(2,1)}, s32[4]{0:...) while((s32[]{:T(128)}, ...), condition=%wide.region_12.13_spmd, body=%wide.region_10.12_spmd.sunk | while | flops 2731147264 | bytes 129811592 | solution.py:175
  1516.0 9.1 fusion.199
  1527.8 11.2 multiply_reduce_fusion.7
  1539.0 8.3 multiply_convert_fusion.8
  1557.1 9.1 fusion.199
  1568.8 11.1 multiply_reduce_fusion.7
  1579.9 8.4 multiply_convert_fusion.8
  1598.1 9.1 fusion.199
  1609.9 11.1 multiply_reduce_fusion.7
  1621.0 8.3 multiply_convert_fusion.8
  1639.1 9.1 fusion.199
  1650.9 11.2 multiply_reduce_fusion.7
  1662.1 8.3 multiply_convert_fusion.8
  1683.6 10.6 convolution_convert_fusion.5
  1694.3 11.0 convolution_convert_fusion.3
  1706.1 168.5 %reduce-scatter.20.cloned.1.call-done = bf16[2048,1024]{1,0:T(8,128)(2,1)} async-done(((bf16[2048,8192]{1,0:T(8,128)(2,1)}), bf16[2048,1024]{1,0:T(8,128)(2,1)}) %reduce-scatter.20.cloned.1.call-update) | async-done | bytes 4194320 | tf_op jit(solution)/shard_map/reduce_scatter | solution.py:200
  1877.8 5.0 fusion.65
  1882.8 23.6 %reduce-scatter.12.cloned.1.call-done = bf16[1,50,256]{2,1,0:T(8,128)(2,1)} async-done(((bf16[1,50,2048]{2,1,0:T(8,128)(2,1)}), bf16[1,50,256]{2,1,0:T(8,128)(2,1)}) %reduce-scatter.12.cloned.1.call-update) | async-done | bytes 25616 | tf_op jit(solution)/shard_map/reduce_scatter | solution.py:226
  1907.8 44.1 %reduce-scatter.14.cloned.1.call-done = bf16[512,768]{1,0:T(8,128)(2,1)} async-done(((bf16[2048,768]{1,0:T(8,128)(2,1)}), bf16[512,768]{1,0:T(8,128)(2,1)}) %reduce-scatter.14.cloned.1.call-update) | async-done | bytes 786448 | tf_op jit(solution)/shard_map/reduce_scatter | solution.py:208
  1953.3 4.6 fusion.77
  1957.9 4.3 convolution_multiply_fusion.3
  1970.7 5.1 fusion.72
  1975.9 67.7 %reduce-scatter.10.cloned.1.call-done = bf16[256,2048]{1,0:T(8,128)(2,1)} async-done(((bf16[2048,2048]{1,0:T(8,128)(2,1)}), bf16[256,2048]{1,0:T(8,128)(2,1)}) %reduce-scatter.10.cloned.1.call-update) | async-done | bytes 1048592 | tf_op jit(solution)/shard_map/reduce_scatter | solution.py:185
  2047.7 38.8 %all-reduce = (f32[]{:T(128)}, f32[2048]{0:T(1024)S(1)}, f32[2,2048]{1,0:T(2,128)S(1)}) all-reduce(f32[]{:T(128)} %get-tuple-element.237, f32[2048]{0:T(1024)S(1)} %bitcast.354, f32[2,2048]{1,0:T(2,128)S(1)} %pad_maximum_fusion.1), channel_id=1, replica_groups=mesh['dp'=4,'mp'=8] {'dp','mp'}, use_global_device_ids=true, to_apply=%region_20.21 | all-reduce | flops 6145 | bytes 49160 | tf_op jit(solution)/shard_map/psum | solution.py:235
  2095.2 4.5 fusion.75
  2103.2 5.0 fusion.70
  2108.1 20.3 reduce-scatter.22.cloned.1.call-done
  2130.0 4.3 fusion.73
  2134.3 5.1 fusion.68
  (233 shorter events, 155.9 us)
Async XLA Ops:
  7.2 4.9 copy-start.7
  7.2 5.9 copy-start
  7.2 32.6 %all-gather.13.cloned.1.call-start = ((), (), s32[]{:S(2)}) async-start(), calls=%async_computation.13 | async-start | bytes 1310720 | tf_op jit(solution)/shard_map/all_gather | solution.py:115
  9.2 4.6 copy-start.26
  9.2 85.8 %all-gather.17.cloned.1.call-start = ((), (), s32[]{:S(2)}) async-start(), calls=%async_computation.15 | async-start | bytes 5242880 | tf_op jit(solution)/shard_map/all_gather | solution.py:116
  12.0 129.4 %all-gather.11.cloned.1.call-start = ((), (), s32[]{:S(2)}) async-start(), calls=%async_computation.12 | async-start | bytes 3932160 | tf_op jit(solution)/shard_map/all_gather | solution.py:114
  13.1 212.5 %all-gather.9.cloned.1.call-start = ((), (), s32[]{:S(2)}) async-start(), calls=%async_computation.11 | async-start | bytes 9437184 | tf_op jit(solution)/shard_map/all_gather | solution.py:126
  13.4 81.7 %copy-start.29 = (f32[256]{0:T(256)}, f32[256]{0:T(256)S(1)}, u32[]{:S(2)}) copy-start(f32[256]{0:T(256)S(1)} %broadcast_multiply_fusion.2) | copy-start | bytes 3076
  13.8 81.2 %copy-start.35 = (f32[256]{0:T(256)}, f32[256]{0:T(256)S(1)}, u32[]{:S(2)}) copy-start(f32[256]{0:T(256)S(1)} %fusion.92) | copy-start | bytes 3076
  13.8 81.2 %copy-start.31 = (f32[256]{0:T(256)}, f32[256]{0:T(256)S(1)}, u32[]{:S(2)}) copy-start(f32[256]{0:T(256)S(1)} %fusion.119) | copy-start | bytes 3076
  14.4 0.6 copy-start.23
  16.4 323.9 %all-gather.15.cloned.1.call-start = ((), (), s32[]{:S(2)}) async-start(), calls=%async_computation.14 | async-start | bytes 9437184 | tf_op jit(solution)/shard_map/all_gather | solution.py:143
  39.9 578.9 %all-gather.19.cloned.1.call-start = ((), (), s32[]{:S(2)}) async-start(), calls=%async_computation.16 | async-start | bytes 37748736 | tf_op jit(solution)/shard_map/all_gather | solution.py:144
  334.4 66.5 %copy-start.1 = (bf16[256,2048]{1,0:T(8,128)(2,1)S(1)}, bf16[256,2048]{1,0:T(8,128)(2,1)}, u32[]{:S(2)}) copy-start(bf16[256,2048]{1,0:T(8,128)(2,1)} %param.20) | copy-start | bytes 3145732
  335.9 65.0 %all-to-all-start = ((bf16[8,256,256]{1,2,0:T(8,128)(2,1)}), bf16[8,256,256]{1,2,0:T(8,128)(2,1)}, u32[]{:S(2)}, u32[]{:S(2)}) async-start(bf16[8,256,256]{1,2,0:T(8,128)(2,1)} %copy.106), calls=%async_computation | async-start | bytes 2097152 | tf_op jit(solution)/shard_map/all_to_all | solution.py:141
  340.2 640.7 %reduce-scatter.24.cloned.1.call-start = ((), (), s32[]{:S(2)}) async-start(), calls=%async_computation.26 | async-start | bytes 37748736 | tf_op jit(solution)/shard_map/reduce_scatter | solution.py:203
  340.3 1089.2 %copy-start.38 = (pred[256]{0:T(512)(128)(4,1)}, pred[256]{0:T(512)(128)(4,1)S(1)}, u32[]{:S(2)}) copy-start(pred[256]{0:T(512)(128)(4,1)S(1)} %fusion.117) | copy-start | bytes 772
  400.9 217.9 %copy-start.21 = (f32[1,2048]{1,0:T(1,128)S(1)}, f32[1,2048]{1,0:T(1,128)}, u32[]{:S(2)}) copy-start(f32[1,2048]{1,0:T(1,128)} %get-tuple-element.286) | copy-start | bytes 24580
  618.8 17.2 copy-start.10
  657.1 378.1 %reduce-scatter.26.cloned.1.call-start = ((), (), s32[]{:S(2)}) async-start(), calls=%async_computation.27 | async-start | bytes 5242880 | tf_op jit(solution)/shard_map/reduce_scatter | solution.py:217
  980.9 117.4 %all-gather.21.cloned.1.call-start = ((), (), s32[]{:S(2)}) async-start(), calls=%async_computation.17 | async-start | bytes 5242880 | tf_op jit(solution)/shard_map/all_gather | solution.py:117
  1037.7 5.7 copy-start.15
  1045.6 342.8 %all-gather.23.cloned.1.call-start = ((), (), s32[]{:S(2)}) async-start(), calls=%async_computation.18 | async-start | bytes 37748736 | tf_op jit(solution)/shard_map/all_gather | solution.py:145
  1098.3 607.0 %reduce-scatter.16.cloned.1.call-start = ((), (), s32[]{:S(2)}) async-start(), calls=%async_computation.22 | async-start | bytes 9437184 | tf_op jit(solution)/shard_map/reduce_scatter | solution.py:197
  1429.4 1.3 copy-start.4
  1429.4 1.3 copy-start.33
  1431.1 1.0 copy-start.11
  1439.0 435.7 %reduce-scatter.20.cloned.1.call-start = ((), (), s32[]{:S(2)}) async-start(), calls=%async_computation.24 | async-start | bytes 37748736 | tf_op jit(solution)/shard_map/reduce_scatter | solution.py:200
  1455.6 1.2 copy-start.12
  1465.9 47.3 %all-to-all-start.1 = ((bf16[256,8,256]{0,2,1:T(8,128)(2,1)}), bf16[256,8,256]{0,2,1:T(8,128)(2,1)S(1)}, u32[]{:S(2)}, u32[]{:S(2)}) async-start(bf16[256,8,256]{0,2,1:T(8,128)(2,1)} %bitcast.331), calls=%async_computation.1 | async-start | bytes 2097152 | tf_op jit(solution)/shard_map/all_to_all | solution.py:169
  1469.4 436.9 %reduce-scatter.12.cloned.1.call-start = ((), (), s32[]{:S(2)}) async-start(), calls=%async_computation.20 | async-start | bytes 258048 | tf_op jit(solution)/shard_map/reduce_scatter | solution.py:226
  1491.5 460.3 %reduce-scatter.14.cloned.1.call-start = ((), (), s32[]{:S(2)}) async-start(), calls=%async_computation.21 | async-start | bytes 3932160 | tf_op jit(solution)/shard_map/reduce_scatter | solution.py:208
  1681.9 1.7 copy-start.13
  1683.6 10.6 copy-start.40
  1694.2 349.4 %reduce-scatter.10.cloned.1.call-start = ((), (), s32[]{:S(2)}) async-start(), calls=%async_computation.19 | async-start | bytes 9437184 | tf_op jit(solution)/shard_map/reduce_scatter | solution.py:185
  1705.3 169.4 %copy-start.3 = (bf16[1024,512]{1,0:T(8,128)(2,1)S(1)}, bf16[1024,512]{1,0:T(8,128)(2,1)}, u32[]{:S(2)}) copy-start(bf16[1024,512]{1,0:T(8,128)(2,1)} %reduce-scatter.26.cloned.1.call-done) | copy-start | bytes 3145732
  1705.3 388.7 %reduce-scatter.18.cloned.1.call-start = ((), (), s32[]{:S(2)}) async-start(), calls=%async_computation.23 | async-start | bytes 1310720 | tf_op jit(solution)/shard_map/reduce_scatter | solution.py:211
  1705.4 171.0 %copy-start.18 = (f32[2,4,1,256,256]{4,3,2,1,0:T(8,128)S(1)}, f32[2,4,1,256,256]{4,3,2,1,0:T(8,128)}, u32[]{:S(2)}) copy-start(f32[2,4,1,256,256]{4,3,2,1,0:T(8,128)} %param.34) | copy-start | bytes 6291460
  1705.9 422.6 %reduce-scatter.22.cloned.1.call-start = ((), (), s32[]{:S(2)}) async-start(), calls=%async_computation.25 | async-start | bytes 5242880 | tf_op jit(solution)/shard_map/reduce_scatter | solution.py:214
  1957.9 7.4 copy-start.8
  1962.2 6.0 copy-start.14
  1965.3 4.1 copy-start.19
  1970.7 72.9 %copy-start.2 = (bf16[256,2048]{1,0:T(8,128)(2,1)S(1)}, bf16[256,2048]{1,0:T(8,128)(2,1)}, u32[]{:S(2)}) copy-start(bf16[256,2048]{1,0:T(8,128)(2,1)} %param.20) | copy-start | bytes 3145732
  1970.7 72.9 %copy-start.24 = (f32[1,2048]{1,0:T(1,128)S(1)}, f32[1,2048]{1,0:T(1,128)}, u32[]{:S(2)}) copy-start(f32[1,2048]{1,0:T(1,128)} %copy-done.23) | copy-start | bytes 24580
  1970.7 72.9 %copy-start.30 = (f32[256]{0:T(256)S(1)}, f32[256]{0:T(256)}, u32[]{:S(2)}) copy-start(f32[256]{0:T(256)} %copy-done.29) | copy-start | bytes 3076
  1970.7 74.7 %copy-start.36 = (f32[256]{0:T(256)S(1)}, f32[256]{0:T(256)}, u32[]{:S(2)}) copy-start(f32[256]{0:T(256)} %copy-done.35) | copy-start | bytes 3076
  1970.7 74.7 %copy-start.32 = (f32[256]{0:T(256)S(1)}, f32[256]{0:T(256)}, u32[]{:S(2)}) copy-start(f32[256]{0:T(256)} %copy-done.31) | copy-start | bytes 3076
  1975.9 71.8 %copy-start.37 = (f32[2048]{0:T(1024)S(1)}, f32[2048]{0:T(1024)}, u32[]{:S(2)}) copy-start(f32[2048]{0:T(1024)} %get-tuple-element.232) | copy-start | bytes 24580
  1975.9 112.7 %copy-start.25 = (bf16[1,50,256]{2,1,0:T(8,128)(2,1)S(1)}, bf16[1,50,256]{2,1,0:T(8,128)(2,1)}, u32[]{:S(2)}) copy-start(bf16[1,50,256]{2,1,0:T(8,128)(2,1)} %reduce-scatter.12.cloned.1.call-done) | copy-start | bytes 76804
  1975.9 113.5 %copy-start.27 = (f32[2,2048]{1,0:T(2,128)S(1)}, f32[2,2048]{1,0:T(2,128)}, u32[]{:S(2)}) copy-start(f32[2,2048]{1,0:T(2,128)} %param.23) | copy-start | bytes 49156
  1975.9 114.2 %copy-start.5 = (f32[256,2048]{1,0:T(8,128)S(1)}, f32[256,2048]{1,0:T(8,128)}, u32[]{:S(2)}) copy-start(f32[256,2048]{1,0:T(8,128)} %copy-done.4) | copy-start | bytes 6291460
  1975.9 114.2 %copy-start.34 = (f32[256]{0:T(256)S(1)}, f32[256]{0:T(256)}, u32[]{:S(2)}) copy-start(f32[256]{0:T(256)} %copy-done.33) | copy-start | bytes 3076
  1975.9 114.2 %copy-start.39 = (pred[256]{0:T(512)(128)(4,1)S(1)}, pred[256]{0:T(512)(128)(4,1)}, u32[]{:S(2)}) copy-start(pred[256]{0:T(512)(128)(4,1)} %copy-done.38) | copy-start | bytes 772
  2086.5 13.2 copy-start.28
  2094.0 5.7 copy-start.22
  2094.0 6.6 copy-start.16
  2095.2 6.2 copy-start.20
  2134.3 5.1 copy-start.17
  2140.9 6.4 copy-start.6
  2144.4 6.3 copy-start.9
Sparse Core Ops, SparseCore 0:
  10.5 29.3 all-gather.12
  42.2 52.6 all-gather.16
  97.4 43.9 all-gather.10
  143.4 82.0 all-gather.8
  227.0 81.0 all-gather.14
  309.5 309.2 all-gather.18
  657.2 323.6 reduce-scatter.23
  984.1 50.9 reduce-scatter.25
  1045.7 52.5 all-gather.20
  1099.7 288.6 all-gather.22
  1439.1 104.6 reduce-scatter.15
  1546.1 328.5 reduce-scatter.19
  1877.6 28.7 reduce-scatter.11
  1909.8 42.0 reduce-scatter.13
  1954.0 89.5 reduce-scatter.9
  2046.4 26.0 reduce-scatter.17
  2075.6 52.8 reduce-scatter.21
where the time goes:
time: 2170 us; the launch traced here: 2160 us
  waiting for transfers between devices  1550 us (71%)
  matrix products  384 us (18%)
  other arithmetic  109 us (5%)
  local copies, waits for them, and re-layouts  53.2 us (2%)
  blocking collectives  38.8 us (2%)
    reduce_scatter x1, waiting for transfers between devices, body(): lax.psum_scatter(grad_down_part.astype(jnp.bfloat16), 'mp', scatter_dimen...  324 us
    all_gather x1, waiting for transfers between devices, body(): lax.all_gather(down_part, 'mp', axis=0, tiled=True)  290 us
    all_gather x1, waiting for transfers between devices, body(): lax.all_gather(up_part, 'mp', axis=1, tiled=True)  211 us
    reduce_scatter x1, waiting for transfers between devices, body(): lax.psum_scatter(grad_up_part.astype(jnp.bfloat16), 'mp', scatter_dimensi...  169 us
    all_gather x1, waiting for transfers between devices, body(): gathered = lax.all_gather(normed_one, 'mp', axis=0, tiled=True)  84.1 us
    dot_general x8, matrix products, masked_scores(): jnp.einsum('qd,kd->qk', queries, key_rows, preferred_element_type=jnp.flo...  70.6 us
    reduce_scatter x1, waiting for transfers between devices, body(): lax.psum_scatter(jnp.einsum('gc,dc->gd', d_qkv, qkv_part, preferred_eleme...  67.7 us
    all_to_all x1, waiting for transfers between devices, body(): lax.all_to_all(ctx_heads, 'mp', split_axis=0, concat_axis=1, tiled=True)  60.6 us
  transfers between devices with their start and end apart: 19, of which 16 were waited for; matrix products, arithmetic and copies ran while one was open for 19% of the time, Pallas kernels for 0%

commit v1 on v0

v1 whole, which is shorter than its diff:
```python
import functools
import math

import jax
import jax.numpy as jnp
from jax import lax
from jax.experimental import pallas as pl
from jax.experimental.pallas import tpu as pltpu
from jax.sharding import PartitionSpec as P

HD = 64
SLOT = 2048
NSUM = 50
BLOCK = 512
FBLK = 256


NORM_EPSILON = 1e-05
SHAMPOO_RATE = 0.5
GAIN_RATE = 0.1
DECAY = 0.5
NEG = -1e30
BF = jnp.bfloat16
F32 = jnp.float32

NT = (((1,),(1,)),((),()))
NN=(((1,),(0,)),((),()))
TN=(((0,),(0,)),((),()))
def dg(a,b,d): return lax.dot_general(a,b,d,preferred_element_type=F32)

def head_masks(width, hp):
    lane = lax.broadcasted_iota(jnp.int32,(1,width),1)
    return [(lane>=h*HD)&(lane<(h+1)*HD) for h in range(hp)]

def fwd_kernel(hp, bq, len_ref, q_ref, k_ref, v_ref, o_ref, lse_ref, s_ref):
    i = pl.program_id(2)
    limit = len_ref[pl.program_id(0)] + NSUM
    width = q_ref.shape[1]
    masks = head_masks(width, hp)
    q = q_ref[...] * jnp.asarray(0.125, BF)
    qs = [jnp.where(m, q, jnp.zeros_like(q)) for m in masks]
    col = lax.broadcasted_iota(jnp.int32,(bq,bq),1)
    row = lax.broadcasted_iota(jnp.int32,(bq,bq),0)
    def score(j, tops, diag):
        k = k_ref[pl.ds(pl.multiple_of(j*bq,bq),bq),:]
        ok = col < limit - j*bq
        if diag: ok = ok & (col <= row)
        out=[]
        for h in range(hp):
            s = jnp.where(ok, dg(qs[h],k,NT), NEG)
            s_ref[h,j] = s
            t = tops[h]
            for c in range(0,bq,128): t = jnp.maximum(t, s[:,c:c+128])
            out.append(t)
        return out
    tops=[jnp.full((bq,128),NEG,F32) for _ in range(hp)]
    tops=lax.fori_loop(0,i,lambda j,t: score(j,t,False), tops)
    tops=score(i,tops,True)
    tops=[jnp.max(t,axis=1,keepdims=True) for t in tops]
    def acc(j, carry):
        v = v_ref[pl.ds(pl.multiple_of(j*bq,bq),bq),:]
        out=[]
        for h in range(hp):
            o,l = carry[h]
            e = jnp.exp(s_ref[h,j]-tops[h])
            for c in range(0,bq,128): l = l + e[:,c:c+128]
            o = o + dg(e.astype(BF),v,NN)
            out.append((o,l))
        return out
    carry=[(jnp.zeros((bq,width),F32),jnp.zeros((bq,128),F32)) for _ in range(hp)]
    carry=lax.fori_loop(0,i+1,acc,carry)
    res=None
    for h in range(hp):
        o,l=carry[h]
        l=jnp.sum(l,axis=1,keepdims=True)
        o=o/l
        res = o if res is None else jnp.where(masks[h],o,res)
        lse = jnp.broadcast_to(tops[h]+jnp.log(l),(bq,128)).T
        lse_ref[0,h]=lse[:8]
    o_ref[...]=res.astype(BF)

def attend_fwd(seg_len,q,k,v,bq=512):
    rows,hw=q.shape
    heads=hw//HD; hp=2 if heads%2==0 else 1
    assert hp==2 or heads==1
    W=hp*HD; nb=SLOT//bq; segs=rows//SLOT; pairs=heads//hp
    return pl.pallas_call(functools.partial(fwd_kernel,hp,bq),
        grid_spec=pltpu.PrefetchScalarGridSpec(num_scalar_prefetch=1, grid=(segs,pairs,nb),
            in_specs=[pl.BlockSpec((bq,W),lambda s,p,i,l:(s*nb+i,p)),
                      pl.BlockSpec((SLOT,W),lambda s,p,i,l:(s,p)),
                      pl.BlockSpec((SLOT,W),lambda s,p,i,l:(s,p))],
            out_specs=[pl.BlockSpec((bq,W),lambda s,p,i,l:(s*nb+i,p)),
                       pl.BlockSpec((1,hp,8,bq),lambda s,p,i,l:(s,p,0,i))],
            scratch_shapes=[pltpu.VMEM((hp,nb,bq,bq),F32)]),
        out_shape=[jax.ShapeDtypeStruct((rows,hw),BF),jax.ShapeDtypeStruct((segs,heads,8,SLOT),F32)],
        compiler_params=pltpu.CompilerParams(vmem_limit_bytes=48<<20),
        cost_estimate=pl.CostEstimate(flops=segs*heads*SLOT*SLOT*64*2, bytes_accessed=rows*hw*8, transcendentals=segs*heads*SLOT*SLOT//2),
    )(seg_len,q,k,v)

def bwd_kernel(hp, bq, len_ref, q_ref, k_ref, v_ref, o_ref, do_ref, lse_ref, dq_ref, dk_ref, dv_ref, dka, dva):
    i = pl.program_id(2)
    nb = pl.num_programs(2)
    limit = len_ref[pl.program_id(0)] + NSUM
    width = q_ref.shape[1]
    masks = head_masks(width, hp)
    @pl.when(i==0)
    def _():
        dka[...]=jnp.zeros_like(dka); dva[...]=jnp.zeros_like(dva)
    q = q_ref[...] * jnp.asarray(0.125, BF)
    do = do_ref[...]
    prod = (do.astype(F32)*o_ref[...].astype(F32)).T
    qs = [jnp.where(m, q, jnp.zeros_like(q)) for m in masks]
    dos = [jnp.where(m, do, jnp.zeros_like(do)) for m in masks]
    dd = [jnp.sum(prod[h*HD:(h+1)*HD],axis=0,keepdims=True) for h in range(hp)]
    ls = [lse_ref[0,h,0:1,:] for h in range(hp)]
    rowk = lax.broadcasted_iota(jnp.int32,(bq,bq),0)
    colq = lax.broadcasted_iota(jnp.int32,(bq,bq),1)
    def step(j, dq, diag):
        at = pl.ds(pl.multiple_of(j*bq,bq),bq)
        k = k_ref[at,:]; v=v_ref[at,:]
        ok = rowk < limit - j*bq
        if diag: ok = ok & (rowk <= colq)
        dk=dka[at,:]; dv=dva[at,:]
        for h in range(hp):
            s = dg(k,qs[h],NT)
            p = jnp.where(ok, jnp.exp(s-ls[h]), 0.0)
            dp = dg(v,dos[h],NT)
            ds = (p*(dp-dd[h])).astype(BF)
            dv = dv + dg(p.astype(BF),dos[h],NN)
            dk = dk + dg(ds,qs[h],NN)
            dq = dq + dg(ds, jnp.where(masks[h],k,jnp.zeros_like(k)), TN)
        dka[at,:]=dk; dva[at,:]=dv
        return dq
    dq = lax.fori_loop(0,i,lambda j,c: step(j,c,False), jnp.zeros((bq,width),F32))
    dq = step(i,dq,True)
    dq_ref[...] = (dq*0.125).astype(BF)
    @pl.when(i==nb-1)
    def _():
        dk_ref[...]=dka[...].astype(BF); dv_ref[...]=dva[...].astype(BF)

def attend_bwd(seg_len,q,k,v,o,do,lse,bq=512):
    rows,hw=q.shape
    heads=hw//HD; hp=2 if heads%2==0 else 1
    W=hp*HD; nb=SLOT//bq; segs=rows//SLOT; pairs=heads//hp
    blk=pl.BlockSpec((bq,W),lambda s,p,i,l:(s*nb+i,p)); full=pl.BlockSpec((SLOT,W),lambda s,p,i,l:(s,p))
    sh=jax.ShapeDtypeStruct((rows,hw),BF)
    return pl.pallas_call(functools.partial(bwd_kernel,hp,bq),
        grid_spec=pltpu.PrefetchScalarGridSpec(num_scalar_prefetch=1, grid=(segs,pairs,nb),
            in_specs=[blk,full,full,blk,blk,pl.BlockSpec((1,hp,8,bq),lambda s,p,i,l:(s,p,0,i))],
            out_specs=[blk,full,full],
            scratch_shapes=[pltpu.VMEM((SLOT,W),F32),pltpu.VMEM((SLOT,W),F32)]),
        out_shape=[sh,sh,sh],
        compiler_params=pltpu.CompilerParams(vmem_limit_bytes=48<<20),
        cost_estimate=pl.CostEstimate(flops=segs*heads*SLOT*SLOT*64*5, bytes_accessed=rows*hw*16, transcendentals=segs*heads*SLOT*SLOT//2),
    )(seg_len,q,k,v,o,do,lse)


def shampoo_kernel(group, tc, w_ref, g_ref, l_ref, r_ref, nw_ref, nl_ref, nr_ref, gf_ref):
    for h in range(group):
        cols = slice(h * tc, (h + 1) * tc)
        g = g_ref[:, cols]
        gf_ref[:, cols] = g.astype(F32)
        nl_ref[0, h] = DECAY * l_ref[0, 0, h] + (1.0 - DECAY) * dg(g, g, NT)
        nr_ref[0, h] = DECAY * r_ref[0, 0, h] + (1.0 - DECAY) * dg(g, g, TN)
        mid = dg(l_ref[1, 0, h].astype(BF), g, NN).astype(BF)
        step = dg(mid, r_ref[1, 0, h].astype(BF), NN)
        nw_ref[:, cols] = w_ref[:, cols] - SHAMPOO_RATE * step


def shampoo(weight, grad, left, right, tr, tc):
    rows, cols = grad.shape
    tiles_c = cols // tc
    group = 1 if tc % 128 == 0 or tiles_c == 1 else 2
    width = group * tc
    wide = pl.BlockSpec((tr, width), lambda i, j: (i, j))

    def stat(size):
        return pl.BlockSpec((2, 1, group, size, size), lambda i, j: (0, i, j, 0, 0))

    def new(size):
        return pl.BlockSpec((1, group, size, size), lambda i, j: (i, j, 0, 0))

    return pl.pallas_call(
        functools.partial(shampoo_kernel, group, tc),
        grid=(rows // tr, tiles_c // group),
        in_specs=[wide, wide, stat(tr), stat(tc)],
        out_specs=[wide, new(tr), new(tc), wide],
        out_shape=[
            jax.ShapeDtypeStruct(weight.shape, F32),
            jax.ShapeDtypeStruct(left.shape[1:], F32),
            jax.ShapeDtypeStruct(right.shape[1:], F32),
            jax.ShapeDtypeStruct(weight.shape, F32),
        ],
        compiler_params=pltpu.CompilerParams(vmem_limit_bytes=48 << 20),
        cost_estimate=pl.CostEstimate(
            flops=4 * rows * cols * (tr + tc),
            bytes_accessed=6 * (left.size + right.size) + 14 * rows * cols,
            transcendentals=0,
        ),
    )(weight, grad, left, right)


def layer_norm(value, gain):
    mean = jnp.mean(value, axis=-1, keepdims=True)
    centred = value - mean
    spread = jnp.mean(centred * centred, axis=-1, keepdims=True)
    return centred * lax.rsqrt(spread + NORM_EPSILON) * gain


def gelu_tanh(value):
    return jax.nn.gelu(value, approximate=True)


def body(
    tokens,
    seg_len,
    cotangent,
    ln_gain,
    qkv_weight,
    out_weight,
    up_weight,
    down_weight,
    left_qkv,
    right_qkv,
    left_out,
    right_out,
    left_up,
    right_up,
    left_down,
    right_down,
):
    row_count, features = tokens.shape
    mp_count = lax.axis_size("mp")
    mp_index = lax.axis_index("mp")
    seg_count = seg_len.shape[0]
    own_rows, own_cols = qkv_weight.shape
    head_count = own_cols // (3 * HD)
    inputs = tokens.astype(F32)
    by_kind = (
        qkv_weight.astype(BF)
        .reshape(own_rows, head_count, 3, HD)
        .transpose(0, 2, 1, 3)
        .reshape(own_rows, own_cols)
    )
    normed_one = layer_norm(inputs, ln_gain[0]).astype(BF)
    gathered = lax.all_gather(normed_one, "mp", axis=0, tiled=True)
    qkv_part = lax.all_gather(by_kind, "dp", axis=0, tiled=True)
    positions = mp_index * row_count + jnp.arange(row_count)
    owner_seg = positions // SLOT
    own_length = jnp.sum(
        jnp.where(owner_seg[:, None] == jnp.arange(seg_count)[None, :], seg_len[None, :], 0), axis=1
    )
    valid = positions % SLOT < own_length + NSUM
    upstream = jnp.where(valid[:, None], cotangent, jnp.zeros_like(cotangent))
    out_part = lax.all_gather(out_weight.astype(BF), "dp", axis=0, tiled=True)
    out_rows = lax.all_to_all(out_part, "mp", split_axis=0, concat_axis=1, tiled=True)
    up_part = lax.all_gather(up_weight.astype(BF), "dp", axis=0, tiled=True)
    down_part = lax.all_gather(down_weight.astype(BF), "dp", axis=1, tiled=True)
    qkv_rows = jnp.dot(gathered, qkv_part, preferred_element_type=F32).astype(BF)
    queries, keys, values = jnp.split(qkv_rows, 3, axis=1)
    context, log_sums = attend_fwd(seg_len, queries, keys, values)
    upstream_all = lax.all_gather(upstream, "mp", axis=0, tiled=True)
    attended = lax.psum_scatter(
        jnp.dot(context, out_rows, preferred_element_type=F32).astype(BF),
        "mp",
        scatter_dimension=0,
        tiled=True,
    )
    resid = inputs + attended.astype(F32)
    normed_two = lax.all_gather(
        layer_norm(resid, ln_gain[1]).astype(BF), "mp", axis=0, tiled=True
    )
    pre_act = jnp.dot(normed_two, up_part, preferred_element_type=F32)
    hidden = gelu_tanh(pre_act).astype(BF)
    d_hidden = jnp.einsum("rd,fd->rf", upstream_all, down_part, preferred_element_type=F32)
    d_pre = jax.vjp(gelu_tanh, pre_act)[1](d_hidden)[0].astype(BF)
    d_normed_two = lax.psum_scatter(
        jnp.einsum("rf,df->rd", d_pre, up_part, preferred_element_type=F32).astype(BF),
        "mp",
        scatter_dimension=0,
        tiled=True,
    ).astype(F32)
    ffn_out = lax.psum_scatter(
        jnp.dot(hidden, down_part, preferred_element_type=F32).astype(BF),
        "mp",
        scatter_dimension=0,
        tiled=True,
    )
    block_out = (resid + ffn_out.astype(F32)).astype(BF)
    norm_back_two = jax.vjp(layer_norm, resid, ln_gain[1])[1]
    d_resid_ln, d_gain_two = norm_back_two(d_normed_two)
    d_resid = upstream.astype(F32) + d_resid_ln
    d_resid_all = lax.all_gather(d_resid.astype(BF), "mp", axis=0, tiled=True)
    d_context = jnp.einsum(
        "re,de->rd", d_resid_all, out_rows, preferred_element_type=F32
    ).astype(BF)
    grad_down_part = jnp.einsum("rf,rd->fd", hidden, upstream_all, preferred_element_type=F32)
    grad_up_part = jnp.einsum("rd,rf->df", normed_two, d_pre, preferred_element_type=F32)
    d_qkv = jnp.concatenate(
        attend_bwd(seg_len, queries, keys, values, context, d_context, log_sums), axis=1
    )
    grad_qkv_part = jnp.einsum("gd,gc->dc", gathered, d_qkv, preferred_element_type=F32)
    d_normed_one = lax.psum_scatter(
        jnp.einsum("gc,dc->gd", d_qkv, qkv_part, preferred_element_type=F32).astype(BF),
        "mp",
        scatter_dimension=0,
        tiled=True,
    ).astype(F32)
    norm_back_one = jax.vjp(layer_norm, inputs, ln_gain[0])[1]
    d_input_ln, d_gain_one = norm_back_one(d_normed_one)
    input_grad = d_resid + d_input_ln
    grad_out_rows = jnp.einsum("rd,re->de", context, d_resid_all, preferred_element_type=F32)
    grad_out_part = lax.all_to_all(
        grad_out_rows.astype(BF), "mp", split_axis=1, concat_axis=0, tiled=True
    )
    grad_qkv, grad_out, grad_up, grad_down = (
        lax.psum_scatter(grad_qkv_part.astype(BF), "dp", scatter_dimension=0, tiled=True),
        lax.psum_scatter(grad_out_part, "dp", scatter_dimension=0, tiled=True),
        lax.psum_scatter(grad_up_part.astype(BF), "dp", scatter_dimension=0, tiled=True),
        lax.psum_scatter(grad_down_part.astype(BF), "dp", scatter_dimension=1, tiled=True),
    )
    grad_qkv = (
        grad_qkv.reshape(own_rows, 3, head_count, HD)
        .transpose(0, 2, 1, 3)
        .reshape(own_rows, own_cols)
    )
    slot_index = (jnp.arange(seg_count) * SLOT + seg_len)[:, None] + jnp.arange(NSUM)[None, :]
    selector = (slot_index.reshape(-1)[:, None] == positions[None, :]).astype(jnp.bfloat16)
    picked = jnp.dot(selector, block_out, preferred_element_type=jnp.float32).reshape(
        seg_count, NSUM, features
    )
    owned_vectors = lax.psum_scatter(
        picked.astype(jnp.bfloat16), "mp", scatter_dimension=2, tiled=True
    ).astype(jnp.float32)
    owned_width = owned_vectors.shape[2]
    col_sums = jnp.sum(owned_vectors, axis=(0, 1))
    spread_sums = (
        (jnp.arange(mp_count) == mp_index).astype(jnp.float32)[:, None] * col_sums[None, :]
    ).reshape(features)
    gain_parts = jnp.stack([d_gain_one, d_gain_two])
    gain_grads, total_cols, total_squares = lax.psum(
        (gain_parts, spread_sums, jnp.sum(owned_vectors * owned_vectors)), ("dp", "mp")
    )
    vector_count = seg_count * lax.axis_size("dp") * NSUM
    centre_all = total_cols / vector_count
    centre = lax.dynamic_slice_in_dim(centre_all, mp_index * owned_width, owned_width, 0)
    variance = total_squares / (vector_count * features) - jnp.mean(centre_all * centre_all)
    summaries = (owned_vectors - centre) * lax.rsqrt(variance + NORM_EPSILON)
    new_gains = ln_gain - GAIN_RATE * gain_grads * lax.rsqrt(
        jnp.mean(gain_grads * gain_grads, axis=-1, keepdims=True) + 1e-06
    )
    new_qkv, new_left_qkv, new_right_qkv, grad_qkv = shampoo(
        qkv_weight, grad_qkv, left_qkv, right_qkv, BLOCK, 3 * HD
    )
    new_out, new_left_out, new_right_out, grad_out = shampoo(
        out_weight, grad_out, left_out, right_out, BLOCK, HD
    )
    new_up, new_left_up, new_right_up, grad_up = shampoo(
        up_weight, grad_up, left_up, right_up, BLOCK, FBLK
    )
    new_down, new_left_down, new_right_down, grad_down = shampoo(
        down_weight, grad_down, left_down, right_down, FBLK, BLOCK
    )
    return (
        block_out,
        input_grad,
        summaries,
        gain_grads,
        new_gains,
        grad_qkv,
        grad_out,
        grad_up,
        grad_down,
        new_qkv,
        new_out,
        new_up,
        new_down,
        new_left_qkv,
        new_right_qkv,
        new_left_out,
        new_right_out,
        new_left_up,
        new_right_up,
        new_left_down,
        new_right_down,
    )


def solution(mesh):
    in_specs = (
        P(("dp", "mp"), None),
        P("dp"),
        P(("dp", "mp"), None),
        P(),
        P("dp", "mp"),
        P("dp", "mp"),
        P("dp", "mp"),
        P("mp", "dp"),
        P(None, "dp", "mp", None, None),
        P(None, "dp", "mp", None, None),
        P(None, "dp", "mp", None, None),
        P(None, "dp", "mp", None, None),
        P(None, "dp", "mp", None, None),
        P(None, "dp", "mp", None, None),
        P(None, "mp", "dp", None, None),
        P(None, "mp", "dp", None, None),
    )
    out_specs = (
        P(("dp", "mp"), None),
        P(("dp", "mp"), None),
        P("dp", None, "mp"),
        P(),
        P(),
        P("dp", "mp"),
        P("dp", "mp"),
        P("dp", "mp"),
        P("mp", "dp"),
        P("dp", "mp"),
        P("dp", "mp"),
        P("dp", "mp"),
        P("mp", "dp"),
        P("dp", "mp", None, None),
        P("dp", "mp", None, None),
        P("dp", "mp", None, None),
        P("dp", "mp", None, None),
        P("dp", "mp", None, None),
        P("dp", "mp", None, None),
        P("mp", "dp", None, None),
        P("mp", "dp", None, None),
    )
    return jax.shard_map(body, mesh=mesh, in_specs=in_specs, out_specs=out_specs, check_vma=False)
```

time: 2170 us -> 1260 us (0.58)
  waiting for transfers between devices: 1550 us -> 883 us
  matrix products: 384 us -> 146 us
  Pallas kernels: 0 us -> 93.8 us
  other arithmetic: 109 us -> 34.9 us
  local copies, waits for them, and re-layouts: 53.2 us -> 25.4 us
    all_gather x7, waiting for transfers between devices: 678 us -> 345 us  [the longest x1 84.3 us: body(): lax.all_gather(layer_norm(resid, ln_gain[1]).astype(BF), 'mp', axis=0, ti...]
    reduce_scatter x7, waiting for transfers between devices: 611 us -> 326 us  [the longest x1 87.2 us: body(): lax.psum_scatter(jnp.dot(hidden, down_part, preferred_element_type=F32).a...]
    dot_general x56 -> x12, matrix products: 382 us -> 144 us  [the longest x1 22.2 us: body(): pre_act = jnp.dot(normed_two, up_part, preferred_element_type=F32)]
    pallas_call x0 -> x6, Pallas kernels: none -> 93.8 us  [the longest x1 36.3 us: attend_bwd(): pl.pallas_call(functools.partial(bwd_kernel, hp, bq), grid_spec=pltpu.Pre...]
    all_to_all x2, waiting for transfers between devices: 82.2 us -> 25.9 us  [the longest x1 25.9 us: body(): lax.all_to_all(out_part, 'mp', split_axis=0, concat_axis=1, tiled=True)]
    convert_element_type x13 -> x6, other arithmetic: 46 us -> 9.87 us  [the longest x1 2.78 us: body(): up_part = lax.all_gather(up_weight.astype(BF), 'dp', axis=0, tiled=True)]
    reduce_sum x4 -> x0, other arithmetic: 32.4 us -> none  [attend_forward(): row_total = jnp.sum(exponent, axis=-1, keepdims=True)]
  transfers between devices with their start and end apart: 19 -> 19, of which waited for: 16 -> 17; matrix products, arithmetic and copies ran while one was open for 19% -> 10% of each run, Pallas kernels for 0% -> 5%
where the time goes in v1:
time: 1260 us; the launch traced here: 1250 us
  waiting for transfers between devices  883 us (70%)
  matrix products  146 us (12%)
  Pallas kernels  93.8 us (7%)
  blocking collectives  38.5 us (3%)
  other arithmetic  34.9 us (3%)
  local copies, waits for them, and re-layouts  25.4 us (2%)
  between operations  16.9 us (1%)
    reduce_scatter x1, waiting for transfers between devices, body(): lax.psum_scatter(jnp.dot(hidden, down_part, preferred_element_type=F32).a...  87.2 us
    all_gather x1, waiting for transfers between devices, body(): gathered = lax.all_gather(normed_one, 'mp', axis=0, tiled=True)  84.3 us
    all_gather x1, waiting for transfers between devices, body(): lax.all_gather(layer_norm(resid, ln_gain[1]).astype(BF), 'mp', axis=0, ti...  84.3 us
    all_gather x1, waiting for transfers between devices, body(): upstream_all = lax.all_gather(upstream, 'mp', axis=0, tiled=True)  84.1 us
    reduce_scatter x1, waiting for transfers between devices, body(): lax.psum_scatter(jnp.einsum('gc,dc->gd', d_qkv, qkv_part, preferred_eleme...  81.6 us
    reduce_scatter x1, waiting for transfers between devices, body(): lax.psum_scatter(jnp.dot(context, out_rows, preferred_element_type=F32).a...  80.2 us
    reduce_scatter x1, waiting for transfers between devices, body(): lax.psum_scatter(jnp.einsum('rf,df->rd', d_pre, up_part, preferred_elemen...  72.6 us
    all_gather x1, waiting for transfers between devices, body(): d_resid_all = lax.all_gather(d_resid.astype(BF), 'mp', axis=0, tiled=True)  50.1 us
  transfers between devices with their start and end apart: 19, of which 17 were waited for; matrix products, arithmetic and copies ran while one was open for 10% of the time, Pallas kernels for 5%

profile of v1, /device:TPU:0, one launch (start us, length us, event | category | flops | bytes accessed | tf_op | source)
XLA Modules:
  0.0 1248.9 jit_solution(14732321649056441815)
XLA Ops:
  7.2 1.9 convert_element_type.99
  9.2 1.7 copy.47
  12.6 1.4 fusion.16
  14.0 25.8 %all-gather.13.cloned.1.call-done = bf16[2048,256]{1,0:T(8,128)(2,1)} async-done(((bf16[512,256]{1,0:T(8,128)(2,1)}), bf16[2048,256]{1,0:T(8,128)(2,1)}) %all-gather.13.cloned.1.call-update) | async-done | bytes 1048592 | tf_op jit(solution)/shard_map/all_gather | solution.py:255
  39.8 4.6 all-to-all-start
  45.1 25.9 %all-to-all-done = bf16[8,256,256]{2,1,0:T(8,128)(2,1)S(1)} async-done(((bf16[8,256,256]{2,1,0:T(8,128)(2,1)}), bf16[8,256,256]{2,1,0:T(8,128)(2,1)S(1)}, u32[]{:S(2)}, u32[]{:S(2)}) %all-to-all-start) | async-done | bytes 1048608 | tf_op jit(solution)/shard_map/all_to_all | solution.py:256
  71.0 1.3 copy.49
  72.3 13.7 %all-gather.11.cloned.1.call-done = bf16[2048,768]{0,1:T(8,128)(2,1)} async-done(((bf16[512,768]{0,1:T(8,128)(2,1)}), bf16[2048,768]{0,1:T(8,128)(2,1)}) %all-gather.11.cloned.1.call-update) | async-done | bytes 3145744 | tf_op jit(solution)/shard_map/all_gather | solution.py:247
  86.1 84.3 %all-gather.9.cloned.1.call-done = bf16[2048,2048]{1,0:T(8,128)(2,1)} async-done(((bf16[256,2048]{1,0:T(8,128)(2,1)}), bf16[2048,2048]{1,0:T(8,128)(2,1)}) %all-gather.9.cloned.1.call-update) | async-done | bytes 8388624 | tf_op jit(solution)/shard_map/all_gather | solution.py:246
  170.4 10.1 convolution_convert_fusion.6
  180.7 28.5 %shard_map.319 = (bf16[2048,256]{1,0:T(8,128)(2,1)S(1)}, f32[1,4,8,2048]{3,2,1,0:T(8,128)S(1)}) custom-call(s32[1]{0:T(128)} %copy.61.len_ref, bf16[2048,256]{1,0:T(8,128)(2,1)S(1)} %get-tuple-element.139.q_ref, bf16[2048,256]{1,0:T(8,128)(2,1)S(1)} %get-tuple-element.138.k_ref, bf16[2048,256]{1,0:T(8,128)(2,1)S(1)} %get-tuple-element.137.v_ref), custom_call_target="tpu_custom_call" | custom-call | flops 2147483648 | bytes 4194304 | tf_op jit(solution)/shard_map/pallas_call | solution.py:87
  209.3 5.6 convolution_convert_fusion.3
  215.0 1.5 copy-done.1
  217.7 2.3 broadcast_select_fusion
  220.1 2.8 convert_element_type.103
  223.0 80.2 %reduce-scatter.10.cloned.1.call-done = bf16[256,2048]{1,0:T(8,128)(2,1)} async-done(((bf16[2048,2048]{1,0:T(8,128)(2,1)}), bf16[256,2048]{1,0:T(8,128)(2,1)}) %reduce-scatter.10.cloned.1.call-update) | async-done | bytes 1048592 | tf_op jit(solution)/shard_map/reduce_scatter | solution.py:263
  303.2 2.0 fusion.23
  305.3 2.0 multiply_reduce_fusion
  307.3 1.4 multiply_convert_fusion.1
  309.1 47.3 %all-gather.19.cloned.1.call-done = bf16[1024,2048]{1,0:T(8,128)(2,1)} async-done(((bf16[1024,512]{1,0:T(8,128)(2,1)}), bf16[1024,2048]{1,0:T(8,128)(2,1)}) %all-gather.19.cloned.1.call-update) | async-done | bytes 4194320 | tf_op jit(solution)/shard_map/all_gather | solution.py:258
  356.4 84.1 %all-gather.21.cloned.1.call-done = bf16[2048,2048]{1,0:T(8,128)(2,1)} async-done(((bf16[256,2048]{1,0:T(8,128)(2,1)}), bf16[2048,2048]{1,0:T(8,128)(2,1)}) %all-gather.21.cloned.1.call-update) | async-done | bytes 8388624 | tf_op jit(solution)/shard_map/all_gather | solution.py:262
  440.5 14.5 %fusion.38 = f32[2048,1024]{1,0:T(8,128)} fusion(bf16[2048,2048]{1,0:T(8,128)(2,1)} %all-gather.21.cloned.1.call-done, bf16[1024,2048]{1,0:T(8,128)(2,1)} %all-gather.19.cloned.1.call-done), kind=kOutput, calls=%fused_computation.98 | convolution fusion | flops 8589934592 | bytes 20971520 | tf_op jit(solution)/shard_map/rd,fd->rf/dot_general | solution.py:275
  455.0 39.2 %all-gather.17.cloned.1.call-done = bf16[2048,1024]{1,0:T(8,128)(2,1)} async-done(((bf16[512,1024]{1,0:T(8,128)(2,1)}), bf16[2048,1024]{1,0:T(8,128)(2,1)}) %all-gather.17.cloned.1.call-update) | async-done | bytes 4194320 | tf_op jit(solution)/shard_map/all_gather | solution.py:257
  494.2 84.3 %all-gather.15.cloned.1.call-done = bf16[2048,2048]{1,0:T(8,128)(2,1)} async-done(((bf16[256,2048]{1,0:T(8,128)(2,1)}), bf16[2048,2048]{1,0:T(8,128)(2,1)}) %all-gather.15.cloned.1.call-update) | async-done | bytes 8388624 | tf_op jit(solution)/shard_map/all_gather | solution.py:270
  578.5 22.2 %fusion.6 = (bf16[2048,1024]{1,0:T(8,128)(2,1)S(1)}, f32[2048,1024]{1,0:T(8,128)}) fusion(f32[2048,1024]{1,0:T(8,128)} %fusion.38, bf16[2048,2048]{1,0:T(8,128)(2,1)} %all-gather.15.cloned.1.call-done, bf16[2048,1024]{1,0:T(8,128)(2,1)} %all-gather.17.cloned.1.call-done), kind=kOutput, calls=%fused_computation.8 | convolution fusion | flops 8631877632 | bytes 33554432 | tf_op jit(solution)/shard_map/dot_general | solution.py:273
  600.7 2.0 copy-done.39
  602.7 10.9 convolution_convert_fusion.1
  614.1 15.1 %convolution_convert_fusion.2 = bf16[2048,2048]{1,0:T(8,128)(2,1)} fusion(bf16[1024,2048]{1,0:T(8,128)(2,1)} %all-gather.19.cloned.1.call-done, f32[2048,1024]{1,0:T(8,128)} %get-tuple-element.146), kind=kOutput, calls=%fused_computation.12 | convolution fusion | flops 8613003264 | bytes 20971520 | tf_op jit(solution)/shard_map/dot_general | solution.py:284
  629.3 72.6 %reduce-scatter.14.cloned.1.call-done = bf16[256,2048]{1,0:T(8,128)(2,1)} async-done(((bf16[2048,2048]{1,0:T(8,128)(2,1)}), bf16[256,2048]{1,0:T(8,128)(2,1)}) %reduce-scatter.14.cloned.1.call-update) | async-done | bytes 1048592 | tf_op jit(solution)/shard_map/reduce_scatter | solution.py:277
  701.9 2.8 fusion.18
  704.8 87.2 %reduce-scatter.12.cloned.1.call-done = bf16[256,2048]{1,0:T(8,128)(2,1)} async-done(((bf16[2048,2048]{1,0:T(8,128)(2,1)}), bf16[256,2048]{1,0:T(8,128)(2,1)}) %reduce-scatter.12.cloned.1.call-update) | async-done | bytes 1048592 | tf_op jit(solution)/shard_map/reduce_scatter | solution.py:283
  792.0 4.2 fusion.35
  796.2 1.3 copy-done.21
  797.5 1.3 fusion.25
  799.0 16.0 %convolution_convert_fusion.4 = bf16[1024,2048]{1,0:T(8,128)(2,1)} fusion(bf16[2048,2048]{1,0:T(8,128)(2,1)} %all-gather.21.cloned.1.call-done, f32[2048,1024]{1,0:T(8,128)} %get-tuple-element.146), kind=kOutput, calls=%fused_computation.14 | convolution fusion | flops 8610906112 | bytes 20971520 | tf_op jit(solution)/shard_map/rf,rd->fd/dot_general | solution.py:297
  815.2 14.1 %convolution_convert_fusion.5 = bf16[2048,1024]{1,0:T(8,128)(2,1)} fusion(bf16[2048,2048]{1,0:T(8,128)(2,1)} %all-gather.15.cloned.1.call-done, bf16[2048,1024]{1,0:T(8,128)(2,1)} %copy-done.39), kind=kOutput, calls=%fused_computation.15 | convolution fusion | flops 8592031744 | bytes 16777216 | tf_op jit(solution)/shard_map/rd,rf->df/dot_general | solution.py:298
  829.3 50.1 %all-gather.23.cloned.1.call-done = bf16[2048,2048]{1,0:T(8,128)(2,1)} async-done(((bf16[256,2048]{1,0:T(8,128)(2,1)}), bf16[2048,2048]{1,0:T(8,128)(2,1)}) %all-gather.23.cloned.1.call-update) | async-done | bytes 8388624 | tf_op jit(solution)/shard_map/all_gather | solution.py:293
  879.5 5.7 convolution_convert_fusion.8
  886.3 4.3 all-to-all-start.1
  891.9 7.3 convolution_convert_fusion.9.do_ref
  899.3 36.3 %shard_map.320 = (bf16[2048,256]{1,0:T(8,128)(2,1)S(1)}, bf16[2048,256]{1,0:T(8,128)(2,1)S(1)}, bf16[2048,256]{1,0:T(8,128)(2,1)S(1)}) custom-call(s32[1]{0:T(128)} %copy.61.len_ref, bf16[2048,256]{1,0:T(8,128)(2,1)S(1)} %copy-done.12, bf16[2048,256]{1,0:T(8,128)(2,1)S(1)} %copy-done.10, bf16[2048,256]{1,0:T(8,128)(2,1)} %copy-done.8, ...), custom_call_target="tpu_custom_call" | custom-call | flops 5368709120 | bytes 8388608 | tf_op jit(solution)/shard_map/pallas_call | solution.py:147
  938.8 11.4 convolution_convert_fusion.7
  950.5 11.5 convolution_convert_fusion
  962.0 1.6 copy-done.5
  963.6 1.2 copy-done.13
  964.9 7.9 shard_map.324
  972.7 17.9 %reduce-scatter.24.cloned.1.call-done.g_ref = bf16[512,1024]{1,0:T(8,128)(2,1)} async-done(((bf16[2048,1024]{1,0:T(8,128)(2,1)}), bf16[512,1024]{1,0:T(8,128)(2,1)}) %reduce-scatter.24.cloned.1.call-update) | async-done | bytes 1048592 | tf_op jit(solution)/shard_map/reduce_scatter | solution.py:319
  990.6 1.6 copy-done.2
  992.2 1.6 copy-done.6
  993.8 1.2 copy-done.14
  995.0 8.2 shard_map.323
  1003.2 20.5 %reduce-scatter.18.cloned.1.call-done = bf16[1,50,256]{2,1,0:T(8,128)(2,1)} async-done(((bf16[1,50,2048]{2,1,0:T(8,128)(2,1)}), bf16[1,50,256]{2,1,0:T(8,128)(2,1)}) %reduce-scatter.18.cloned.1.call-update) | async-done | bytes 25616 | tf_op jit(solution)/shard_map/reduce_scatter | solution.py:332
  1023.7 1.4 convert_reduce_fusion.1
  1025.2 27.5 %reduce-scatter.22.cloned.1.call-done.g_ref = bf16[512,256]{1,0:T(8,128)(2,1)} async-done(((bf16[2048,256]{1,0:T(8,128)(2,1)}), bf16[512,256]{1,0:T(8,128)(2,1)}) %reduce-scatter.22.cloned.1.call-update) | async-done | bytes 262160 | tf_op jit(solution)/shard_map/reduce_scatter | solution.py:318
  1053.6 6.0 shard_map.322
  1059.6 40.4 %reduce-scatter.20.cloned.1.call-done = bf16[512,768]{1,0:T(8,128)(2,1)} async-done(((bf16[2048,768]{1,0:T(8,128)(2,1)}), bf16[512,768]{1,0:T(8,128)(2,1)}) %reduce-scatter.20.cloned.1.call-update) | async-done | bytes 786448 | tf_op jit(solution)/shard_map/reduce_scatter | solution.py:317
  1100.1 1.4 copy.50
  1101.9 1.4 copy-done.7
  1103.3 7.0 shard_map.321
  1110.3 81.6 %reduce-scatter.16.cloned.1.call-done = bf16[256,2048]{1,0:T(8,128)(2,1)} async-done(((bf16[2048,2048]{1,0:T(8,128)(2,1)}), bf16[256,2048]{1,0:T(8,128)(2,1)}) %reduce-scatter.16.cloned.1.call-update) | async-done | bytes 1048592 | tf_op jit(solution)/shard_map/reduce_scatter | solution.py:303
  1191.8 1.8 fusion.21
  1193.6 2.3 fusion.19
  1195.9 38.5 %all-reduce = (f32[]{:T(128)}, f32[2048]{0:T(1024)S(1)}, f32[2,2048]{1,0:T(2,128)S(1)}) all-reduce(f32[]{:T(128)} %get-tuple-element.131, f32[2048]{0:T(1024)S(1)} %bitcast.71, f32[2,2048]{1,0:T(2,128)S(1)} %pad_maximum_fusion), channel_id=1, replica_groups=mesh['dp'=4,'mp'=8] {'dp','mp'}, use_global_device_ids=true, to_apply=%region_16.17 | all-reduce | flops 6145 | bytes 49160 | tf_op jit(solution)/shard_map/psum | solution.py:341
  1238.0 3.9 add_add_fusion.2
  (142 shorter events, 14.2 us)
Async XLA Ops:
  7.2 4.7 copy-start.17
  7.2 32.6 %all-gather.13.cloned.1.call-start = ((), (), s32[]{:S(2)}) async-start(), calls=%async_computation.13 | async-start | bytes 1310720 | tf_op jit(solution)/shard_map/all_gather | solution.py:255
  9.1 3.4 copy-start.29
  9.1 76.9 %all-gather.11.cloned.1.call-start = ((), (), s32[]{:S(2)}) async-start(), calls=%async_computation.12 | async-start | bytes 3932160 | tf_op jit(solution)/shard_map/all_gather | solution.py:247
  11.8 158.5 %all-gather.9.cloned.1.call-start = ((), (), s32[]{:S(2)}) async-start(), calls=%async_computation.11 | async-start | bytes 9437184 | tf_op jit(solution)/shard_map/all_gather | solution.py:246
  12.1 27.7 %copy-start.32 = (f32[256]{0:T(256)}, f32[256]{0:T(256)S(1)}, u32[]{:S(2)}) copy-start(f32[256]{0:T(256)S(1)} %broadcast_multiply_fusion.2) | copy-start | bytes 3076
  12.5 59.8 %copy-start.36 = (f32[256]{0:T(256)}, f32[256]{0:T(256)S(1)}, u32[]{:S(2)}) copy-start(f32[256]{0:T(256)S(1)} %fusion.20) | copy-start | bytes 3076
  12.6 59.7 %copy-start.34 = (f32[256]{0:T(256)}, f32[256]{0:T(256)S(1)}, u32[]{:S(2)}) copy-start(f32[256]{0:T(256)S(1)} %fusion.33) | copy-start | bytes 3076
  12.6 59.7 %copy-start.26 = (f32[1,2048]{1,0:T(1,128)}, f32[1,2048]{1,0:T(1,128)S(1)}, u32[]{:S(2)}) copy-start(f32[1,2048]{1,0:T(1,128)S(1)} %get-tuple-element.142) | copy-start | bytes 24580
  39.8 31.2 %all-to-all-start = ((bf16[8,256,256]{2,1,0:T(8,128)(2,1)}), bf16[8,256,256]{2,1,0:T(8,128)(2,1)S(1)}, u32[]{:S(2)}, u32[]{:S(2)}) async-start(bf16[8,256,256]{2,1,0:T(8,128)(2,1)} %bitcast.61), calls=%async_computation | async-start | bytes 2097152 | tf_op jit(solution)/shard_map/all_to_all | solution.py:256
  44.4 258.8 %reduce-scatter.10.cloned.1.call-start = ((), (), s32[]{:S(2)}) async-start(), calls=%async_computation.14 | async-start | bytes 9437184 | tf_op jit(solution)/shard_map/reduce_scatter | solution.py:263
  180.7 28.6 %copy-start.8 = (bf16[2048,256]{1,0:T(8,128)(2,1)}, bf16[2048,256]{1,0:T(8,128)(2,1)S(1)}, u32[]{:S(2)}) copy-start(bf16[2048,256]{1,0:T(8,128)(2,1)S(1)} %get-tuple-element.137.v_ref) | copy-start | bytes 3145732
  180.7 28.6 %copy-start.9 = (bf16[2048,256]{1,0:T(8,128)(2,1)}, bf16[2048,256]{1,0:T(8,128)(2,1)S(1)}, u32[]{:S(2)}) copy-start(bf16[2048,256]{1,0:T(8,128)(2,1)S(1)} %get-tuple-element.138.k_ref) | copy-start | bytes 3145732
  180.7 28.6 %copy-start.11 = (bf16[2048,256]{1,0:T(8,128)(2,1)}, bf16[2048,256]{1,0:T(8,128)(2,1)S(1)}, u32[]{:S(2)}) copy-start(bf16[2048,256]{1,0:T(8,128)(2,1)S(1)} %get-tuple-element.139.q_ref) | copy-start | bytes 3145732
  180.7 28.6 %copy-start.25 = (bf16[256,8,256]{0,2,1:T(8,128)(2,1)S(1)}, bf16[256,8,256]{0,2,1:T(8,128)(2,1)}, u32[]{:S(2)}) copy-start(bf16[256,8,256]{0,2,1:T(8,128)(2,1)} %copy.49) | copy-start | bytes 3145732
  209.2 670.2 %copy-start = (bf16[2048,256]{1,0:T(8,128)(2,1)}, bf16[2048,256]{1,0:T(8,128)(2,1)S(1)}, u32[]{:S(2)}) copy-start(bf16[2048,256]{1,0:T(8,128)(2,1)S(1)} %get-tuple-element.42.o_ref) | copy-start | bytes 3145732
  214.9 1.6 copy-start.1
  214.9 141.5 %all-gather.19.cloned.1.call-start = ((), (), s32[]{:S(2)}) async-start(), calls=%async_computation.17 | async-start | bytes 5242880 | tf_op jit(solution)/shard_map/all_gather | solution.py:258
  217.6 222.9 %all-gather.21.cloned.1.call-start = ((), (), s32[]{:S(2)}) async-start(), calls=%async_computation.19 | async-start | bytes 9437184 | tf_op jit(solution)/shard_map/all_gather | solution.py:262
  220.1 274.2 %all-gather.17.cloned.1.call-start = ((), (), s32[]{:S(2)}) async-start(), calls=%async_computation.16 | async-start | bytes 5242880 | tf_op jit(solution)/shard_map/all_gather | solution.py:257
  222.9 355.6 %all-gather.15.cloned.1.call-start = ((), (), s32[]{:S(2)}) async-start(), calls=%async_computation.15 | async-start | bytes 9437184 | tf_op jit(solution)/shard_map/all_gather | solution.py:270
  303.2 4.1 copy-start.18
  303.2 4.1 copy-start.20
  308.8 393.2 %reduce-scatter.14.cloned.1.call-start = ((), (), s32[]{:S(2)}) async-start(), calls=%async_computation.20 | async-start | bytes 9437184 | tf_op jit(solution)/shard_map/reduce_scatter | solution.py:277
  578.5 24.2 %copy-start.38 = (bf16[2048,1024]{1,0:T(8,128)(2,1)S(1)}, bf16[2048,1024]{1,0:T(8,128)(2,1)}, u32[]{:S(2)}) copy-start(bf16[2048,1024]{1,0:T(8,128)(2,1)} %all-gather.17.cloned.1.call-done) | copy-start | bytes 12582916
  600.7 2.0 copy-start.39
  613.6 178.4 %reduce-scatter.12.cloned.1.call-start = ((), (), s32[]{:S(2)}) async-start(), calls=%async_computation.18 | async-start | bytes 9437184 | tf_op jit(solution)/shard_map/reduce_scatter | solution.py:283
  629.2 250.2 %all-gather.23.cloned.1.call-start = ((), (), s32[]{:S(2)}) async-start(), calls=%async_computation.21 | async-start | bytes 9437184 | tf_op jit(solution)/shard_map/all_gather | solution.py:293
  792.0 5.5 copy-start.23
  796.2 1.3 copy-start.21
  798.9 163.1 %reduce-scatter.26.cloned.1.call-start = ((), (), s32[]{:S(2)}) async-start(), calls=%async_computation.27 | async-start | bytes 5242880 | tf_op jit(solution)/shard_map/reduce_scatter | solution.py:320
  815.0 175.6 %reduce-scatter.24.cloned.1.call-start = ((), (), s32[]{:S(2)}) async-start(), calls=%async_computation.26 | async-start | bytes 5242880 | tf_op jit(solution)/shard_map/reduce_scatter | solution.py:319
  885.2 5.4 copy-start.24
  886.3 51.4 %all-to-all-start.1 = ((bf16[256,8,256]{2,0,1:T(8,128)(2,1)}), bf16[256,8,256]{2,0,1:T(8,128)(2,1)}, u32[]{:S(2)}, u32[]{:S(2)}) async-start(bf16[256,8,256]{2,0,1:T(8,128)(2,1)} %bitcast.50), calls=%async_computation.7 | async-start | bytes 2097152 | tf_op jit(solution)/shard_map/all_to_all | solution.py:313
  890.5 133.2 %reduce-scatter.18.cloned.1.call-start = ((), (), s32[]{:S(2)}) async-start(), calls=%async_computation.23 | async-start | bytes 258048 | tf_op jit(solution)/shard_map/reduce_scatter | solution.py:332
  891.6 161.0 %reduce-scatter.22.cloned.1.call-start = ((), (), s32[]{:S(2)}) async-start(), calls=%async_computation.25 | async-start | bytes 1310720 | tf_op jit(solution)/shard_map/reduce_scatter | solution.py:318
  891.9 7.4 copy-start.10
  891.9 7.4 copy-start.12
  937.7 162.4 %reduce-scatter.20.cloned.1.call-start = ((), (), s32[]{:S(2)}) async-start(), calls=%async_computation.24 | async-start | bytes 3932160 | tf_op jit(solution)/shard_map/reduce_scatter | solution.py:317
  950.2 241.6 %reduce-scatter.16.cloned.1.call-start = ((), (), s32[]{:S(2)}) async-start(), calls=%async_computation.22 | async-start | bytes 9437184 | tf_op jit(solution)/shard_map/reduce_scatter | solution.py:303
  962.0 1.6 copy-start.5
  963.6 1.2 copy-start.13
  990.6 1.6 copy-start.2
  992.2 1.6 copy-start.6
  993.8 1.2 copy-start.14
  995.0 57.6 %copy-start.4 = (f32[512,256]{1,0:T(8,128)S(1)}, f32[512,256]{1,0:T(8,128)}, u32[]{:S(2)}) copy-start(f32[512,256]{1,0:T(8,128)} %w_ref.5) | copy-start | bytes 1572868
  995.0 57.6 %copy-start.15 = (f32[2,1,4,64,64]{4,3,2,1,0:T(8,128)S(1)}, f32[2,1,4,64,64]{4,3,2,1,0:T(8,128)}, u32[]{:S(2)}) copy-start(f32[2,1,4,64,64]{4,3,2,1,0:T(8,128)} %r_ref.5) | copy-start | bytes 393220
  1052.7 1.0 copy-start.16
  1059.6 42.2 %copy-start.3 = (f32[512,768]{1,0:T(8,128)S(1)}, f32[512,768]{1,0:T(8,128)}, u32[]{:S(2)}) copy-start(f32[512,768]{1,0:T(8,128)} %w_ref.4) | copy-start | bytes 4718596
  1101.8 1.4 copy-start.7
  1103.3 88.6 %copy-start.19 = (bf16[256,2048]{1,0:T(8,128)(2,1)S(1)}, bf16[256,2048]{1,0:T(8,128)(2,1)}, u32[]{:S(2)}) copy-start(bf16[256,2048]{1,0:T(8,128)(2,1)} %param.16) | copy-start | bytes 3145732
  1103.3 88.6 %copy-start.27 = (f32[1,2048]{1,0:T(1,128)S(1)}, f32[1,2048]{1,0:T(1,128)}, u32[]{:S(2)}) copy-start(f32[1,2048]{1,0:T(1,128)} %copy-done.26) | copy-start | bytes 24580
  1103.3 88.6 %copy-start.33 = (f32[256]{0:T(256)S(1)}, f32[256]{0:T(256)}, u32[]{:S(2)}) copy-start(f32[256]{0:T(256)} %copy-done.32) | copy-start | bytes 3076
  1103.3 90.3 %copy-start.37 = (f32[256]{0:T(256)S(1)}, f32[256]{0:T(256)}, u32[]{:S(2)}) copy-start(f32[256]{0:T(256)} %copy-done.36) | copy-start | bytes 3076
  1103.3 90.4 %copy-start.35 = (f32[256]{0:T(256)S(1)}, f32[256]{0:T(256)}, u32[]{:S(2)}) copy-start(f32[256]{0:T(256)} %copy-done.34) | copy-start | bytes 3076
  1110.2 126.3 %copy-start.30 = (f32[2,2048]{1,0:T(2,128)S(1)}, f32[2,2048]{1,0:T(2,128)}, u32[]{:S(2)}) copy-start(f32[2,2048]{1,0:T(2,128)} %param.19) | copy-start | bytes 49156
  1110.2 127.1 %copy-start.28 = (bf16[1,50,256]{2,1,0:T(8,128)(2,1)S(1)}, bf16[1,50,256]{2,1,0:T(8,128)(2,1)}, u32[]{:S(2)}) copy-start(bf16[1,50,256]{2,1,0:T(8,128)(2,1)} %reduce-scatter.18.cloned.1.call-done) | copy-start | bytes 76804
  1110.2 127.7 %copy-start.22 = (f32[256,2048]{1,0:T(8,128)S(1)}, f32[256,2048]{1,0:T(8,128)}, u32[]{:S(2)}) copy-start(f32[256,2048]{1,0:T(8,128)} %copy-done.21) | copy-start | bytes 6291460
  1234.4 7.5 copy-start.31
Sparse Core Ops, SparseCore 0:
  10.5 29.3 all-gather.12
  42.2 43.8 all-gather.10
  88.3 82.0 all-gather.8
  215.0 88.1 reduce-scatter.9
  305.4 50.9 all-gather.18
  358.4 82.0 all-gather.20
  442.9 51.2 all-gather.16
  496.4 82.0 all-gather.14
  613.8 88.1 reduce-scatter.13
  704.1 87.9 reduce-scatter.11
  799.0 80.4 all-gather.22
  882.9 51.1 reduce-scatter.25
  937.9 52.6 reduce-scatter.23
  993.3 30.3 reduce-scatter.17
  1026.7 25.8 reduce-scatter.21
  1056.1 43.9 reduce-scatter.19
  1102.2 89.5 reduce-scatter.15

commit v2 on v1

--- a/solution.py
+++ b/solution.py
@@ -155,6 +155,533 @@
     )(seg_len,q,k,v,o,do,lse)
 
 
+MESH = pl.DeviceIdType.MESH
+HBM = pl.BlockSpec(memory_space=pl.ANY)
+VM = pl.BlockSpec(memory_space=pltpu.VMEM)
+DMA = pltpu.SemaphoreType.DMA
+
+
+def on_mp(index):
+    return (lax.axis_index("dp"), index)
+
+
+def on_dp(index):
+    return (index, lax.axis_index("mp"))
+
+
+def remote(src, dst, send, recv, device):
+    return pltpu.make_async_remote_copy(
+        src_ref=src,
+        dst_ref=dst,
+        send_sem=send,
+        recv_sem=recv,
+        device_id=device,
+        device_id_type=MESH,
+    )
+
+
+def local(src, dst, sem):
+    copy = pltpu.make_async_copy(src, dst, sem)
+    copy.start()
+    return copy
+
+
+class Line:
+    def __init__(self, mp_count):
+        self.n = mp_count // 2
+        self.me = lax.axis_index("mp")
+        self.chip = self.me // 2
+        self.core = self.me % 2
+        self.twin = on_mp(2 * self.chip + 1 - self.core)
+        self.right = on_mp(self.me + 2)
+        self.left = on_mp(self.me - 2)
+        self.has_right = self.chip < self.n - 1
+        self.has_left = self.chip > 0
+
+    def greet(self, others=()):
+        barrier = pltpu.get_barrier_semaphore()
+
+        def hello(device):
+            pl.semaphore_signal(barrier, inc=1, device_id=device, device_id_type=MESH)
+
+        hello(self.twin)
+        for device in others:
+            hello(device)
+        pl.when(self.has_right)(lambda: hello(self.right))
+        pl.when(self.has_left)(lambda: hello(self.left))
+        met = 1 + len(others) + self.has_right.astype(jnp.int32) + self.has_left.astype(jnp.int32)
+        pl.semaphore_wait(barrier, met)
+
+
+class Gather:
+    def __init__(self, line, own, full, recv, sends, sem):
+        self.line, self.own, self.full, self.recv, self.sends, self.sem = (
+            line,
+            own,
+            full,
+            recv,
+            sends,
+            sem,
+        )
+
+    def copy(self, src, block, way, k):
+        line = self.line
+        device = (line.right, line.left, line.twin)[way]
+        return remote(
+            src, self.full.at[block], self.sends.at[way, k], self.recv.at[block], device
+        )
+
+    def start(self):
+        line = self.line
+        mine = self.copy
+        pl.when(line.has_right)(lambda: mine(self.own, line.me, 0, 0).start())
+        pl.when(line.has_left)(lambda: mine(self.own, line.me, 1, 0).start())
+        mine(self.own, line.me, 2, line.chip).start()
+        local(self.own, self.full.at[line.me], self.sem).wait()
+
+    def arrived(self, block):
+        self.copy(self.own, block, 2, 0).wait_recv()
+
+    def forward(self, away):
+        line = self.line
+
+        def take(chip, way, onward):
+            block = 2 * chip + line.core
+            self.arrived(block)
+            got = self.full.at[block]
+            pl.when(onward)(lambda: self.copy(got, block, way, away).start())
+            self.copy(got, block, 2, chip).start()
+
+        pl.when(line.chip >= away)(lambda: take(line.chip - away, 0, line.has_right))
+        pl.when(line.chip + away < line.n)(lambda: take(line.chip + away, 1, line.has_left))
+
+    def each(self, away, use, core):
+        line = self.line
+        pl.when(line.chip >= away)(lambda: use(2 * (line.chip - away) + core))
+        pl.when(line.chip + away < line.n)(lambda: use(2 * (line.chip + away) + core))
+
+    def run(self, use):
+        line = self.line
+        self.start()
+        use(line.me)
+
+        def from_twin(block):
+            self.arrived(block)
+            use(block)
+
+        from_twin(2 * line.chip + 1 - line.core)
+
+        def step(away, _):
+            self.forward(away)
+            self.each(away, use, line.core)
+            self.each(away, from_twin, 1 - line.core)
+            return 0
+
+        lax.fori_loop(1, line.n, step, 0)
+        self.finish()
+
+    def finish(self):
+        line = self.line
+
+        def sent(away, _):
+            wait = lambda way, k: self.copy(self.own, line.me, way, k).wait_send()
+            pl.when(line.has_right & (line.chip >= away))(lambda: wait(0, away))
+            pl.when(line.has_left & (line.chip + away < line.n))(lambda: wait(1, away))
+            wait(2, away)
+            return 0
+
+        lax.fori_loop(0, line.n, sent, 0)
+
+
+def gather_sems(mp_count):
+    return [DMA((mp_count,)), DMA((3, mp_count // 2)), DMA(())]
+
+
+def gather_kernel(mp_count, own, full, recv, sends, sem):
+    line = Line(mp_count)
+    line.greet()
+    Gather(line, own, full, recv, sends, sem).run(lambda block: None)
+
+
+def gather_rows(own, mp_count, cid):
+    rows, width = own.shape
+    return pl.pallas_call(
+        functools.partial(gather_kernel, mp_count),
+        in_specs=[HBM],
+        out_specs=HBM,
+        out_shape=jax.ShapeDtypeStruct((mp_count, rows, width), own.dtype),
+        scratch_shapes=gather_sems(mp_count),
+        compiler_params=pltpu.CompilerParams(collective_id=cid, has_side_effects=True),
+        cost_estimate=pl.CostEstimate(
+            flops=0, bytes_accessed=25 * mp_count * rows * width, transcendentals=0
+        ),
+    )(own)
+
+
+def qkv_kernel(
+    dp_count, mp_count, own, w_own, full, q_out, k_out, v_out, w_full,
+    w, x, y, recv, sends, sem, w_recv, w_send, w_sem, io_sem
+):
+    line = Line(mp_count)
+    dp = lax.axis_index("dp")
+    peers = [lax.rem(dp + k, dp_count) for k in range(1, dp_count)]
+    line.greet([on_dp(peer) for peer in peers])
+    rows = own.shape[0]
+    part = w_own.shape[1]
+
+    def place(ref, index):
+        return ref.at[:, pl.ds(pl.multiple_of(index * part, part), part), :]
+
+    def weight_copy(k, index):
+        return remote(
+            w_own, place(w_full, index), w_send.at[k], w_recv.at[index], on_dp(peers[k])
+        )
+
+    for k in range(dp_count - 1):
+        weight_copy(k, dp).start()
+    mine = local(w_own, place(w_full, dp), w_sem)
+    gather = Gather(line, own, full, recv, sends, sem)
+    gather.start()
+    mine.wait()
+    for k in range(dp_count - 1):
+        weight_copy(k, peers[k]).wait_recv()
+    local(w_full, w, w_sem).wait()
+
+    def use(block):
+        local(full.at[block], x, io_sem.at[0]).wait()
+        at = pl.ds(pl.multiple_of(block * rows, rows), rows)
+        copies = []
+        for j, ref in enumerate((q_out, k_out, v_out)):
+            y[j] = jnp.dot(x[...], w[j], preferred_element_type=F32).astype(BF)
+            copies.append(local(y.at[j], ref.at[at, :], io_sem.at[j]))
+        for copy in copies:
+            copy.wait()
+
+    use(line.me)
+
+    def from_twin(block):
+        gather.arrived(block)
+        use(block)
+
+    gather.forward(1)
+    from_twin(2 * line.chip + 1 - line.core)
+
+    def step(away, _):
+        pl.when(away > 1)(lambda: gather.forward(away))
+        gather.each(away, use, line.core)
+        gather.each(away, from_twin, 1 - line.core)
+        return 0
+
+    lax.fori_loop(1, line.n, step, 0)
+    gather.finish()
+    for k in range(dp_count - 1):
+        weight_copy(k, dp).wait_send()
+
+
+def gather_qkv(own, w_own, dp_count, mp_count, cid):
+    rows, width = own.shape
+    _, part, hw = w_own.shape
+    depth = part * dp_count
+    head = jax.ShapeDtypeStruct((mp_count * rows, hw), BF)
+    return pl.pallas_call(
+        functools.partial(qkv_kernel, dp_count, mp_count),
+        in_specs=[HBM, HBM],
+        out_specs=[HBM] * 5,
+        out_shape=[
+            jax.ShapeDtypeStruct((mp_count, rows, width), BF),
+            head,
+            head,
+            head,
+            jax.ShapeDtypeStruct((3, depth, hw), BF),
+        ],
+        scratch_shapes=[
+            pltpu.VMEM((3, depth, hw), BF),
+            pltpu.VMEM((rows, width), BF),
+            pltpu.VMEM((3, rows, hw), BF),
+            *gather_sems(mp_count),
+            DMA((dp_count,)),
+            DMA((dp_count,)),
+            DMA(()),
+            DMA((3,)),
+        ],
+        compiler_params=pltpu.CompilerParams(
+            collective_id=cid, has_side_effects=True, vmem_limit_bytes=40 << 20
+        ),
+        cost_estimate=pl.CostEstimate(
+            flops=6 * mp_count * rows * depth * hw,
+            bytes_accessed=25 * mp_count * rows * width,
+            transcendentals=0,
+        ),
+    )(own, w_own)
+
+
+def exchange_kernel(mp_count, x, y, send, recv, sem):
+    me = lax.axis_index("mp")
+    barrier = pltpu.get_barrier_semaphore()
+    peers = [lax.rem(me + k, mp_count) for k in range(1, mp_count)]
+    for peer in peers:
+        pl.semaphore_signal(barrier, inc=1, device_id=on_mp(peer), device_id_type=MESH)
+    pl.semaphore_wait(barrier, mp_count - 1)
+
+    def copy(k, index):
+        return remote(x.at[peers[k]], y.at[index], send.at[k], recv.at[index], on_mp(peers[k]))
+
+    for k in range(mp_count - 1):
+        copy(k, me).start()
+    local(x.at[me], y.at[me], sem).wait()
+    for k in range(mp_count - 1):
+        copy(k, peers[k]).wait_recv()
+    for k in range(mp_count - 1):
+        copy(k, me).wait_send()
+
+
+def exchange(x, mp_count, cid):
+    return pl.pallas_call(
+        functools.partial(exchange_kernel, mp_count),
+        in_specs=[HBM],
+        out_specs=HBM,
+        out_shape=jax.ShapeDtypeStruct(x.shape, x.dtype),
+        scratch_shapes=[DMA((mp_count,)), DMA((mp_count,)), DMA(())],
+        compiler_params=pltpu.CompilerParams(collective_id=cid, has_side_effects=True),
+        cost_estimate=pl.CostEstimate(flops=0, bytes_accessed=40 * x.size, transcendentals=0),
+    )(x)
+
+
+class Scatter:
+    def __init__(self, line, both, slots, stage, tmp, twin_sems, slot_recv, sends):
+        self.line, self.both, self.slots, self.stage, self.tmp = line, both, slots, stage, tmp
+        self.twin_sems, self.slot_recv, self.sends = twin_sems, slot_recv, sends
+
+    def add(self, chip, other, out=None):
+        rows = self.both.shape[1]
+        step = 32
+
+        def body(i, _):
+            at = pl.ds(pl.multiple_of(i * step, step), step)
+            total = self.both[chip, at, :].astype(F32) + other(at)
+            if out is None:
+                self.both[chip, at, :] = total.astype(BF)
+            else:
+                out[at, :] = total
+            return 0
+
+        lax.fori_loop(0, rows // step, body, 0)
+
+    def make(self, chip, block_sum):
+        line = self.line
+        copy = remote(
+            self.stage,
+            self.both.at[chip],
+            self.twin_sems.at[0, chip],
+            self.twin_sems.at[1, chip],
+            line.twin,
+        )
+        block_sum(2 * chip + 1 - line.core, self.stage)
+        copy.start()
+        block_sum(2 * chip + line.core, self.tmp)
+        copy.wait()
+        self.add(chip, lambda at: self.tmp[at, :].astype(F32))
+
+    def onward(self, chip, slot, way, away):
+        line = self.line
+        device = (line.right, line.left)[way]
+        return remote(
+            self.both.at[chip],
+            self.slots.at[slot],
+            self.sends.at[way, away],
+            self.slot_recv.at[slot],
+            device,
+        )
+
+    def arrived(self, slot):
+        self.onward(0, slot, 0, 0).wait_recv()
+
+    def pass_on(self, away):
+        line = self.line
+
+        def take(chip, way, fed):
+            def join():
+                self.arrived(chip)
+                self.add(chip, lambda at: self.slots[chip, at, :].astype(F32))
+
+            pl.when(fed)(join)
+            last = jnp.where(away == 1, line.n, chip) if way == 1 else chip
+            self.onward(chip, last, way, away).start()
+
+        pl.when(line.chip + away < line.n)(lambda: take(line.chip + away, 0, line.has_left))
+        pl.when(line.chip >= away)(lambda: take(line.chip - away, 1, line.has_right))
+
+    def each(self, away, block_sum):
+        line = self.line
+        pl.when(line.chip + away < line.n)(lambda: self.make(line.chip + away, block_sum))
+        pl.when(line.chip >= away)(lambda: self.make(line.chip - away, block_sum))
+
+    def last(self, out):
+        line = self.line
+
+        def join():
+            self.arrived(line.chip)
+            self.add(line.chip, lambda at: self.slots[line.chip, at, :].astype(F32))
+
+        pl.when(line.has_left & line.has_right)(join)
+        end = jnp.where(line.has_right, line.n, line.chip)
+        self.arrived(end)
+        self.add(line.chip, lambda at: self.slots[end, at, :].astype(F32), out)
+
+        def sent(away, _):
+            wait = lambda way: self.onward(0, 0, way, away).wait_send()
+            pl.when(line.chip + away < line.n)(lambda: wait(0))
+            pl.when(line.chip >= away)(lambda: wait(1))
+            return 0
+
+        lax.fori_loop(1, line.n, sent, 0)
+
+    def run(self, block_sum, out, between=lambda part: None):
+        line = self.line
+
+        def step(k, _):
+            away = line.n - 1 - k
+            self.each(away, block_sum)
+            self.pass_on(away)
+            return 0
+
+        lax.fori_loop(0, line.n - 2, step, 0)
+        self.each(1, block_sum)
+        self.make(line.chip, block_sum)
+        between(0)
+        self.pass_on(1)
+        between(1)
+        self.last(out)
+
+
+def scatter_scratch(mp_count, rows, width):
+    n = mp_count // 2
+    return [
+        pltpu.VMEM((n, rows, width), BF),
+        pltpu.VMEM((n + 1, rows, width), BF),
+        pltpu.VMEM((rows, width), BF),
+        pltpu.VMEM((rows, width), BF),
+        DMA((2, n)),
+        DMA((n + 1,)),
+        DMA((2, n)),
+    ]
+
+
+def tiled(width, size=512):
+    return [slice(at, min(at + size, width)) for at in range(0, width, size)]
+
+
+def d_normed_kernel(mp_count, dq, dk, dv, w, out, *scratch):
+    line = Line(mp_count)
+    line.greet()
+    rows, width = out.shape
+
+    def block_sum(block, ref):
+        at = pl.ds(pl.multiple_of(block * rows, rows), rows)
+        for cols in tiled(width):
+            total = dg(dq[at, :], w[0, cols, :], NT)
+            total += dg(dk[at, :], w[1, cols, :], NT)
+            total += dg(dv[at, :], w[2, cols, :], NT)
+            ref[:, cols] = total.astype(BF)
+
+    Scatter(line, *scratch).run(block_sum, out)
+
+
+def scatter_d_normed(dq, dk, dv, w, mp_count, cid):
+    rows = dq.shape[0] // mp_count
+    width = w.shape[1]
+    return pl.pallas_call(
+        functools.partial(d_normed_kernel, mp_count),
+        in_specs=[VM] * 4,
+        out_specs=VM,
+        out_shape=jax.ShapeDtypeStruct((rows, width), F32),
+        scratch_shapes=scatter_scratch(mp_count, rows, width),
+        compiler_params=pltpu.CompilerParams(
+            collective_id=cid, has_side_effects=True, vmem_limit_bytes=60 << 20
+        ),
+        cost_estimate=pl.CostEstimate(
+            flops=6 * dq.size * width, bytes_accessed=25 * dq.shape[0] * width, transcendentals=0
+        ),
+    )(dq, dk, dv, w)
+
+
+GELU_C = math.sqrt(2.0 / math.pi)
+
+
+def ffn_kernel(
+    mp_count, x_all, u_all, up, down, out, hid_out, pre_out, part_out,
+    x, u, hid, pre, part, io_sem, *scratch
+):
+    line = Line(mp_count)
+    line.greet()
+    rows, width = out.shape
+    units = up.shape[1]
+
+    def block_sum(block, ref):
+        at = pl.ds(pl.multiple_of(block * rows, rows), rows)
+        first = local(x_all.at[block], x, io_sem.at[0])
+        second = local(u_all.at[block], u, io_sem.at[1])
+        first.wait()
+        second.wait()
+        for cols in tiled(units, 256):
+            value = dg(x[...], up[:, cols], NN)
+            d_hidden = dg(u[...], down[cols, :], NT)
+            square = value * value
+            bend = jnp.tanh(GELU_C * (value + 0.044715 * value * square))
+            half = 0.5 * (1.0 + bend)
+            hid[:, cols] = (value * half).astype(BF)
+            slope = half + 0.5 * value * (1.0 - bend * bend) * (
+                GELU_C * (1.0 + 3.0 * 0.044715 * square)
+            )
+            pre[:, cols] = (d_hidden * slope).astype(BF)
+        copies = [
+            local(hid, hid_out.at[at, :], io_sem.at[0]),
+            local(pre, pre_out.at[at, :], io_sem.at[1]),
+        ]
+        for cols in tiled(width):
+            ref[:, cols] = dg(pre[...], up[cols, :], NT).astype(BF)
+            part[:, cols] = dg(hid[...], down[:, cols], NN).astype(BF)
+        copies.append(local(part, part_out.at[at, :], io_sem.at[2]))
+        for copy in copies:
+            copy.wait()
+
+    Scatter(line, *scratch).run(block_sum, out)
+
+
+def ffn(x_all, u_all, up, down, mp_count, cid):
+    _, rows, width = x_all.shape
+    units = up.shape[1]
+    total = mp_count * rows
+    return pl.pallas_call(
+        functools.partial(ffn_kernel, mp_count),
+        in_specs=[HBM, HBM, VM, VM],
+        out_specs=[VM, HBM, HBM, HBM],
+        out_shape=[
+            jax.ShapeDtypeStruct((rows, width), F32),
+            jax.ShapeDtypeStruct((total, units), BF),
+            jax.ShapeDtypeStruct((total, units), BF),
+            jax.ShapeDtypeStruct((total, width), BF),
+        ],
+        scratch_shapes=[
+            pltpu.VMEM((rows, width), BF),
+            pltpu.VMEM((rows, width), BF),
+            pltpu.VMEM((rows, units), BF),
+            pltpu.VMEM((rows, units), BF),
+            pltpu.VMEM((rows, width), BF),
+            DMA((3,)),
+            *scatter_scratch(mp_count, rows, width),
+        ],
+        compiler_params=pltpu.CompilerParams(
+            collective_id=cid, has_side_effects=True, vmem_limit_bytes=60 << 20
+        ),
+        cost_estimate=pl.CostEstimate(
+            flops=8 * total * width * units,
+            bytes_accessed=25 * total * width,
+            transcendentals=total * units,
+        ),
+    )(x_all, u_all, up, down)
+
+
 def shampoo_kernel(group, tc, w_ref, g_ref, l_ref, r_ref, nw_ref, nl_ref, nr_ref, gf_ref):
     for h in range(group):
         cols = slice(h * tc, (h + 1) * tc)
@@ -230,21 +757,27 @@
     right_down,
 ):
     row_count, features = tokens.shape
-    mp_count = lax.axis_size("mp")
+    dp_count, mp_count = lax.axis_size("dp"), lax.axis_size("mp")
+    chips = mp_count // 2
+    lines = [[2 * chip + core for chip in range(chips)] for core in range(2)]
+    twins = [[2 * chip, 2 * chip + 1] for chip in range(chips)]
     mp_index = lax.axis_index("mp")
     seg_count = seg_len.shape[0]
     own_rows, own_cols = qkv_weight.shape
     head_count = own_cols // (3 * HD)
+    head_width = head_count * HD
+    out_width = out_weight.shape[1]
     inputs = tokens.astype(F32)
     by_kind = (
         qkv_weight.astype(BF)
         .reshape(own_rows, head_count, 3, HD)
-        .transpose(0, 2, 1, 3)
-        .reshape(own_rows, own_cols)
+        .transpose(2, 0, 1, 3)
+        .reshape(3, own_rows, head_width)
     )
     normed_one = layer_norm(inputs, ln_gain[0]).astype(BF)
-    gathered = lax.all_gather(normed_one, "mp", axis=0, tiled=True)
-    qkv_part = lax.all_gather(by_kind, "dp", axis=0, tiled=True)
+    gathered, queries, keys, values, qkv_full = gather_qkv(
+        normed_one, by_kind, dp_count, mp_count, 1
+    )
     positions = mp_index * row_count + jnp.arange(row_count)
     owner_seg = positions // SLOT
     own_length = jnp.sum(
@@ -252,70 +785,66 @@
     )
     valid = positions % SLOT < own_length + NSUM
     upstream = jnp.where(valid[:, None], cotangent, jnp.zeros_like(cotangent))
-    out_part = lax.all_gather(out_weight.astype(BF), "dp", axis=0, tiled=True)
-    out_rows = lax.all_to_all(out_part, "mp", split_axis=0, concat_axis=1, tiled=True)
+    out_line = lax.all_gather(
+        out_weight.astype(BF), "mp", axis=1, tiled=True, axis_index_groups=lines
+    )
+    out_half = lax.all_gather(out_line, "dp", axis=0, tiled=True)
+    out_full = lax.all_gather(out_half, "mp", axis=0, tiled=False, axis_index_groups=twins)
+    out_full = out_full.reshape(2, mp_count, head_width, chips, out_width)
+    upstream_all = lax.all_gather(upstream, "mp", axis=0, tiled=False)
     up_part = lax.all_gather(up_weight.astype(BF), "dp", axis=0, tiled=True)
     down_part = lax.all_gather(down_weight.astype(BF), "dp", axis=1, tiled=True)
-    qkv_rows = jnp.dot(gathered, qkv_part, preferred_element_type=F32).astype(BF)
-    queries, keys, values = jnp.split(qkv_rows, 3, axis=1)
     context, log_sums = attend_fwd(seg_len, queries, keys, values)
-    upstream_all = lax.all_gather(upstream, "mp", axis=0, tiled=True)
-    attended = lax.psum_scatter(
-        jnp.dot(context, out_rows, preferred_element_type=F32).astype(BF),
-        "mp",
-        scatter_dimension=0,
-        tiled=True,
-    )
-    resid = inputs + attended.astype(F32)
-    normed_two = lax.all_gather(
-        layer_norm(resid, ln_gain[1]).astype(BF), "mp", axis=0, tiled=True
-    )
-    pre_act = jnp.dot(normed_two, up_part, preferred_element_type=F32)
-    hidden = gelu_tanh(pre_act).astype(BF)
-    d_hidden = jnp.einsum("rd,fd->rf", upstream_all, down_part, preferred_element_type=F32)
-    d_pre = jax.vjp(gelu_tanh, pre_act)[1](d_hidden)[0].astype(BF)
-    d_normed_two = lax.psum_scatter(
-        jnp.einsum("rf,df->rd", d_pre, up_part, preferred_element_type=F32).astype(BF),
-        "mp",
-        scatter_dimension=0,
-        tiled=True,
-    ).astype(F32)
-    ffn_out = lax.psum_scatter(
-        jnp.dot(hidden, down_part, preferred_element_type=F32).astype(BF),
-        "mp",
-        scatter_dimension=0,
-        tiled=True,
-    )
+    ctx_rows = exchange(context.reshape(mp_count, row_count, head_width), mp_count, 2)
+    attended = jnp.einsum(
+        "prh,cphze->rzce", ctx_rows, out_full, preferred_element_type=F32
+    ).reshape(row_count, features)
+    resid = inputs + attended
+    normed_two = gather_rows(layer_norm(resid, ln_gain[1]).astype(BF), mp_count, 3)
+    d_normed_two, hidden, d_pre, ffn_part = ffn(
+        normed_two, upstream_all, up_part, down_part, mp_count, 4
+    )
+    ffn_out = lax.psum_scatter(ffn_part, "mp", scatter_dimension=0, tiled=True)
     block_out = (resid + ffn_out.astype(F32)).astype(BF)
     norm_back_two = jax.vjp(layer_norm, resid, ln_gain[1])[1]
     d_resid_ln, d_gain_two = norm_back_two(d_normed_two)
     d_resid = upstream.astype(F32) + d_resid_ln
-    d_resid_all = lax.all_gather(d_resid.astype(BF), "mp", axis=0, tiled=True)
+    d_resid_low = d_resid.astype(BF)
+    d_resid_split = d_resid_low.reshape(row_count, chips, 2, out_width)
     d_context = jnp.einsum(
-        "re,de->rd", d_resid_all, out_rows, preferred_element_type=F32
+        "rzce,cphze->prh", d_resid_split, out_full, preferred_element_type=F32
     ).astype(BF)
-    grad_down_part = jnp.einsum("rf,rd->fd", hidden, upstream_all, preferred_element_type=F32)
-    grad_up_part = jnp.einsum("rd,rf->df", normed_two, d_pre, preferred_element_type=F32)
-    d_qkv = jnp.concatenate(
-        attend_bwd(seg_len, queries, keys, values, context, d_context, log_sums), axis=1
-    )
+    d_context = exchange(d_context, mp_count, 5).reshape(mp_count * row_count, head_width)
+    upstream_flat = upstream_all.reshape(mp_count * row_count, features)
+    normed_flat = normed_two.reshape(mp_count * row_count, features)
+    grad_down_part = jnp.einsum("rf,rd->fd", hidden, upstream_flat, preferred_element_type=F32)
+    grad_up_part = jnp.einsum("rd,rf->df", normed_flat, d_pre, preferred_element_type=F32)
+    d_queries, d_keys, d_values = attend_bwd(
+        seg_len, queries, keys, values, context, d_context, log_sums
+    )
+    d_qkv = jnp.concatenate([d_queries, d_keys, d_values], axis=1)
+    gathered = gathered.reshape(mp_count * row_count, features)
     grad_qkv_part = jnp.einsum("gd,gc->dc", gathered, d_qkv, preferred_element_type=F32)
-    d_normed_one = lax.psum_scatter(
-        jnp.einsum("gc,dc->gd", d_qkv, qkv_part, preferred_element_type=F32).astype(BF),
-        "mp",
-        scatter_dimension=0,
-        tiled=True,
-    ).astype(F32)
+    d_normed_one = scatter_d_normed(d_queries, d_keys, d_values, qkv_full, mp_count, 6)
     norm_back_one = jax.vjp(layer_norm, inputs, ln_gain[0])[1]
     d_input_ln, d_gain_one = norm_back_one(d_normed_one)
     input_grad = d_resid + d_input_ln
-    grad_out_rows = jnp.einsum("rd,re->de", context, d_resid_all, preferred_element_type=F32)
-    grad_out_part = lax.all_to_all(
-        grad_out_rows.astype(BF), "mp", split_axis=1, concat_axis=0, tiled=True
-    )
-    grad_qkv, grad_out, grad_up, grad_down = (
+    grad_out_part = jnp.einsum(
+        "prh,rzce->cphze", ctx_rows, d_resid_split, preferred_element_type=F32
+    ).astype(BF)
+    grad_out_half = lax.psum_scatter(
+        grad_out_part.reshape(2, mp_count * head_width, chips * out_width),
+        "mp",
+        scatter_dimension=0,
+        tiled=False,
+        axis_index_groups=twins,
+    )
+    grad_out_line = lax.psum_scatter(grad_out_half, "dp", scatter_dimension=0, tiled=True)
+    grad_out = lax.psum_scatter(
+        grad_out_line, "mp", scatter_dimension=1, tiled=True, axis_index_groups=lines
+    )
+    grad_qkv, grad_up, grad_down = (
         lax.psum_scatter(grad_qkv_part.astype(BF), "dp", scatter_dimension=0, tiled=True),
-        lax.psum_scatter(grad_out_part, "dp", scatter_dimension=0, tiled=True),
         lax.psum_scatter(grad_up_part.astype(BF), "dp", scatter_dimension=0, tiled=True),
         lax.psum_scatter(grad_down_part.astype(BF), "dp", scatter_dimension=1, tiled=True),
     )

time: 1260 us -> 999 us (0.79); the launches traced: 1250 us -> 1000 us
  waiting for transfers between devices: 883 us -> 181 us
  Pallas kernels: 93.8 us -> 564 us
  matrix products: 146 us -> 63.5 us
  local copies, waits for them, and re-layouts: 25.4 us -> 101 us
    pallas_call x0 -> x6, Pallas kernels: none -> 470 us  [the longest x1 117 us: ffn(): pl.pallas_call(functools.partial(ffn_kernel, mp_count), in_specs=[HBM, HB...]
    reduce_scatter x5 -> x4, waiting for transfers between devices: 349 us -> 86.4 us  [the longest x1 83.7 us: body(): ffn_out = lax.psum_scatter(ffn_part, 'mp', scatter_dimension=0, tiled=True)]
    all_gather x6 -> x4, waiting for transfers between devices: 342 us -> 86.9 us  [the longest x1 52.8 us: body(): out_half = lax.all_gather(out_line, 'dp', axis=0, tiled=True)]
    dot_general x11 -> x5, matrix products: 133 us -> 49.8 us  [the longest x1 14.1 us: body(): jnp.einsum('rf,rd->fd', hidden, upstream_flat, preferred_element_type=F32)]
    reshape x0 -> x5, local copies, waits for them, and re-layouts: none -> 53.4 us  [the longest x1 30.8 us: body(): out_full = out_full.reshape(2, mp_count, head_width, chips, out_width)]
    all_gather x1, waiting for transfers between devices: 47.3 us -> 0.02 us  [body(): down_part = lax.all_gather(down_weight.astype(BF), 'dp', axis=1, tiled=True)]
    reduce_scatter x1, waiting for transfers between devices: 40.4 us -> 0.01 us  [body(): lax.psum_scatter(grad_qkv_part.astype(BF), 'dp', scatter_dimension=0, til...]
    all_gather x1, waiting for transfers between devices: 39.2 us -> 0.02 us  [body(): up_part = lax.all_gather(up_weight.astype(BF), 'dp', axis=0, tiled=True)]
  transfers between devices with their start and end apart: 19 -> 14, of which waited for: 17 -> 5; matrix products, arithmetic and copies ran while one was open for 10% -> 13% of each run, Pallas kernels for 5% -> 44%
where the time goes in v2:
time: 999 us; the launch traced here: 1000 us
  Pallas kernels  564 us (56%)
  waiting for transfers between devices  181 us (18%)
  local copies, waits for them, and re-layouts  101 us (10%)
  matrix products  63.5 us (6%)
  blocking collectives  39.2 us (4%)
  other arithmetic  34.4 us (3%)
  between operations  16.7 us (2%)
    pallas_call x1, Pallas kernels, ffn(): pl.pallas_call(functools.partial(ffn_kernel, mp_count), in_specs=[HBM, HB...  117 us
    pallas_call x1, Pallas kernels, gather_qkv(): pl.pallas_call(functools.partial(qkv_kernel, dp_count, mp_count), in_spec...  110 us
    pallas_call x1, Pallas kernels, gather_rows(): pl.pallas_call(functools.partial(gather_kernel, mp_count), in_specs=[HBM]...  102 us
    pallas_call x1, Pallas kernels, scatter_d_normed(): pl.pallas_call(functools.partial(d_normed_kernel, mp_count), in_specs=[VM...  84.8 us
    reduce_scatter x1, waiting for transfers between devices, body(): ffn_out = lax.psum_scatter(ffn_part, 'mp', scatter_dimension=0, tiled=True)  83.7 us
    pallas_call x2, Pallas kernels, exchange(): pl.pallas_call(functools.partial(exchange_kernel, mp_count), in_specs=[HB...  56.3 us
    all_gather x1, waiting for transfers between devices, body(): out_half = lax.all_gather(out_line, 'dp', axis=0, tiled=True)  52.8 us
    psum x1, blocking collectives, body(): lax.psum((gain_parts, spread_sums, jnp.sum(owned_vectors * owned_vectors)...  39.2 us
  transfers between devices with their start and end apart: 14, of which 5 were waited for; matrix products, arithmetic and copies ran while one was open for 13% of the time, Pallas kernels for 44%

profile of v2, /device:TPU:0, one launch (start us, length us, event | category | flops | bytes accessed | tf_op | source)
XLA Modules:
  0.0 1001.5 jit_solution(3811809681252033395)
XLA Ops:
  7.2 1.8 convert_element_type.73
  9.1 34.0 %all-gather.9.cloned.1.call-done = bf16[512,1024]{1,0:T(8,128)(2,1)} async-done(((bf16[512,256]{1,0:T(8,128)(2,1)}), bf16[512,1024]{1,0:T(8,128)(2,1)}) %all-gather.9.cloned.1.call-update) | async-done | bytes 1048592 | tf_op jit(solution)/shard_map/all_gather | solution.py:788
  43.2 52.8 %all-gather.11.cloned.1.call-done = bf16[2048,1024]{1,0:T(8,128)(2,1)} async-done(((bf16[512,1024]{1,0:T(8,128)(2,1)}), bf16[2048,1024]{1,0:T(8,128)(2,1)}) %all-gather.11.cloned.1.call-update) | async-done | bytes 4194320 | tf_op jit(solution)/shard_map/all_gather | solution.py:791
  96.0 1.5 copy-done
  97.6 1.1 convert_element_type.75
  98.8 2.8 convert_element_type.76
  102.3 1.1 broadcast_select_fusion
  103.5 1.9 copy.45
  105.5 1.0 copy.46
  106.4 1.6 copy.47.w_own
  108.0 1.7 convert_reduce_fusion
  109.7 1.8 fusion.18
  113.1 109.9 %shard_map.319 = (bf16[8,256,2048]{2,1,0:T(8,128)(2,1)}, bf16[2048,256]{1,0:T(8,128)(2,1)S(1)}, bf16[2048,256]{1,0:T(8,128)(2,1)S(1)}, bf16[2048,256]{1,0:T(8,128)(2,1)S(1)}, bf16[3,2048,256]{2,1,0:T(8,128)(2,1)S(1)}) custom-call(bf16[256,2048]{1,0:T(8,128)(2,1)S(1)} %fusion.16.own, bf16[3,512,256]{2,1,0:T(8,128)(2,1)S(1)} %copy.47.w_own), custom_call_target="tpu_custom_call" | custom-call | flops 6442450944 | bytes 104857600 | tf_op jit(solution)/shard_map/pallas_call | solution.py:386
  223.1 1.7 copy-done.12
  224.7 28.5 %shard_map.320 = (bf16[2048,256]{1,0:T(8,128)(2,1)S(1)}, f32[1,4,8,2048]{3,2,1,0:T(8,128)S(1)}) custom-call(s32[1]{0:T(128)} %copy.85.len_ref, bf16[2048,256]{1,0:T(8,128)(2,1)S(1)} %get-tuple-element.51.q_ref, bf16[2048,256]{1,0:T(8,128)(2,1)S(1)} %get-tuple-element.52.k_ref, bf16[2048,256]{1,0:T(8,128)(2,1)S(1)} %get-tuple-element.53.v_ref), custom_call_target="tpu_custom_call" | custom-call | flops 2147483648 | bytes 4194304 | tf_op jit(solution)/shard_map/pallas_call | solution.py:87
  254.2 36.4 %shard_map.321 = bf16[8,256,256]{2,1,0:T(8,128)(2,1)} custom-call(bf16[8,256,256]{2,1,0:T(8,128)(2,1)} %bitcast.58), custom_call_target="tpu_custom_call" | custom-call | bytes 20971520 | tf_op jit(solution)/shard_map/pallas_call | solution.py:439
  290.7 30.8 %reshape.238 = bf16[2,8,256,4,256]{4,3,2,1,0:T(4,128)(2,1)} reshape(bf16[4096,1024]{1,0:T(8,128)(2,1)} %all-gather.17.cloned.1.call-done) | data formatting | bytes 16777216 | tf_op jit(solution)/shard_map/reshape | solution.py:793
  321.5 8.1 fusion.20
  329.6 4.2 copy.50
  333.8 4.0 reshape.218
  337.8 1.9 fusion.46
  341.0 1.3 multiply_convert_fusion.own
  342.3 102.0 %shard_map.322.x_all = bf16[8,256,2048]{2,1,0:T(8,128)(2,1)} custom-call(bf16[256,2048]{1,0:T(8,128)(2,1)} %multiply_convert_fusion.own), custom_call_target="tpu_custom_call" | custom-call | bytes 104857600 | tf_op jit(solution)/shard_map/pallas_call | solution.py:308
  444.4 116.7 %shard_map.323 = (f32[256,2048]{1,0:T(8,128)}, bf16[2048,1024]{1,0:T(8,128)(2,1)}, bf16[2048,1024]{1,0:T(8,128)(2,1)}, bf16[2048,2048]{1,0:T(8,128)(2,1)}) custom-call(bf16[8,256,2048]{2,1,0:T(8,128)(2,1)} %shard_map.322.x_all, bf16[8,256,2048]{2,1,0:T(8,128)(2,1)} %bitcast.77, bf16[2048,1024]{1,0:T(8,128)(2,1)} %all-gather.13.cloned.1.call-done.up, ...), custom_call_target="tpu_custom_call" | custom-call | flops 34359738368 | bytes 104857600 | tf_op jit(solution)/shard_map/pallas_call | solution.py:655
  561.6 2.8 multiply_reduce_fusion
  564.5 83.7 %reduce-scatter.9.cloned.1.call-done = bf16[256,2048]{1,0:T(8,128)(2,1)} async-done(((bf16[2048,2048]{1,0:T(8,128)(2,1)}), bf16[256,2048]{1,0:T(8,128)(2,1)}) %reduce-scatter.9.cloned.1.call-update) | async-done | bytes 1048592 | tf_op jit(solution)/shard_map/reduce_scatter | solution.py:807
  648.1 4.1 fusion.45
  652.3 1.3 copy-done.25
  653.6 1.3 fusion.28
  655.0 2.7 reshape.219
  657.7 6.9 convert_bitcast_fusion
  664.5 13.6 %copy.57 = bf16[2,8,256,4,256]{4,3,2,1,0:T(4,128)(2,1)} copy(bf16[2,8,256,4,256]{2,4,1,0,3:T(8,128)(2,1)} %convert_bitcast_fusion) | data formatting | bytes 16777216 | tf_op jit(solution)/shard_map/convert_element_type | solution.py:834
  678.2 14.3 %reshape.226 = bf16[2,2048,1024]{2,1,0:T(8,128)(2,1)} reshape(bf16[2,8,256,4,256]{4,3,2,1,0:T(4,128)(2,1)} %copy.57) | data formatting | bytes 16777216 | tf_op jit(solution)/shard_map/reshape | solution.py:836
  692.6 14.0 %convolution_convert_fusion.1 = bf16[2048,1024]{1,0:T(8,128)(2,1)} fusion(bf16[2048,2048]{1,0:T(8,128)(2,1)} %bitcast.59, bf16[2048,1024]{1,0:T(8,128)(2,1)} %get-tuple-element.65), kind=kOutput, calls=%fused_computation.6 | convolution fusion | flops 8592031744 | bytes 16777216 | tf_op jit(solution)/shard_map/rd,rf->df/dot_general | solution.py:821
  706.8 14.1 %convolution_convert_fusion = bf16[1024,2048]{1,0:T(8,128)(2,1)} fusion(bf16[2048,1024]{1,0:T(8,128)(2,1)} %get-tuple-element.67, bf16[2048,2048]{1,0:T(8,128)(2,1)} %all-gather.19.cloned.1.call-done), kind=kOutput, calls=%fused_computation.5 | convolution fusion | flops 8592031744 | bytes 16777216 | tf_op jit(solution)/shard_map/rf,rd->fd/dot_general | solution.py:820
  722.2 6.7 fusion.25.x
  729.0 19.9 %shard_map.324 = bf16[8,256,256]{2,1,0:T(8,128)(2,1)} custom-call(bf16[8,256,256]{2,1,0:T(8,128)(2,1)} %fusion.25.x), custom_call_target="tpu_custom_call" | custom-call | bytes 20971520 | tf_op jit(solution)/shard_map/pallas_call | solution.py:439
  748.8 2.2 fusion.15
  751.1 1.3 copy-done.16
  752.4 36.2 %shard_map.325 = (bf16[2048,256]{1,0:T(8,128)(2,1)S(1)}, bf16[2048,256]{1,0:T(8,128)(2,1)S(1)}, bf16[2048,256]{1,0:T(8,128)(2,1)S(1)}) custom-call(s32[1]{0:T(128)} %copy.85.len_ref, bf16[2048,256]{1,0:T(8,128)(2,1)S(1)} %copy-done.14, bf16[2048,256]{1,0:T(8,128)(2,1)S(1)} %copy-done.16, bf16[2048,256]{1,0:T(8,128)(2,1)} %copy-done.17, ...), custom_call_target="tpu_custom_call" | custom-call | flops 5368709120 | bytes 8388608 | tf_op jit(solution)/shard_map/pallas_call | solution.py:147
  788.5 1.0 copy-done.18
  789.5 1.0 copy-done.19
  790.5 1.0 copy-done.20
  791.8 11.4 %convolution_convert_fusion.2 = bf16[2048,768]{1,0:T(8,128)(2,1)} fusion(bf16[2048,2048]{1,0:T(8,128)(2,1)} %bitcast.78, bf16[2048,256]{1,0:T(8,128)(2,1)} %copy-done.20, bf16[2048,256]{1,0:T(8,128)(2,1)} %copy-done.19, bf16[2048,256]{1,0:T(8,128)(2,1)} %copy-done.18), kind=kOutput, calls=%fused_computation.7 | convolution fusion | flops 6453460992 | bytes 14680064 | tf_op jit(solution)/shard_map/gd,gc->dc/dot_general | solution.py:827
  803.3 1.6 copy-done.4
  804.9 1.2 copy-done.8
  806.1 8.7 shard_map.329
  814.8 7.0 reduce-scatter.23.cloned.1.call-done.g_ref
  821.8 1.6 copy-done.1
  823.3 1.6 copy-done.5
  824.9 1.2 copy-done.9
  826.2 8.2 shard_map.330
  834.4 84.8 %shard_map.326 = f32[256,2048]{1,0:T(8,128)} custom-call(bf16[2048,256]{1,0:T(8,128)(2,1)} %copy-done.18, bf16[2048,256]{1,0:T(8,128)(2,1)} %copy-done.19, bf16[2048,256]{1,0:T(8,128)(2,1)} %copy-done.20, bf16[3,2048,256]{2,1,0:T(8,128)(2,1)} %copy-done.12), custom_call_target="tpu_custom_call" | custom-call | flops 6442450944 | bytes 104857600 | tf_op jit(solution)/shard_map/pallas_call | solution.py:593
  919.3 2.7 fusion.19
  923.3 4.6 add_add_fusion.2
  927.9 1.4 convert_reduce_fusion.1
  929.4 39.2 %all-reduce = (f32[]{:T(128)}, f32[2048]{0:T(1024)S(1)}, f32[2,2048]{1,0:T(2,128)S(1)}) all-reduce(f32[]{:T(128)} %get-tuple-element.128, f32[2048]{0:T(1024)S(1)} %bitcast.76, f32[2,2048]{1,0:T(2,128)S(1)} %pad_maximum_fusion), channel_id=1, replica_groups=mesh['dp'=4,'mp'=8] {'dp','mp'}, use_global_device_ids=true, to_apply=%region_13.14 | all-reduce | flops 6145 | bytes 49160 | tf_op jit(solution)/shard_map/psum | solution.py:870
  972.8 1.5 copy.53
  974.4 1.0 copy.54
  975.3 1.4 copy.55.g_ref
  976.8 1.4 copy-done.2
  978.2 6.9 shard_map.327
  985.0 2.7 reduce-scatter.19.cloned.1.call-done.g_ref
  988.7 6.0 shard_map.328
  (138 shorter events, 12.1 us)
Async XLA Ops:
  7.2 35.9 %all-gather.9.cloned.1.call-start = ((), (), s32[]{:S(2)}) async-start(), calls=%async_computation.8 | async-start | bytes 1310720 | tf_op jit(solution)/shard_map/all_gather | solution.py:788
  9.0 86.9 %all-gather.11.cloned.1.call-start = ((), (), s32[]{:S(2)}) async-start(), calls=%async_computation.9 | async-start | bytes 5242880 | tf_op jit(solution)/shard_map/all_gather | solution.py:791
  43.1 247.6 %all-gather.17.cloned.1.call-start = ((), (), s32[]{:S(2)}) async-start(), calls=%async_computation.20 | async-start | bytes 12582912 | tf_op jit(solution)/shard_map/all_gather | solution.py:792
  96.0 1.6 copy-start
  96.0 348.3 %all-gather.13.cloned.1.call-start = ((), (), s32[]{:S(2)}) async-start(), calls=%async_computation.10 | async-start | bytes 5242880 | tf_op jit(solution)/shard_map/all_gather | solution.py:795
  98.7 3.6 copy-start.27
  98.7 345.6 %all-gather.15.cloned.1.call-start = ((), (), s32[]{:S(2)}) async-start(), calls=%async_computation.11 | async-start | bytes 5242880 | tf_op jit(solution)/shard_map/all_gather | solution.py:796
  101.6 342.8 %all-gather.19.cloned.1.call-start = ((), (), s32[]{:S(2)}) async-start(), calls=%async_computation.21 | async-start | bytes 9437184 | tf_op jit(solution)/shard_map/all_gather | solution.py:794
  103.5 544.7 %reduce-scatter.9.cloned.1.call-start = ((), (), s32[]{:S(2)}) async-start(), calls=%async_computation.12 | async-start | bytes 9437184 | tf_op jit(solution)/shard_map/reduce_scatter | solution.py:807
  106.4 5.6 copy-start.35
  108.0 4.7 copy-start.22
  109.7 113.3 %copy-start.38 = (f32[256]{0:T(256)}, f32[256]{0:T(256)S(1)}, u32[]{:S(2)}) copy-start(f32[256]{0:T(256)S(1)} %broadcast_multiply_fusion.2) | copy-start | bytes 3076
  111.5 0.6 copy-start.42
  112.1 111.0 %copy-start.40 = (f32[256]{0:T(256)}, f32[256]{0:T(256)S(1)}, u32[]{:S(2)}) copy-start(f32[256]{0:T(256)S(1)} %fusion.41) | copy-start | bytes 3076
  112.1 0.6 copy-start.33
  223.1 1.7 copy-start.12
  224.7 28.5 %copy-start.13 = (bf16[2048,256]{1,0:T(8,128)(2,1)}, bf16[2048,256]{1,0:T(8,128)(2,1)S(1)}, u32[]{:S(2)}) copy-start(bf16[2048,256]{1,0:T(8,128)(2,1)S(1)} %get-tuple-element.51.q_ref) | copy-start | bytes 3145732
  224.7 28.5 %copy-start.15 = (bf16[2048,256]{1,0:T(8,128)(2,1)}, bf16[2048,256]{1,0:T(8,128)(2,1)S(1)}, u32[]{:S(2)}) copy-start(bf16[2048,256]{1,0:T(8,128)(2,1)S(1)} %get-tuple-element.52.k_ref) | copy-start | bytes 3145732
  224.7 28.5 %copy-start.17 = (bf16[2048,256]{1,0:T(8,128)(2,1)}, bf16[2048,256]{1,0:T(8,128)(2,1)S(1)}, u32[]{:S(2)}) copy-start(bf16[2048,256]{1,0:T(8,128)(2,1)S(1)} %get-tuple-element.53.v_ref) | copy-start | bytes 3145732
  253.3 1.0 copy-start.7
  290.6 30.9 %copy-start.30 = (bf16[8,256,256]{2,1,0:T(8,128)(2,1)S(1)}, bf16[8,256,256]{2,1,0:T(8,128)(2,1)}, u32[]{:S(2)}) copy-start(bf16[8,256,256]{2,1,0:T(8,128)(2,1)} %shard_map.321) | copy-start | bytes 3145732
  333.8 4.0 copy-start.23
  339.7 1.3 copy-start.21
  561.1 159.9 %reduce-scatter.15.cloned.1.call-start = ((), (), s32[]{:S(2)}) async-start(), calls=%async_computation.15 | async-start | bytes 12582912 | tf_op jit(solution)/shard_map/reduce_scatter | solution.py:835
  564.4 89.2 %copy-start.28 = (bf16[256,2048]{1,0:T(8,128)(2,1)S(1)}, bf16[256,2048]{1,0:T(8,128)(2,1)}, u32[]{:S(2)}) copy-start(bf16[256,2048]{1,0:T(8,128)(2,1)} %param.18) | copy-start | bytes 3145732
  652.3 1.3 copy-start.25
  655.0 2.7 copy-start.31
  692.5 110.8 %reduce-scatter.21.cloned.1.call-start = ((), (), s32[]{:S(2)}) async-start(), calls=%async_computation.18 | async-start | bytes 5242880 | tf_op jit(solution)/shard_map/reduce_scatter | solution.py:848
  706.6 115.2 %reduce-scatter.23.cloned.1.call-start = ((), (), s32[]{:S(2)}) async-start(), calls=%async_computation.19 | async-start | bytes 5242880 | tf_op jit(solution)/shard_map/reduce_scatter | solution.py:849
  720.9 202.1 %reduce-scatter.17.cloned.1.call-start = ((), (), s32[]{:S(2)}) async-start(), calls=%async_computation.16 | async-start | bytes 5242880 | tf_op jit(solution)/shard_map/reduce_scatter | solution.py:842
  721.0 1.2 copy-start.32
  721.7 206.2 %reduce-scatter.11.cloned.1.call-start = ((), (), s32[]{:S(2)}) async-start(), calls=%async_computation.13 | async-start | bytes 258048 | tf_op jit(solution)/shard_map/reduce_scatter | solution.py:861
  729.0 22.1 %copy-start.14 = (bf16[2048,256]{1,0:T(8,128)(2,1)S(1)}, bf16[2048,256]{1,0:T(8,128)(2,1)}, u32[]{:S(2)}) copy-start(bf16[2048,256]{1,0:T(8,128)(2,1)} %copy-done.13) | copy-start | bytes 3145732
  751.1 1.3 copy-start.16
  788.5 1.0 copy-start.18
  789.5 1.0 copy-start.19
  790.5 1.0 copy-start.20
  791.5 181.3 %reduce-scatter.13.cloned.1.call-start = ((), (), s32[]{:S(2)}) async-start(), calls=%async_computation.14 | async-start | bytes 3932160 | tf_op jit(solution)/shard_map/reduce_scatter | solution.py:847
  803.2 184.5 %reduce-scatter.19.cloned.1.call-start = ((), (), s32[]{:S(2)}) async-start(), calls=%async_computation.17 | async-start | bytes 1310720 | tf_op jit(solution)/shard_map/reduce_scatter | solution.py:843
  803.3 1.6 copy-start.4
  804.9 1.2 copy-start.8
  821.7 1.6 copy-start.1
  823.3 1.6 copy-start.5
  824.9 1.2 copy-start.9
  834.4 84.9 %copy-start.24 = (bf16[256,2048]{1,0:T(8,128)(2,1)S(1)}, bf16[256,2048]{1,0:T(8,128)(2,1)}, u32[]{:S(2)}) copy-start(bf16[256,2048]{1,0:T(8,128)(2,1)} %param.16) | copy-start | bytes 3145732
  834.4 84.9 %copy-start.34 = (f32[1,2048]{1,0:T(1,128)S(1)}, f32[1,2048]{1,0:T(1,128)}, u32[]{:S(2)}) copy-start(f32[1,2048]{1,0:T(1,128)} %copy-done.33) | copy-start | bytes 24580
  834.4 84.9 %copy-start.39 = (f32[256]{0:T(256)S(1)}, f32[256]{0:T(256)}, u32[]{:S(2)}) copy-start(f32[256]{0:T(256)} %copy-done.38) | copy-start | bytes 3076
  919.3 2.7 copy-start.43
  919.3 2.7 copy-start.26
  919.3 2.7 copy-start.41
  922.0 1.2 copy-start.29
  923.3 48.9 %copy-start.36 = (f32[2,2048]{1,0:T(2,128)S(1)}, f32[2,2048]{1,0:T(2,128)}, u32[]{:S(2)}) copy-start(f32[2,2048]{1,0:T(2,128)} %param.19) | copy-start | bytes 49156
  968.5 8.2 copy-start.37
  972.8 3.9 copy-start.6
  976.8 1.4 copy-start.2
  978.2 9.6 copy-start.3
  978.2 9.6 copy-start.10
  987.7 1.0 copy-start.11
Sparse Core Ops, SparseCore 0:
  10.2 32.8 all-gather.8
  44.9 51.0 all-gather.10
  97.5 21.3 all-gather.16
  121.2 65.2 all-gather.12
  188.8 52.5 all-gather.14
  243.4 104.2 all-gather.18
  561.3 86.8 reduce-scatter.8
  692.6 15.1 reduce-scatter.14
  711.6 53.9 reduce-scatter.20
  769.0 52.6 reduce-scatter.22
  825.0 52.6 reduce-scatter.16
  880.4 31.9 reduce-scatter.10
  915.6 42.6 reduce-scatter.12
  960.6 27.0 reduce-scatter.18

commit v3 on v2

v3 whole, which is shorter than its diff:
```python
import functools
import math

import jax
import jax.numpy as jnp
from jax import lax
from jax.experimental import pallas as pl
from jax.experimental.pallas import tpu as pltpu
from jax.sharding import PartitionSpec as P

HD = 64
SLOT = 2048
NSUM = 50
BLOCK = 512
FBLK = 256


NORM_EPSILON = 1e-05
SHAMPOO_RATE = 0.5
GAIN_RATE = 0.1
DECAY = 0.5
NEG = -1e30
BF = jnp.bfloat16
F32 = jnp.float32

NT = (((1,),(1,)),((),()))
NN=(((1,),(0,)),((),()))
TN=(((0,),(0,)),((),()))
def dg(a,b,d): return lax.dot_general(a,b,d,preferred_element_type=F32)

def head_masks(width, hp):
    lane = lax.broadcasted_iota(jnp.int32,(1,width),1)
    return [(lane>=h*HD)&(lane<(h+1)*HD) for h in range(hp)]

def fwd_block(hp, bq, len_ref, q_ref, k_ref, v_ref, lse_ref, s_ref):
    i = pl.program_id(2)
    limit = len_ref[pl.program_id(0)] + NSUM
    width = q_ref.shape[1]
    masks = head_masks(width, hp)
    q = q_ref[...] * jnp.asarray(0.125, BF)
    qs = [jnp.where(m, q, jnp.zeros_like(q)) for m in masks]
    col = lax.broadcasted_iota(jnp.int32,(bq,bq),1)
    row = lax.broadcasted_iota(jnp.int32,(bq,bq),0)
    def score(j, tops, diag):
        k = k_ref[pl.ds(pl.multiple_of(j*bq,bq),bq),:]
        ok = col < limit - j*bq
        if diag: ok = ok & (col <= row)
        out=[]
        for h in range(hp):
            s = jnp.where(ok, dg(qs[h],k,NT), NEG)
            s_ref[h,j] = s
            t = tops[h]
            for c in range(0,bq,128): t = jnp.maximum(t, s[:,c:c+128])
            out.append(t)
        return out
    tops=[jnp.full((bq,128),NEG,F32) for _ in range(hp)]
    tops=lax.fori_loop(0,i,lambda j,t: score(j,t,False), tops)
    tops=score(i,tops,True)
    tops=[jnp.max(t,axis=1,keepdims=True) for t in tops]
    def acc(j, carry):
        v = v_ref[pl.ds(pl.multiple_of(j*bq,bq),bq),:]
        out=[]
        for h in range(hp):
            o,l = carry[h]
            e = jnp.exp(s_ref[h,j]-tops[h])
            for c in range(0,bq,128): l = l + e[:,c:c+128]
            o = o + dg(e.astype(BF),v,NN)
            out.append((o,l))
        return out
    carry=[(jnp.zeros((bq,width),F32),jnp.zeros((bq,128),F32)) for _ in range(hp)]
    carry=lax.fori_loop(0,i+1,acc,carry)
    res=None
    for h in range(hp):
        o,l=carry[h]
        l=jnp.sum(l,axis=1,keepdims=True)
        o=o/l
        res = o if res is None else jnp.where(masks[h],o,res)
        lse = jnp.broadcast_to(tops[h]+jnp.log(l),(bq,128)).T
        lse_ref[0,h]=lse[:8]
    return res.astype(BF)

def bwd_block(hp, bq, len_ref, q_ref, k_ref, v_ref, o_ref, do_ref, lse_ref, dq_ref, dk_ref, dv_ref, dka, dva):
    i = pl.program_id(2)
    nb = pl.num_programs(2)
    limit = len_ref[pl.program_id(0)] + NSUM
    width = q_ref.shape[1]
    masks = head_masks(width, hp)
    @pl.when(i==0)
    def _():
        dka[...]=jnp.zeros_like(dka); dva[...]=jnp.zeros_like(dva)
    q = q_ref[...] * jnp.asarray(0.125, BF)
    do = do_ref[...]
    prod = (do.astype(F32)*o_ref[...].astype(F32)).T
    qs = [jnp.where(m, q, jnp.zeros_like(q)) for m in masks]
    dos = [jnp.where(m, do, jnp.zeros_like(do)) for m in masks]
    dd = [jnp.sum(prod[h*HD:(h+1)*HD],axis=0,keepdims=True) for h in range(hp)]
    ls = [lse_ref[0,h,0:1,:] for h in range(hp)]
    rowk = lax.broadcasted_iota(jnp.int32,(bq,bq),0)
    colq = lax.broadcasted_iota(jnp.int32,(bq,bq),1)
    def step(j, dq, diag):
        at = pl.ds(pl.multiple_of(j*bq,bq),bq)
        k = k_ref[at,:]; v=v_ref[at,:]
        ok = rowk < limit - j*bq
        if diag: ok = ok & (rowk <= colq)
        dk=dka[at,:]; dv=dva[at,:]
        for h in range(hp):
            s = dg(k,qs[h],NT)
            p = jnp.where(ok, jnp.exp(s-ls[h]), 0.0)
            dp = dg(v,dos[h],NT)
            ds = (p*(dp-dd[h])).astype(BF)
            dv = dv + dg(p.astype(BF),dos[h],NN)
            dk = dk + dg(ds,qs[h],NN)
            dq = dq + dg(ds, jnp.where(masks[h],k,jnp.zeros_like(k)), TN)
        dka[at,:]=dk; dva[at,:]=dv
        return dq
    dq = lax.fori_loop(0,i,lambda j,c: step(j,c,False), jnp.zeros((bq,width),F32))
    dq = step(i,dq,True)
    dq_ref[...] = (dq*0.125).astype(BF)
    @pl.when(i==nb-1)
    def _():
        dk_ref[...]=dka[...].astype(BF); dv_ref[...]=dva[...].astype(BF)

MESH = pl.DeviceIdType.MESH
HBM = pl.BlockSpec(memory_space=pl.ANY)
VM = pl.BlockSpec(memory_space=pltpu.VMEM)
DMA = pltpu.SemaphoreType.DMA


def on_mp(index):
    return (lax.axis_index("dp"), index)


def on_dp(index):
    return (index, lax.axis_index("mp"))


def remote(src, dst, send, recv, device):
    return pltpu.make_async_remote_copy(
        src_ref=src,
        dst_ref=dst,
        send_sem=send,
        recv_sem=recv,
        device_id=device,
        device_id_type=MESH,
    )


def local(src, dst, sem):
    copy = pltpu.make_async_copy(src, dst, sem)
    copy.start()
    return copy


class Line:
    def __init__(self, mp_count):
        self.n = mp_count // 2
        self.me = lax.axis_index("mp")
        self.chip = self.me // 2
        self.core = self.me % 2
        self.twin = on_mp(2 * self.chip + 1 - self.core)
        self.right = on_mp(self.me + 2)
        self.left = on_mp(self.me - 2)
        self.has_right = self.chip < self.n - 1
        self.has_left = self.chip > 0

    def greet(self, others=()):
        barrier = pltpu.get_barrier_semaphore()

        def hello(device):
            pl.semaphore_signal(barrier, inc=1, device_id=device, device_id_type=MESH)

        hello(self.twin)
        for device in others:
            hello(device)
        pl.when(self.has_right)(lambda: hello(self.right))
        pl.when(self.has_left)(lambda: hello(self.left))
        met = 1 + len(others) + self.has_right.astype(jnp.int32) + self.has_left.astype(jnp.int32)
        pl.semaphore_wait(barrier, met)


class Gather:
    def __init__(self, line, own, full, recv, sends, sem):
        self.line, self.own, self.full, self.recv, self.sends, self.sem = (
            line,
            own,
            full,
            recv,
            sends,
            sem,
        )

    def copy(self, src, block, way, k):
        line = self.line
        device = (line.right, line.left, line.twin)[way]
        return remote(
            src, self.full(block), self.sends.at[way, k], self.recv.at[block], device
        )

    def start(self):
        line = self.line
        mine = self.copy
        pl.when(line.has_right)(lambda: mine(self.own, line.me, 0, 0).start())
        pl.when(line.has_left)(lambda: mine(self.own, line.me, 1, 0).start())
        mine(self.own, line.me, 2, line.chip).start()
        self.mine = local(self.own, self.full(line.me), self.sem)

    def arrived(self, block):
        self.copy(self.own, block, 2, 0).wait_recv()

    def forward(self, away, only=None):
        line = self.line

        def take(chip, way, onward):
            block = 2 * chip + line.core
            self.arrived(block)
            got = self.full(block)
            pl.when(onward)(lambda: self.copy(got, block, way, away).start())
            self.copy(got, block, 2, chip).start()

        from_left, from_right = line.chip >= away, line.chip + away < line.n
        if only is not None:
            from_left &= line.has_right == only
            from_right &= line.has_left == only
        pl.when(from_left)(lambda: take(line.chip - away, 0, line.has_right))
        pl.when(from_right)(lambda: take(line.chip + away, 1, line.has_left))

    def each(self, away, use, core):
        line = self.line
        pl.when(line.chip >= away)(lambda: use(2 * (line.chip - away) + core))
        pl.when(line.chip + away < line.n)(lambda: use(2 * (line.chip + away) + core))

    def finish(self):
        line = self.line

        def sent(away, _):
            wait = lambda way, k: self.copy(self.own, line.me, way, k).wait_send()
            pl.when(line.has_right & (line.chip >= away))(lambda: wait(0, away))
            pl.when(line.has_left & (line.chip + away < line.n))(lambda: wait(1, away))
            wait(2, away)
            return 0

        lax.fori_loop(0, line.n, sent, 0)


def gather_sems(mp_count):
    return [DMA((mp_count,)), DMA((3, mp_count // 2)), DMA(())]


def qkv_kernel(
    dp_count, mp_count, own, w_own, full, q_out, k_out, v_out, w_full,
    w, x, y, recv, sends, sem, w_recv, w_send, w_sem, io_sem
):
    line = Line(mp_count)
    dp = lax.axis_index("dp")
    peers = [lax.rem(dp + k, dp_count) for k in range(1, dp_count)]
    line.greet([on_dp(peer) for peer in peers])
    rows = own.shape[0]
    part = w_own.shape[1]

    def place(ref, index):
        return ref.at[:, pl.ds(pl.multiple_of(index * part, part), part), :]

    def weight_copy(k, index):
        return remote(
            w_own, place(w_full, index), w_send.at[k], w_recv.at[index], on_dp(peers[k])
        )

    for k in range(dp_count - 1):
        weight_copy(k, dp).start()
    mine = local(w_own, place(w_full, dp), w_sem)
    gather = Gather(line, own, lambda block: full.at[block], recv, sends, sem)
    gather.start()
    gather.forward(1)
    gather.mine.wait()
    mine.wait()
    for k in range(dp_count - 1):
        weight_copy(k, peers[k]).wait_recv()
    local(w_full, w, w_sem).wait()

    def use(block):
        local(full.at[block], x, io_sem.at[0]).wait()
        at = pl.ds(pl.multiple_of(block * rows, rows), rows)
        copies = []
        for j, ref in enumerate((q_out, k_out, v_out)):
            y[j] = jnp.dot(x[...], w[j], preferred_element_type=F32).astype(BF)
            copies.append(local(y.at[j], ref.at[at, :], io_sem.at[j]))
        for copy in copies:
            copy.wait()

    def from_twin(block):
        gather.arrived(block)
        use(block)

    use(line.me)
    from_twin(2 * line.chip + 1 - line.core)

    def both(away):
        gather.each(away, use, line.core)
        gather.each(away, from_twin, 1 - line.core)

    def step(away, _):
        gather.forward(away)
        pl.when(away == 2)(lambda: both(1))
        both(away)
        return 0

    lax.fori_loop(2, line.n, step, 0)
    gather.finish()
    for k in range(dp_count - 1):
        weight_copy(k, dp).wait_send()


def gather_qkv(own, w_own, dp_count, mp_count, cid):
    rows, width = own.shape
    _, part, hw = w_own.shape
    depth = part * dp_count
    head = jax.ShapeDtypeStruct((mp_count * rows, hw), BF)
    return pl.pallas_call(
        functools.partial(qkv_kernel, dp_count, mp_count),
        in_specs=[HBM, HBM],
        out_specs=[HBM] * 5,
        out_shape=[
            jax.ShapeDtypeStruct((mp_count, rows, width), BF),
            head,
            head,
            head,
            jax.ShapeDtypeStruct((3, depth, hw), BF),
        ],
        scratch_shapes=[
            pltpu.VMEM((3, depth, hw), BF),
            pltpu.VMEM((rows, width), BF),
            pltpu.VMEM((3, rows, hw), BF),
            *gather_sems(mp_count),
            DMA((dp_count,)),
            DMA((dp_count,)),
            DMA(()),
            DMA((3,)),
        ],
        compiler_params=pltpu.CompilerParams(
            collective_id=cid, has_side_effects=True, vmem_limit_bytes=40 << 20
        ),
        cost_estimate=pl.CostEstimate(
            flops=6 * mp_count * rows * depth * hw,
            bytes_accessed=280 << 20,
            transcendentals=0,
        ),
    )(own, w_own)


def greet_all(devices):
    barrier = pltpu.get_barrier_semaphore()
    for device in devices:
        pl.semaphore_signal(barrier, inc=1, device_id=device, device_id_type=MESH)
    pl.semaphore_wait(barrier, len(devices))


def others(axis, count):
    return [lax.rem(lax.axis_index(axis) + k, count) for k in range(1, count)]


def flat_step():
    index = pl.program_id(0)
    for axis in (1, 2):
        index = index * pl.num_programs(axis) + pl.program_id(axis)
    return index


def attend_fwd_kernel(
    hp, bq, steps, dp_count, mp_count,
    len_ref, q_ref, k_ref, v_ref, up_own, out_own,
    ctx_out, lse_ref, rows_out, up_full, out_full,
    s_ref, ctx, a_send, a_recv, a_local, u_recv, u_sends, u_sem, o_recv, o_sends, o_sem,
    d_send, d_recv, t_send, t_recv
):
    line = Line(mp_count)
    dp = lax.axis_index("dp")
    me, core = line.me, line.core
    mp_peers, dp_peers = others("mp", mp_count), others("dp", dp_count)
    flat = flat_step()
    rows = up_own.shape[0]
    part = out_own.shape[0]
    pairs = a_send.shape[0]
    width = q_ref.shape[1]

    def owned(index):
        return pl.ds(pl.multiple_of(index * part, part), part)

    ups = Gather(line, up_own, lambda block: up_full.at[block], u_recv, u_sends, u_sem)
    outs = Gather(
        line, out_own, lambda block: out_full.at[block % 2, block // 2, owned(dp), :],
        o_recv, o_sends, o_sem,
    )

    def across(k, index):
        at = (core, slice(None), owned(index), slice(None))
        return remote(
            out_full.at[core, :, owned(dp), :], out_full.at[at], d_send.at[k], d_recv.at[index],
            on_dp(dp_peers[k]),
        )

    def to_twin(k, side):
        at = out_full.at[side, :, owned(dp_peers[k]), :]
        return remote(at, at, t_send.at[k], t_recv.at[k], line.twin)

    def lanes(pair):
        if pairs == 1:
            return slice(None)
        return pl.ds(pl.multiple_of(pair * width, width), width)

    def ctx_copy(pair, block, source, device):
        at = pl.ds(pl.multiple_of(block * rows, rows), rows)
        return remote(
            ctx.at[at, lanes(pair)], rows_out.at[source, :, lanes(pair)],
            a_send.at[pair, block], a_recv.at[pair, source], on_mp(device),
        )

    def ctx_local(pair):
        at = pl.ds(pl.multiple_of(me * rows, rows), rows)
        return pltpu.make_async_copy(
            ctx.at[at, lanes(pair)], rows_out.at[me, :, lanes(pair)], a_local.at[pair]
        )

    @pl.when(flat == 0)
    def _():
        greet_all([on_mp(peer) for peer in mp_peers] + [on_dp(peer) for peer in dp_peers])
        outs.start()

    @pl.when(flat == 1)
    def _():
        ups.start()

    pair = pl.program_id(1)
    start = pl.program_id(0) * SLOT + pl.program_id(2) * bq
    at = pl.ds(pl.multiple_of(start, bq), bq)
    ctx[at, lanes(pair)] = fwd_block(hp, bq, len_ref, q_ref, k_ref, v_ref, lse_ref, s_ref)
    for k in range(bq // rows):
        block = start // rows + k
        pl.when(block == me)(lambda: ctx_local(pair).start())
        pl.when(block != me)(lambda block=block: ctx_copy(pair, block, me, block).start())

    for away in range(1, line.n):
        @pl.when(flat == min(1 + away, steps - 1))
        def _(away=away):
            outs.forward(away)

    @pl.when(flat == min(line.n + 1, steps - 1))
    def _():
        pltpu.make_async_copy(out_own, outs.full(me), o_sem).wait()
        for k in range(dp_count - 1):
            across(k, dp).start()

    @pl.when(flat == steps - 1)
    def _():
        keep = pltpu.make_async_copy(ctx, ctx_out, o_sem)
        keep.start()
        ups_step = lambda away, _: (ups.forward(away), 0)[1]
        lax.fori_loop(1, line.n, ups_step, 0)
        for k in range(dp_count - 1):
            across(k, dp_peers[k]).wait_recv()
            to_twin(k, core).start()

        def twins(chip, _):
            block = 2 * chip + 1 - core
            outs.arrived(block)
            ups.arrived(block)
            return 0

        lax.fori_loop(0, line.n, twins, 0)
        for k in range(dp_count - 1):
            to_twin(k, 1 - core).wait_recv()
            to_twin(k, core).wait_send()
            across(k, dp).wait_send()
        for p in range(pairs):
            ctx_local(p).wait()
            for peer in mp_peers:
                ctx_copy(p, peer, peer, peer).wait_recv()
                ctx_copy(p, peer, me, peer).wait_send()
        outs.finish()
        ups.finish()
        pltpu.make_async_copy(up_own, up_full.at[me], u_sem).wait()
        keep.wait()


def attend_fwd(seg_len, q, k, v, up_own, out_own, dp_count, mp_count, cid, bq=512):
    total, hw = q.shape
    rows, features = up_own.shape
    part, cols = out_own.shape
    heads = hw // HD
    hp = 2 if heads % 2 == 0 else 1
    assert hp == 2 or heads == 1
    width, nb, segs, pairs = hp * HD, SLOT // bq, total // SLOT, heads // hp
    chips = mp_count // 2
    return pl.pallas_call(
        functools.partial(
            attend_fwd_kernel, hp, bq, segs * pairs * nb, dp_count, mp_count
        ),
        grid=(segs, pairs, nb),
        in_specs=[
            pl.BlockSpec(memory_space=pltpu.SMEM),
            pl.BlockSpec((bq, width), lambda s, p, i: (s * nb + i, p)),
            pl.BlockSpec((SLOT, width), lambda s, p, i: (s, p)),
            pl.BlockSpec((SLOT, width), lambda s, p, i: (s, p)),
            HBM,
            HBM,
        ],
        out_specs=[
            HBM,
            pl.BlockSpec((1, hp, 8, bq), lambda s, p, i: (s, p, 0, i)),
            HBM,
            HBM,
            HBM,
        ],
        out_shape=[
            jax.ShapeDtypeStruct((total, hw), BF),
            jax.ShapeDtypeStruct((segs, heads, 8, SLOT), F32),
            jax.ShapeDtypeStruct((mp_count, rows, hw), BF),
            jax.ShapeDtypeStruct((mp_count, rows, features), BF),
            jax.ShapeDtypeStruct((2, chips, part * dp_count, cols), BF),
        ],
        scratch_shapes=[
            pltpu.VMEM((hp, nb, bq, bq), F32),
            pltpu.VMEM((total, hw), BF),
            DMA((pairs, mp_count)),
            DMA((pairs, mp_count)),
            DMA((pairs,)),
            *gather_sems(mp_count),
            *gather_sems(mp_count),
            DMA((dp_count,)),
            DMA((dp_count,)),
            DMA((dp_count,)),
            DMA((dp_count,)),
        ],
        compiler_params=pltpu.CompilerParams(
            collective_id=cid, has_side_effects=True, vmem_limit_bytes=48 << 20
        ),
        cost_estimate=pl.CostEstimate(
            flops=segs * heads * SLOT * SLOT * 128,
            bytes_accessed=380 << 20,
            transcendentals=segs * heads * SLOT * SLOT // 2,
        ),
    )(seg_len, q, k, v, up_own, out_own)


ROWS_AT_ONCE = 32


def row_chunks(rows, body, init=0):
    def step(i, carry):
        return body(pl.ds(pl.multiple_of(i * ROWS_AT_ONCE, ROWS_AT_ONCE), ROWS_AT_ONCE), carry)

    return lax.fori_loop(0, rows // ROWS_AT_ONCE, step, init)


def normed(value):
    centred = value - jnp.mean(value, axis=-1, keepdims=True)
    scale = lax.rsqrt(jnp.mean(centred * centred, axis=-1, keepdims=True) + NORM_EPSILON)
    return centred * scale, scale


def norm_back(value, gain, grad):
    unit, scale = normed(value)
    u = grad * gain
    mean_u = jnp.mean(u, axis=-1, keepdims=True)
    mean_un = jnp.mean(u * unit, axis=-1, keepdims=True)
    return scale * (u - mean_u - unit * mean_un), jnp.sum(grad * unit, axis=0, keepdims=True)


def out_kernel(mp_count, ctx, out_part, tokens, gain, resid, own, flat, acc):
    m = pl.program_id(0)
    rows = tokens.shape[0]
    hw = ctx.shape[2]

    @pl.when(m == 0)
    def _():
        for p in range(mp_count):
            flat[:, p * hw : (p + 1) * hw] = ctx[p]

    acc[m] = dg(flat[...], out_part[0, 0], NN)

    @pl.when(m == mp_count - 1)
    def _():
        def norm(at, carry):
            value = jnp.concatenate([acc[k, at, :] for k in range(mp_count)], axis=1)
            value = value + tokens[at, :].astype(F32)
            resid[at, :] = value
            unit, _ = normed(value)
            own[at, :] = (unit * gain[1:2, :]).astype(BF)
            return carry

        row_chunks(rows, norm)


def out_and_norm(ctx, out_full, tokens, gain, mp_count):
    rows, features = tokens.shape
    _, _, depth, cols = out_full.shape
    whole = lambda *shape: pl.BlockSpec(shape, lambda m: (0,) * len(shape))
    return pl.pallas_call(
        functools.partial(out_kernel, mp_count),
        grid=(mp_count,),
        in_specs=[
            whole(*ctx.shape),
            pl.BlockSpec((1, 1, depth, cols), lambda m: (m % 2, m // 2, 0, 0)),
            whole(rows, features),
            whole(*gain.shape),
        ],
        out_specs=[whole(rows, features), whole(rows, features)],
        out_shape=[
            jax.ShapeDtypeStruct((rows, features), F32),
            jax.ShapeDtypeStruct((rows, features), BF),
        ],
        scratch_shapes=[
            pltpu.VMEM((rows, depth), BF),
            pltpu.VMEM((mp_count, rows, cols), F32),
        ],
        compiler_params=pltpu.CompilerParams(vmem_limit_bytes=40 << 20),
        cost_estimate=pl.CostEstimate(
            flops=2 * rows * features * depth, bytes_accessed=36 << 20, transcendentals=0
        ),
    )(ctx, out_full, tokens, gain)


def resid_back_kernel(
    dp_count, mp_count, dn, resid, up_own, gain, out_hbm, ctx,
    d_resid, d_gain, d_ctx, g_out,
    out_full, low, mine, grad, land, send, recv, g_send, g_recv, sem
):
    line = Line(mp_count)
    me, core = line.me, line.core
    rows, features = dn.shape
    hw, cols = ctx.shape[2], out_full.shape[3]
    per = grad.shape[3] // hw
    peers = others("mp", mp_count)
    fetch = local(out_hbm, out_full, sem.at[0])

    def back(at, total):
        d_value, d_g = norm_back(resid[at, :], gain[1:2, :], dn[at, :])
        d_value = up_own[at, :].astype(F32) + d_value
        d_resid[at, :] = d_value
        low[at, :] = d_value.astype(BF)
        return total + d_g

    d_gain[...] = row_chunks(rows, back, jnp.zeros((1, features), F32))
    greet_all([on_mp(peer) for peer in peers])
    fetch.wait()

    def copy(device, source):
        return remote(
            mine.at[device], d_ctx.at[source], send.at[device], recv.at[source], on_mp(device)
        )

    def term(p):
        at = pl.ds(pl.multiple_of(p * hw, hw), hw)
        total = jnp.zeros((rows, hw), F32)
        for m in range(mp_count):
            here = slice(m * cols, (m + 1) * cols)
            total += dg(low[:, here], out_full[m % 2, m // 2, at, :], NT)
        mine[p] = total.astype(BF)

    def produce(k, _):
        p = lax.rem(me + k, mp_count)
        term(p)
        copy(p, me).start()
        return 0

    lax.fori_loop(1, mp_count, produce, 0)
    term(me)
    keep = local(mine.at[me], d_ctx.at[me], sem.at[1])

    def piece(p):
        at = pl.ds(pl.multiple_of(lax.rem(p, per) * hw, hw), hw)
        return lax.div(p, per), at

    def to_twin(p, side):
        owner, at = piece(p)
        return remote(
            grad.at[side, owner, :, at, :], land.at[owner, :, at, :],
            g_send.at[p], g_recv.at[p], line.twin,
        )

    def weigh(p, _):
        owner, at = piece(p)
        value = dg(ctx[p], low[...], TN)
        for m in range(mp_count):
            grad[m % 2, owner, m // 2, at, :] = value[:, m * cols : (m + 1) * cols].astype(BF)
        to_twin(p, 1 - core).start()
        return 0

    lax.fori_loop(0, mp_count, weigh, 0)

    def join(p, _):
        owner, at = piece(p)
        to_twin(p, 1 - core).wait_recv()
        total = grad[core, owner, :, at, :].astype(F32) + land[owner, :, at, :].astype(F32)
        land[owner, :, at, :] = total.astype(BF)
        return 0

    lax.fori_loop(0, mp_count, join, 0)
    result = local(land, g_out, sem.at[0])
    for peer in peers:
        copy(peer, peer).wait_recv()
        copy(peer, me).wait_send()

    def sent(p, _):
        to_twin(p, 1 - core).wait_send()
        return 0

    lax.fori_loop(0, mp_count, sent, 0)
    keep.wait()
    result.wait()


def resid_back(dn, resid, up_own, gain, out_full, ctx, dp_count, mp_count, cid):
    rows, features = dn.shape
    _, chips, depth, cols = out_full.shape
    part = depth // dp_count
    return pl.pallas_call(
        functools.partial(resid_back_kernel, dp_count, mp_count),
        in_specs=[VM, VM, VM, VM, HBM, VM],
        out_specs=[VM, VM, HBM, HBM],
        out_shape=[
            jax.ShapeDtypeStruct((rows, features), F32),
            jax.ShapeDtypeStruct((1, features), F32),
            jax.ShapeDtypeStruct(ctx.shape, BF),
            jax.ShapeDtypeStruct((dp_count, chips, part, cols), BF),
        ],
        scratch_shapes=[
            pltpu.VMEM(out_full.shape, BF),
            pltpu.VMEM((rows, features), BF),
            pltpu.VMEM(ctx.shape, BF),
            pltpu.VMEM((2, dp_count, chips, part, cols), BF),
            pltpu.VMEM((dp_count, chips, part, cols), BF),
            DMA((mp_count,)),
            DMA((mp_count,)),
            DMA((mp_count,)),
            DMA((mp_count,)),
            DMA((2,)),
        ],
        compiler_params=pltpu.CompilerParams(
            collective_id=cid, has_side_effects=True, vmem_limit_bytes=62 << 20
        ),
        cost_estimate=pl.CostEstimate(
            flops=4 * rows * features * depth, bytes_accessed=110 << 20, transcendentals=0
        ),
    )(dn, resid, up_own, gain, out_full, ctx)


class Scatter:
    def __init__(self, line, both, slots, stage, tmp, twin_sems, slot_recv, sends):
        self.line, self.both, self.slots, self.stage, self.tmp = line, both, slots, stage, tmp
        self.twin_sems, self.slot_recv, self.sends = twin_sems, slot_recv, sends

    def add(self, chip, other, out=None):
        rows = self.both.shape[1]
        step = 32

        def body(i, _):
            at = pl.ds(pl.multiple_of(i * step, step), step)
            total = self.both[chip, at, :].astype(F32) + other(at)
            if out is None:
                self.both[chip, at, :] = total.astype(BF)
            else:
                out[at, :] = total
            return 0

        lax.fori_loop(0, rows // step, body, 0)

    def make(self, chip, block_sum):
        line = self.line
        copy = remote(
            self.stage,
            self.both.at[chip],
            self.twin_sems.at[0, chip],
            self.twin_sems.at[1, chip],
            line.twin,
        )
        block_sum(2 * chip + 1 - line.core, self.stage)
        copy.start()
        block_sum(2 * chip + line.core, self.tmp)
        copy.wait()
        self.add(chip, lambda at: self.tmp[at, :].astype(F32))

    def onward(self, chip, slot, way, away):
        line = self.line
        device = (line.right, line.left)[way]
        return remote(
            self.both.at[chip],
            self.slots.at[slot],
            self.sends.at[way, away],
            self.slot_recv.at[slot],
            device,
        )

    def arrived(self, slot):
        self.onward(0, slot, 0, 0).wait_recv()

    def pass_on(self, away, fed):
        line = self.line

        def take(chip, way):
            if fed:
                self.arrived(chip)
                self.add(chip, lambda at: self.slots[chip, at, :].astype(F32))
            last = jnp.where(away == 1, line.n, chip) if way == 1 else chip
            self.onward(chip, last, way, away).start()

        def wanted(has):
            return has if fed else jnp.logical_not(has)

        right = (line.chip + away < line.n) & wanted(line.has_left)
        left = (line.chip >= away) & wanted(line.has_right)
        pl.when(right)(lambda: take(line.chip + away, 0))
        pl.when(left)(lambda: take(line.chip - away, 1))

    def each(self, away, block_sum):
        line = self.line
        pl.when(line.chip + away < line.n)(lambda: self.make(line.chip + away, block_sum))
        pl.when(line.chip >= away)(lambda: self.make(line.chip - away, block_sum))

    def last(self, out):
        line = self.line

        def join():
            self.arrived(line.chip)
            self.add(line.chip, lambda at: self.slots[line.chip, at, :].astype(F32))

        pl.when(line.has_left & line.has_right)(join)
        end = jnp.where(line.has_right, line.n, line.chip)
        self.arrived(end)
        self.add(line.chip, lambda at: self.slots[end, at, :].astype(F32), out)

        def sent(away, _):
            wait = lambda way: self.onward(0, 0, way, away).wait_send()
            pl.when(line.chip + away < line.n)(lambda: wait(0))
            pl.when(line.chip >= away)(lambda: wait(1))
            return 0

        lax.fori_loop(1, line.n, sent, 0)

    def produce(self, away, block_sum):
        self.each(away, block_sum)
        self.pass_on(away, False)

    def run(self, block_sum, out, between=lambda: None):
        line = self.line
        far = line.n - 1
        self.produce(far, block_sum)

        def step(k, _):
            self.produce(far - 1 - k, block_sum)
            pl.when(k > 0)(lambda: self.pass_on(far - k, True))
            return 0

        lax.fori_loop(0, far - 1, step, 0)
        self.make(line.chip, block_sum)
        self.pass_on(1, True)
        between()
        self.last(out)


def scatter_scratch(mp_count, rows, width):
    n = mp_count // 2
    return [
        pltpu.VMEM((n, rows, width), BF),
        pltpu.VMEM((n + 1, rows, width), BF),
        pltpu.VMEM((rows, width), BF),
        pltpu.VMEM((rows, width), BF),
        DMA((2, n)),
        DMA((n + 1,)),
        DMA((2, n)),
    ]


def tiled(width, size=512):
    return [slice(at, min(at + size, width)) for at in range(0, width, size)]


def d_normed_kernel(
    mp_count, dq, dk, dv, w, tokens, gain, d_resid, picked, out, d_gain, owned,
    total, land, p_send, p_recv, *scratch
):
    line = Line(mp_count)
    rows, width = out.shape
    peers = others("mp", mp_count)
    greet_all([on_mp(peer) for peer in peers])

    def pick(device, source):
        return remote(
            picked.at[device], land.at[source], p_send.at[device], p_recv.at[source], on_mp(device)
        )

    for peer in peers:
        pick(peer, line.me).start()
    land[line.me] = picked[line.me]

    def block_sum(block, ref):
        at = pl.ds(pl.multiple_of(block * rows, rows), rows)
        for cols in tiled(width):
            part = dg(dq[at, :], w[0, cols, :], NT)
            part += dg(dk[at, :], w[1, cols, :], NT)
            part += dg(dv[at, :], w[2, cols, :], NT)
            ref[:, cols] = part.astype(BF)

    Scatter(line, *scratch).run(block_sum, total)

    def back(at, carry):
        d_value, d_g = norm_back(tokens[at, :].astype(F32), gain[0:1, :], total[at, :])
        out[at, :] = d_resid[at, :] + d_value
        return carry + d_g

    d_gain[...] = row_chunks(rows, back, jnp.zeros((1, width), F32))
    for peer in peers:
        pick(peer, peer).wait_recv()
        pick(peer, line.me).wait_send()
    owned[...] = lax.fori_loop(
        0, mp_count, lambda p, s: s + land[p].astype(F32), jnp.zeros(owned.shape, F32)
    )


def input_back(dq, dk, dv, w, tokens, gain, d_resid, picked, mp_count, cid):
    rows, width = tokens.shape
    return pl.pallas_call(
        functools.partial(d_normed_kernel, mp_count),
        in_specs=[VM] * 8,
        out_specs=[VM, VM, VM],
        out_shape=[
            jax.ShapeDtypeStruct((rows, width), F32),
            jax.ShapeDtypeStruct((1, width), F32),
            jax.ShapeDtypeStruct(picked.shape[1:], F32),
        ],
        scratch_shapes=[
            pltpu.VMEM((rows, width), F32),
            pltpu.VMEM(picked.shape, BF),
            DMA((mp_count,)),
            DMA((mp_count,)),
            *scatter_scratch(mp_count, rows, width),
        ],
        compiler_params=pltpu.CompilerParams(
            collective_id=cid, has_side_effects=True, vmem_limit_bytes=60 << 20
        ),
        cost_estimate=pl.CostEstimate(
            flops=6 * dq.size * width, bytes_accessed=280 << 20, transcendentals=0
        ),
    )(dq, dk, dv, w, tokens, gain, d_resid, picked)


def total_kernel(dp_count, mp_count, x, out, mid, by_mp, by_dp, m_send, m_recv, d_send, d_recv):
    me, dp = lax.axis_index("mp"), lax.axis_index("dp")
    mp_peers, dp_peers = others("mp", mp_count), others("dp", dp_count)
    greet_all([on_mp(peer) for peer in mp_peers] + [on_dp(peer) for peer in dp_peers])

    def over_mp(device, source):
        return remote(x, by_mp.at[source], m_send.at[device], m_recv.at[source], on_mp(device))

    def over_dp(device, source):
        return remote(mid, by_dp.at[source], d_send.at[device], d_recv.at[source], on_dp(device))

    def added(ref, count):
        total = ref[0]
        for k in range(1, count):
            total = total + ref[k]
        return total

    for peer in mp_peers:
        over_mp(peer, me).start()
    by_mp[me] = x[...]
    for peer in mp_peers:
        over_mp(peer, peer).wait_recv()
    mid[...] = added(by_mp, mp_count)
    for peer in dp_peers:
        over_dp(peer, dp).start()
    by_dp[dp] = mid[...]
    for peer in dp_peers:
        over_dp(peer, peer).wait_recv()
    out[...] = added(by_dp, dp_count)
    for peer in mp_peers:
        over_mp(peer, me).wait_send()
    for peer in dp_peers:
        over_dp(peer, dp).wait_send()


def total_everywhere(x, dp_count, mp_count, cid):
    return pl.pallas_call(
        functools.partial(total_kernel, dp_count, mp_count),
        in_specs=[VM],
        out_specs=VM,
        out_shape=jax.ShapeDtypeStruct(x.shape, F32),
        scratch_shapes=[
            pltpu.VMEM(x.shape, F32),
            pltpu.VMEM((mp_count, *x.shape), F32),
            pltpu.VMEM((dp_count, *x.shape), F32),
            DMA((mp_count,)),
            DMA((mp_count,)),
            DMA((dp_count,)),
            DMA((dp_count,)),
        ],
        compiler_params=pltpu.CompilerParams(collective_id=cid, has_side_effects=True),
        cost_estimate=pl.CostEstimate(flops=0, bytes_accessed=36 << 20, transcendentals=0),
    )(x)


def attend_bwd_kernel(
    hp, bq, steps, mp_count,
    len_ref, q_ref, k_ref, v_ref, o_ref, do_ref, lse_ref, part,
    dq_ref, dk_ref, dv_ref, out,
    dka, dva, io_sem, *scratch
):
    line = Line(mp_count)
    flat = flat_step()
    scatter = Scatter(line, *scratch)

    def block_sum(block, ref):
        local(part.at[block], ref, io_sem).wait()

    @pl.when(flat == 0)
    def _():
        line.greet()
        for away in range(line.n - 1, 0, -1):
            scatter.produce(away, block_sum)
        scatter.make(line.chip, block_sum)

    bwd_block(
        hp, bq, len_ref, q_ref, k_ref, v_ref, o_ref, do_ref, lse_ref,
        dq_ref, dk_ref, dv_ref, dka, dva,
    )
    for away in range(line.n - 2, 0, -1):
        turn = min(steps - 1, (line.n - 1 - away) * steps // (line.n - 2))

        @pl.when(flat == turn)
        def _(away=away):
            scatter.pass_on(away, True)

    @pl.when(flat == steps - 1)
    def _():
        scatter.last(out)


def attend_bwd(seg_len, q, k, v, o, do, lse, part, mp_count, cid, bq=512):
    total, hw = q.shape
    _, rows, features = part.shape
    heads = hw // HD
    hp = 2 if heads % 2 == 0 else 1
    width, nb, segs, pairs = hp * HD, SLOT // bq, total // SLOT, heads // hp
    blk = pl.BlockSpec((bq, width), lambda s, p, i: (s * nb + i, p))
    full = pl.BlockSpec((SLOT, width), lambda s, p, i: (s, p))
    sh = jax.ShapeDtypeStruct((total, hw), BF)
    return pl.pallas_call(
        functools.partial(attend_bwd_kernel, hp, bq, segs * pairs * nb, mp_count),
        grid=(segs, pairs, nb),
        in_specs=[
            pl.BlockSpec(memory_space=pltpu.SMEM),
            blk,
            full,
            full,
            blk,
            blk,
            pl.BlockSpec((1, hp, 8, bq), lambda s, p, i: (s, p, 0, i)),
            HBM,
        ],
        out_specs=[
            blk,
            full,
            full,
            pl.BlockSpec((rows, features), lambda s, p, i: (0, 0)),
        ],
        out_shape=[sh, sh, sh, jax.ShapeDtypeStruct((rows, features), F32)],
        scratch_shapes=[
            pltpu.VMEM((SLOT, width), F32),
            pltpu.VMEM((SLOT, width), F32),
            DMA(()),
            *scatter_scratch(mp_count, rows, features),
        ],
        compiler_params=pltpu.CompilerParams(
            collective_id=cid, has_side_effects=True, vmem_limit_bytes=60 << 20
        ),
        cost_estimate=pl.CostEstimate(
            flops=segs * heads * SLOT * SLOT * 320,
            bytes_accessed=290 << 20,
            transcendentals=segs * heads * SLOT * SLOT // 2,
        ),
    )(seg_len, q, k, v, o, do, lse, part)


GELU_C = math.sqrt(2.0 / math.pi)


class NearScatter:
    def __init__(self, line, kept, both, slots, stage, tmp, t_send, t_recv, slot_recv, sends, sem):
        self.line, self.kept, self.both, self.slots = line, kept, both, slots
        self.stage, self.tmp, self.t_send, self.t_recv = stage, tmp, t_send, t_recv
        self.slot_recv, self.sends, self.sem = slot_recv, sends, sem
        self.pieces = slot_recv.shape[1]
        self.size = both.shape[1] // self.pieces

    def add(self, chip, other, piece, out=None):
        step = 32

        def body(i, _):
            at = pl.ds(pl.multiple_of(piece * self.size + i * step, step), step)
            total = self.both[chip, at, :].astype(F32) + other(at)
            if out is None:
                self.both[chip, at, :] = total.astype(BF)
            else:
                out[at, :] = total
            return 0

        lax.fori_loop(0, self.size // step, body, 0)

    def across(self, chip):
        return remote(
            self.stage, self.both.at[chip], self.t_send, self.t_recv.at[chip], self.line.twin
        )

    def keep(self, block):
        local(self.tmp, self.kept.at[block // 2], self.sem).wait()

    def join(self, chip):
        self.across(chip).wait_recv()
        local(self.kept.at[chip], self.tmp, self.sem).wait()
        for piece in range(self.pieces):
            self.add(chip, lambda at: self.tmp[at, :].astype(F32), piece)

    def onward(self, chip, slot, way, away, piece):
        line = self.line
        device = (line.right, line.left)[way]
        at = slice(piece * self.size, (piece + 1) * self.size)
        return remote(
            self.both.at[chip, at, :], self.slots.at[slot, at, :],
            self.sends.at[way, away, piece], self.slot_recv.at[slot, piece], device,
        )

    def arrived(self, slot, piece):
        self.onward(0, slot, 0, 0, piece).wait_recv()

    def pass_on(self, chip, way, away, fed):
        last = jnp.where(away == 1, self.line.n, chip) if way == 1 else chip
        for piece in range(self.pieces):
            if fed:
                self.arrived(chip, piece)
                self.add(chip, lambda at: self.slots[chip, at, :].astype(F32), piece)
            self.onward(chip, last, way, away, piece).start()

    def pass_unfed(self, away):
        line = self.line
        right = (line.chip + away < line.n) & jnp.logical_not(line.has_left)
        left = (line.chip >= away) & jnp.logical_not(line.has_right)
        pl.when(right)(lambda: self.pass_on(line.chip + away, 0, away, False))
        pl.when(left)(lambda: self.pass_on(line.chip - away, 1, away, False))

    def pass_fed(self, turn):
        line = self.line
        right = turn - 2 * line.chip
        left = turn - 2 * (line.n - 1 - line.chip)
        to_right = line.has_left & (right >= 1) & (line.chip + right < line.n)
        to_left = line.has_right & (left >= 1) & (line.chip >= left)
        pl.when(to_right)(lambda: self.pass_on(line.chip + right, 0, right, True))
        pl.when(to_left)(lambda: self.pass_on(line.chip - left, 1, left, True))

    def last(self, out):
        line = self.line
        end = jnp.where(line.has_right, line.n, line.chip)
        for piece in range(self.pieces):
            def join(piece=piece):
                self.arrived(line.chip, piece)
                self.add(line.chip, lambda at: self.slots[line.chip, at, :].astype(F32), piece)

            pl.when(line.has_left & line.has_right)(join)
            self.arrived(end, piece)
            self.add(line.chip, lambda at: self.slots[end, at, :].astype(F32), piece, out)

        def sent(away, _):
            def wait(way):
                for piece in range(self.pieces):
                    self.onward(0, 0, way, away, piece).wait_send()

            pl.when(line.chip + away < line.n)(lambda: wait(0))
            pl.when(line.chip >= away)(lambda: wait(1))
            return 0

        lax.fori_loop(1, line.n, sent, 0)


PIECES = 4


def ffn_kernel(
    mp_count, own, u_all, up, down, out, x_all, part_out, kept, g_out,
    x, u, hid, pre, part, tile, g_tile, io_sem, recv, sends, sem, *scratch
):
    line = Line(mp_count)
    line.greet()
    rows, width = out.shape
    units = up.shape[1]
    span = tile.shape[3]
    per = g_out.shape[2] // span
    gather = Gather(line, own, lambda block: x_all.at[block], recv, sends, sem)
    scatter = NearScatter(line, kept, *scratch)
    gather.start()

    def saved(block):
        return pltpu.make_async_copy(part, part_out.at[block], io_sem.at[2])

    def terms(block, ref, first=False):
        at = pl.ds(pl.multiple_of(block * rows, rows), rows)
        one = local(x_all.at[block], x, io_sem.at[0])
        two = local(u_all.at[block], u, io_sem.at[1])
        one.wait()
        two.wait()
        for cols in tiled(units, 256):
            value = dg(x[...], up[:, cols], NN)
            d_hidden = dg(u[...], down[cols, :], NT)
            square = value * value
            bend = jnp.tanh(GELU_C * (value + 0.044715 * value * square))
            half = 0.5 * (1.0 + bend)
            hid[at, cols] = (value * half).astype(BF)
            slope = half + 0.5 * value * (1.0 - bend * bend) * (
                GELU_C * (1.0 + 3.0 * 0.044715 * square)
            )
            pre[at, cols] = (d_hidden * slope).astype(BF)
        if not first:
            saved(block).wait()
        for cols in tiled(width):
            ref[:, cols] = dg(pre[at, :], up[cols, :], NT).astype(BF)
            part[:, cols] = dg(hid[at, :], down[:, cols], NN).astype(BF)
        saved(block).start()

    def mine(block, first=False):
        terms(block, scatter.tmp, first)
        scatter.keep(block)

    def other(block, first=False):
        gather.arrived(block)
        if not first:
            scatter.across(0).wait_send()
        terms(block, scatter.stage)
        scatter.across(block // 2).start()

    gather.mine.wait()
    mine(line.me, True)
    other(2 * line.chip + 1 - line.core, True)
    gather.forward(1, True)

    def step(away, _):
        gather.forward(away, False)
        gather.each(away, mine, line.core)
        pl.when(away < line.n - 1)(lambda: gather.forward(away + 1, True))
        gather.each(away, other, 1 - line.core)
        gather.each(away, lambda block: scatter.join(block // 2), line.core)
        scatter.pass_unfed(away)
        return 0

    lax.fori_loop(1, line.n, step, 0)
    saved(0).wait()
    scatter.across(0).wait_send()

    def fetch(i, which):
        source = (x_all, u_all)[which]
        at = pl.ds(pl.multiple_of(i * span, span), span)
        return pltpu.make_async_copy(source.at[:, :, at], tile.at[which], io_sem.at[which])

    def store(i, which):
        at = pl.ds(pl.multiple_of(lax.rem(i, per) * span, span), span)
        target = g_out.at[lax.div(i, per), which, at, :]
        return pltpu.make_async_copy(g_tile.at[which], target, io_sem.at[2 + which])

    tiles = width // span

    def weigh(i, _):
        fetch(i, 1).start()
        for which, factor in ((0, pre), (1, hid)):
            fetch(i, which).wait()
            value = tile[which].reshape(mp_count * rows, span)
            pl.when(i > 0)(lambda which=which: store(0, which).wait())
            g_tile[which] = dg(value, factor[...], TN).astype(BF)
            store(i, which).start()
            if which == 0:
                pl.when(i + 1 < tiles)(lambda: fetch(i + 1, 0).start())
        return 0

    turns = 2 * line.n - 3
    early = tiles // 2
    share = -(-early // max(turns - 3, 1))
    fetch(0, 0).start()

    def turn(k, _):
        scatter.pass_fed(k + 1)
        lax.fori_loop(
            jnp.minimum(k * share, early), jnp.minimum((k + 1) * share, early), weigh, 0
        )
        return 0

    lax.fori_loop(0, turns, turn, 0)
    lax.fori_loop(early, tiles, weigh, 0)
    store(0, 0).wait()
    store(0, 1).wait()
    scatter.join(line.chip)
    scatter.last(out)
    gather.finish()


def ffn(own, u_all, up, down, dp_count, mp_count, cid):
    rows, width = own.shape
    units = up.shape[1]
    total = mp_count * rows
    chips = mp_count // 2
    span = 256 if mp_count <= 8 else 128
    return pl.pallas_call(
        functools.partial(ffn_kernel, mp_count),
        in_specs=[HBM, HBM, VM, VM],
        out_specs=[VM, HBM, HBM, HBM, HBM],
        out_shape=[
            jax.ShapeDtypeStruct((rows, width), F32),
            jax.ShapeDtypeStruct((mp_count, rows, width), BF),
            jax.ShapeDtypeStruct((mp_count, rows, width), BF),
            jax.ShapeDtypeStruct((chips, rows, width), BF),
            jax.ShapeDtypeStruct((dp_count, 2, width // dp_count, units), BF),
        ],
        scratch_shapes=[
            pltpu.VMEM((rows, width), BF),
            pltpu.VMEM((rows, width), BF),
            pltpu.VMEM((total, units), BF),
            pltpu.VMEM((total, units), BF),
            pltpu.VMEM((rows, width), BF),
            pltpu.VMEM((2, mp_count, rows, span), BF),
            pltpu.VMEM((2, span, units), BF),
            DMA((4,)),
            *gather_sems(mp_count),
            pltpu.VMEM((chips, rows, width), BF),
            pltpu.VMEM((chips + 1, rows, width), BF),
            pltpu.VMEM((rows, width), BF),
            pltpu.VMEM((rows, width), BF),
            DMA(()),
            DMA((chips,)),
            DMA((chips + 1, PIECES)),
            DMA((2, chips, PIECES)),
            DMA(()),
        ],
        compiler_params=pltpu.CompilerParams(
            collective_id=cid, has_side_effects=True, vmem_limit_bytes=62 << 20
        ),
        cost_estimate=pl.CostEstimate(
            flops=12 * total * width * units,
            bytes_accessed=530 << 20,
            transcendentals=total * units,
        ),
    )(own, u_all, up, down)


def shampoo_kernel(group, tc, flipped, w_ref, g_ref, l_ref, r_ref, nw_ref, nl_ref, nr_ref, gf_ref):
    for h in range(group):
        cols = slice(h * tc, (h + 1) * tc)
        g = g_ref[...].T if flipped else g_ref[:, cols]
        gf_ref[:, cols] = g.astype(F32)
        nl_ref[0, h] = DECAY * l_ref[0, 0, h] + (1.0 - DECAY) * dg(g, g, NT)
        nr_ref[0, h] = DECAY * r_ref[0, 0, h] + (1.0 - DECAY) * dg(g, g, TN)
        mid = dg(l_ref[1, 0, h].astype(BF), g, NN).astype(BF)
        step = dg(mid, r_ref[1, 0, h].astype(BF), NN)
        nw_ref[:, cols] = w_ref[:, cols] - SHAMPOO_RATE * step


def shampoo(weight, grad, left, right, tr, tc, flipped=False):
    rows, cols = weight.shape
    tiles_c = cols // tc
    group = 1 if tc % 128 == 0 or tiles_c == 1 else 2
    width = group * tc
    wide = pl.BlockSpec((tr, width), lambda i, j: (i, j))
    grad_block = pl.BlockSpec((width, tr), lambda i, j: (j, i)) if flipped else wide

    def stat(size):
        return pl.BlockSpec((2, 1, group, size, size), lambda i, j: (0, i, j, 0, 0))

    def new(size):
        return pl.BlockSpec((1, group, size, size), lambda i, j: (i, j, 0, 0))

    return pl.pallas_call(
        functools.partial(shampoo_kernel, group, tc, flipped),
        grid=(rows // tr, tiles_c // group),
        in_specs=[wide, grad_block, stat(tr), stat(tc)],
        out_specs=[wide, new(tr), new(tc), wide],
        out_shape=[
            jax.ShapeDtypeStruct(weight.shape, F32),
            jax.ShapeDtypeStruct(left.shape[1:], F32),
            jax.ShapeDtypeStruct(right.shape[1:], F32),
            jax.ShapeDtypeStruct(weight.shape, F32),
        ],
        compiler_params=pltpu.CompilerParams(vmem_limit_bytes=48 << 20),
        cost_estimate=pl.CostEstimate(
            flops=4 * rows * cols * (tr + tc),
            bytes_accessed=6 * (left.size + right.size) + 14 * rows * cols,
            transcendentals=0,
        ),
    )(weight, grad, left, right)


def layer_norm(value, gain):
    mean = jnp.mean(value, axis=-1, keepdims=True)
    centred = value - mean
    spread = jnp.mean(centred * centred, axis=-1, keepdims=True)
    return centred * lax.rsqrt(spread + NORM_EPSILON) * gain


def body(
    tokens,
    seg_len,
    cotangent,
    ln_gain,
    qkv_weight,
    out_weight,
    up_weight,
    down_weight,
    left_qkv,
    right_qkv,
    left_out,
    right_out,
    left_up,
    right_up,
    left_down,
    right_down,
):
    row_count, features = tokens.shape
    dp_count, mp_count = lax.axis_size("dp"), lax.axis_size("mp")
    chips = mp_count // 2
    lines = [[2 * chip + core for chip in range(chips)] for core in range(2)]
    mp_index = lax.axis_index("mp")
    seg_count = seg_len.shape[0]
    own_rows, own_cols = qkv_weight.shape
    head_count = own_cols // (3 * HD)
    head_width = head_count * HD
    inputs = tokens.astype(F32)
    by_kind = (
        qkv_weight.astype(BF)
        .reshape(own_rows, head_count, 3, HD)
        .transpose(2, 0, 1, 3)
        .reshape(3, own_rows, head_width)
    )
    normed_one = layer_norm(inputs, ln_gain[0]).astype(BF)
    gathered, queries, keys, values, qkv_full = gather_qkv(
        normed_one, by_kind, dp_count, mp_count, 1
    )
    positions = mp_index * row_count + jnp.arange(row_count)
    owner_seg = positions // SLOT
    own_length = jnp.sum(
        jnp.where(owner_seg[:, None] == jnp.arange(seg_count)[None, :], seg_len[None, :], 0), axis=1
    )
    valid = positions % SLOT < own_length + NSUM
    upstream = jnp.where(valid[:, None], cotangent, jnp.zeros_like(cotangent))
    up_part = lax.all_gather(up_weight.astype(BF), "dp", axis=0, tiled=True)
    down_part = lax.all_gather(down_weight.astype(BF), "dp", axis=1, tiled=True)
    context, log_sums, ctx_rows, upstream_all, out_full = attend_fwd(
        seg_len, queries, keys, values, upstream, out_weight.astype(BF), dp_count, mp_count, 2
    )
    resid, normed_two = out_and_norm(ctx_rows, out_full, tokens, ln_gain, mp_count)
    d_normed_two, _, ffn_part, _, grad_ffn = ffn(
        normed_two, upstream_all, up_part, down_part, dp_count, mp_count, 4
    )
    d_resid, d_gain_two, d_context, grad_out = resid_back(
        d_normed_two, resid, upstream, ln_gain, out_full, ctx_rows, dp_count, mp_count, 5
    )
    grad_ffn = lax.psum_scatter(grad_ffn, "dp", scatter_dimension=0, tiled=False)
    d_queries, d_keys, d_values, ffn_out = attend_bwd(
        seg_len,
        queries,
        keys,
        values,
        context,
        d_context.reshape(mp_count * row_count, head_width),
        log_sums,
        ffn_part,
        mp_count,
        6,
    )
    block_out = (resid + ffn_out).astype(BF)
    d_qkv = jnp.concatenate([d_queries, d_keys, d_values], axis=1)
    d_qkv, grad_out, grad_ffn = lax.optimization_barrier((d_qkv, grad_out, grad_ffn))
    grad_out = lax.psum_scatter(grad_out, "dp", scatter_dimension=0, tiled=False)
    gathered = gathered.reshape(mp_count * row_count, features)
    grad_qkv_part = jnp.einsum("gd,gc->dc", gathered, d_qkv, preferred_element_type=F32)
    grad_qkv = lax.psum_scatter(
        grad_qkv_part.astype(BF), "dp", scatter_dimension=0, tiled=True
    )
    picks = seg_count * NSUM
    padded = -(-picks // 16) * 16
    slot_index = (jnp.arange(seg_count) * SLOT + seg_len)[:, None] + jnp.arange(NSUM)[None, :]
    slot_index = jnp.pad(slot_index.reshape(-1), (0, padded - picks), constant_values=-1)
    selector = (slot_index[:, None] == positions[None, :]).astype(BF)
    picked = jnp.dot(selector, block_out, preferred_element_type=F32).astype(BF)
    picked = picked.reshape(padded, mp_count, features // mp_count).transpose(1, 0, 2)
    input_grad, d_gain_one, owned_vectors = input_back(
        d_queries, d_keys, d_values, qkv_full, tokens, ln_gain, d_resid, picked, mp_count, 7
    )
    d_gain_one, grad_ffn, grad_qkv, grad_out = lax.optimization_barrier(
        (d_gain_one, grad_ffn, grad_qkv, grad_out)
    )
    grad_up, grad_down = grad_ffn[0], grad_ffn[1]
    grad_out = lax.psum_scatter(
        grad_out, "mp", scatter_dimension=0, tiled=False, axis_index_groups=lines
    )
    grad_qkv = (
        grad_qkv.reshape(own_rows, 3, head_count, HD)
        .transpose(0, 2, 1, 3)
        .reshape(own_rows, own_cols)
    )
    owned_vectors = owned_vectors[:picks].reshape(seg_count, NSUM, features // mp_count)
    owned_width = owned_vectors.shape[2]
    col_sums = jnp.sum(owned_vectors, axis=(0, 1))
    spread_sums = (
        (jnp.arange(mp_count) == mp_index).astype(F32)[:, None] * col_sums[None, :]
    ).reshape(1, features)
    squares = jnp.full((1, features), jnp.sum(owned_vectors * owned_vectors))
    stats = jnp.concatenate([d_gain_one, d_gain_two, spread_sums, squares] * 2)
    stats = total_everywhere(stats, dp_count, mp_count, 8)
    gain_grads, total_cols, total_squares = stats[:2], stats[2], stats[3, 0]
    vector_count = seg_count * dp_count * NSUM
    centre_all = total_cols / vector_count
    centre = lax.dynamic_slice_in_dim(centre_all, mp_index * owned_width, owned_width, 0)
    variance = total_squares / (vector_count * features) - jnp.mean(centre_all * centre_all)
    summaries = (owned_vectors - centre) * lax.rsqrt(variance + NORM_EPSILON)
    new_gains = ln_gain - GAIN_RATE * gain_grads * lax.rsqrt(
        jnp.mean(gain_grads * gain_grads, axis=-1, keepdims=True) + 1e-06
    )
    new_qkv, new_left_qkv, new_right_qkv, grad_qkv = shampoo(
        qkv_weight, grad_qkv, left_qkv, right_qkv, BLOCK, 3 * HD
    )
    new_out, new_left_out, new_right_out, grad_out = shampoo(
        out_weight, grad_out, left_out, right_out, BLOCK, HD
    )
    new_up, new_left_up, new_right_up, grad_up = shampoo(
        up_weight, grad_up, left_up, right_up, BLOCK, FBLK
    )
    new_down, new_left_down, new_right_down, grad_down = shampoo(
        down_weight, grad_down, left_down, right_down, FBLK, BLOCK, True
    )
    return (
        block_out,
        input_grad,
        summaries,
        gain_grads,
        new_gains,
        grad_qkv,
        grad_out,
        grad_up,
        grad_down,
        new_qkv,
        new_out,
        new_up,
        new_down,
        new_left_qkv,
        new_right_qkv,
        new_left_out,
        new_right_out,
        new_left_up,
        new_right_up,
        new_left_down,
        new_right_down,
    )


def solution(mesh):
    in_specs = (
        P(("dp", "mp"), None),
        P("dp"),
        P(("dp", "mp"), None),
        P(),
        P("dp", "mp"),
        P("dp", "mp"),
        P("dp", "mp"),
        P("mp", "dp"),
        P(None, "dp", "mp", None, None),
        P(None, "dp", "mp", None, None),
        P(None, "dp", "mp", None, None),
        P(None, "dp", "mp", None, None),
        P(None, "dp", "mp", None, None),
        P(None, "dp", "mp", None, None),
        P(None, "mp", "dp", None, None),
        P(None, "mp", "dp", None, None),
    )
    out_specs = (
        P(("dp", "mp"), None),
        P(("dp", "mp"), None),
        P("dp", None, "mp"),
        P(),
        P(),
        P("dp", "mp"),
        P("dp", "mp"),
        P("dp", "mp"),
        P("mp", "dp"),
        P("dp", "mp"),
        P("dp", "mp"),
        P("dp", "mp"),
        P("mp", "dp"),
        P("dp", "mp", None, None),
        P("dp", "mp", None, None),
        P("dp", "mp", None, None),
        P("dp", "mp", None, None),
        P("dp", "mp", None, None),
        P("dp", "mp", None, None),
        P("mp", "dp", None, None),
        P("mp", "dp", None, None),
    )
    return jax.shard_map(body, mesh=mesh, in_specs=in_specs, out_specs=out_specs, check_vma=False)
```

time: 999 us -> 760 us (0.76)
  waiting for transfers between devices: 181 us -> 2.99 us
  Pallas kernels: 564 us -> 675 us
  local copies, waits for them, and re-layouts: 101 us -> 29.9 us
  matrix products: 63.5 us -> 11.7 us
  blocking collectives: 39.2 us -> 0 us
  other arithmetic: 34.4 us -> 17.8 us
    reduce_scatter x7 -> x1, waiting for transfers between devices: 93.4 us -> 0.01 us  [body(): lax.psum_scatter(grad_out, 'mp', scatter_dimension=0, tiled=False, axis_i...]
    all_gather x4 -> x0, waiting for transfers between devices: 86.9 us -> none  [the longest x1 52.8 us: body(): out_half = lax.all_gather(out_line, 'dp', axis=0, tiled=True)]
    pallas_call x10, Pallas kernels: 337 us -> 404 us  [the longest x1 122 us: attend_fwd(): pl.pallas_call(functools.partial(attend_fwd_kernel, hp, bq, segs * pairs...]
    pallas_call x1, Pallas kernels: 117 us -> 182 us  [ffn(): pl.pallas_call(functools.partial(ffn_kernel, mp_count), in_specs=[HBM, HB...]
    dot_general x6 -> x1, matrix products: 52.1 us -> 0.33 us  [body(): picked = jnp.dot(selector, block_out, preferred_element_type=F32).astype(BF)]
    reshape x4 -> x1, local copies, waits for them, and re-layouts: 51.8 us -> 0.72 us  [body(): picked.reshape(padded, mp_count, features // mp_count).transpose(1, 0, 2)]
    psum x1 -> x0, blocking collectives: 39.2 us -> none  [body(): lax.psum((gain_parts, spread_sums, jnp.sum(owned_vectors * owned_vectors)...]
    pallas_call x1, Pallas kernels: 110 us -> 89.7 us  [gather_qkv(): pl.pallas_call(functools.partial(qkv_kernel, dp_count, mp_count), in_spec...]
  transfers between devices with their start and end apart: 14 -> 6, of which waited for: 5 -> 1; matrix products, arithmetic and copies ran while one was open for 13% -> 3% of each run, Pallas kernels for 44% -> 62%
where the time goes in v3:
time: 760 us; the launch traced here: 755 us
  Pallas kernels  675 us (89%)
  local copies, waits for them, and re-layouts  29.9 us (4%)
  other arithmetic  17.8 us (2%)
  between operations  16.8 us (2%)
  matrix products  11.7 us (2%)
    pallas_call x1, Pallas kernels, ffn(): pl.pallas_call(functools.partial(ffn_kernel, mp_count), in_specs=[HBM, HB...  182 us
    pallas_call x1, Pallas kernels, attend_fwd(): pl.pallas_call(functools.partial(attend_fwd_kernel, hp, bq, segs * pairs...  122 us
    pallas_call x1, Pallas kernels, attend_bwd(): pl.pallas_call(functools.partial(attend_bwd_kernel, hp, bq, segs * pairs...  95.5 us
    pallas_call x1, Pallas kernels, gather_qkv(): pl.pallas_call(functools.partial(qkv_kernel, dp_count, mp_count), in_spec...  89.7 us
    pallas_call x1, Pallas kernels, input_back(): pl.pallas_call(functools.partial(d_normed_kernel, mp_count), in_specs=[VM...  88.3 us
    pallas_call x1, Pallas kernels, resid_back(): pl.pallas_call(functools.partial(resid_back_kernel, dp_count, mp_count),...  43.2 us
    pallas_call x4, Pallas kernels, shampoo(): pl.pallas_call(functools.partial(shampoo_kernel, group, tc, flipped), gri...  29.6 us
    pallas_call x1, Pallas kernels, total_everywhere(): pl.pallas_call(functools.partial(total_kernel, dp_count, mp_count), in_sp...  19.6 us
  transfers between devices with their start and end apart: 6, of which 1 were waited for; matrix products, arithmetic and copies ran while one was open for 3% of the time, Pallas kernels for 62%

profile of v3, /device:TPU:0, one launch (start us, length us, event | category | flops | bytes accessed | tf_op | source)
XLA Modules:
  0.0 755.0 jit_solution(18228489729006425514)
XLA Ops:
  7.2 0.0 all-gather.3.cloned.1.call-start
  7.2 2.9 convert_element_type.39
  10.1 0.0 all-gather.5.cloned.1.call-start
  10.2 1.1 convert_element_type.40
  11.3 0.0 all-gather.5.cloned.1.call-update
  11.3 0.0 reduce-scatter.13.cloned.1.call-start
  12.1 1.8 copy.48
  13.9 1.0 copy.49
  14.8 1.4 copy.50.w_own
  16.3 0.2 convert_reduce_fusion
  16.6 0.4 fusion.2
  17.0 2.3 broadcast_select_fusion.up_own
  19.3 0.4 fusion.4.own
  19.7 89.7 %shard_map.319 = (bf16[8,256,2048]{2,1,0:T(8,128)(2,1)}, bf16[2048,256]{1,0:T(8,128)(2,1)S(1)}, bf16[2048,256]{1,0:T(8,128)(2,1)S(1)}, bf16[2048,256]{1,0:T(8,128)(2,1)S(1)}, bf16[3,2048,256]{2,1,0:T(8,128)(2,1)S(1)}) custom-call(bf16[256,2048]{1,0:T(8,128)(2,1)S(1)} %fusion.4.own, bf16[3,512,256]{2,1,0:T(8,128)(2,1)S(1)} %copy.50.w_own), custom_call_target="tpu_custom_call" | custom-call | flops 6442450944 | bytes 293601280 | tf_op jit(solution)/shard_map/pallas_call | solution.py:318
  109.5 1.7 copy-done.22
  111.1 121.8 %shard_map.320 = (bf16[2048,256]{1,0:T(8,128)(2,1)S(1)}, f32[1,4,8,2048]{3,2,1,0:T(8,128)S(1)}, bf16[8,256,256]{2,1,0:T(8,128)(2,1)S(1)}, bf16[8,256,2048]{2,1,0:T(8,128)(2,1)}, bf16[2,4,2048,256]{3,2,1,0:T(8,128)(2,1)}) custom-call(s32[1]{0:T(128)} %copy.61.len_ref, bf16[2048,256]{1,0:T(8,128)(2,1)S(1)} %get-tuple-element.70.q_ref, ...), custom_call_target="tpu_custom_call" | custom-call | flops 2147483648 | bytes 398458880 | tf_op jit(solution)/shard_map/pallas_call | solution.py:493
  233.0 1.0 copy-done.21
  234.0 0.7 copy-done.23
  234.7 3.8 copy-done.1
  238.4 5.6 shard_map.321
  244.1 1.3 copy-done.7
  245.4 1.0 copy-done.17
  246.4 182.1 %shard_map.322 = (f32[256,2048]{1,0:T(8,128)}, bf16[8,256,2048]{2,1,0:T(8,128)(2,1)}, bf16[8,256,2048]{2,1,0:T(8,128)(2,1)}, bf16[4,256,2048]{2,1,0:T(8,128)(2,1)}, bf16[4,2,512,1024]{3,2,1,0:T(8,128)(2,1)}) custom-call(bf16[256,2048]{1,0:T(8,128)(2,1)} %copy-done.17, bf16[8,256,2048]{2,1,0:T(8,128)(2,1)} %get-tuple-element.78.u_all, ...), custom_call_target="tpu_custom_call" | custom-call | flops 51539607552 | bytes 555745280 | tf_op jit(solution)/shard_map/pallas_call | solution.py:1306
  428.5 0.0 reduce-scatter.13.cloned.1.call-update
  428.5 0.0 reduce-scatter.9.cloned.1.call-start
  428.6 43.2 %shard_map.323 = (f32[256,2048]{1,0:T(8,128)}, f32[1,2048]{1,0:T(1,128)}, bf16[8,256,256]{2,1,0:T(8,128)(2,1)}, bf16[4,4,512,256]{3,2,1,0:T(8,128)(2,1)}) custom-call(f32[256,2048]{1,0:T(8,128)} %get-tuple-element.79.dn, f32[256,2048]{1,0:T(8,128)} %copy-done.7, bf16[256,2048]{1,0:T(8,128)(2,1)} %broadcast_select_fusion.up_own, f32[2,2048]{1,0:T(2,128)} %gain.5, ...), custom_call_target="tpu_custom_call" | custom-call | flops 4294967296 | bytes 115343360 | tf_op jit(solution)/shard_map/pallas_call | solution.py:716
  471.8 95.5 %shard_map.324 = (bf16[2048,256]{1,0:T(8,128)(2,1)}, bf16[2048,256]{1,0:T(8,128)(2,1)}, bf16[2048,256]{1,0:T(8,128)(2,1)}, f32[256,2048]{1,0:T(8,128)}) custom-call(s32[1]{0:T(128)} %copy.61.len_ref, bf16[2048,256]{1,0:T(8,128)(2,1)} %copy-done.18, bf16[2048,256]{1,0:T(8,128)(2,1)} %copy-done.19, bf16[2048,256]{1,0:T(8,128)(2,1)} %copy-done.20, ...), custom_call_target="tpu_custom_call" | custom-call | flops 5368709120 | bytes 304087040 | tf_op jit(solution)/shard_map/pallas_call | solution.py:1046
  567.3 3.1 pad_maximum_fusion
  570.5 11.4 %convolution_convert_fusion = bf16[2048,768]{1,0:T(8,128)(2,1)} fusion(bf16[2048,2048]{1,0:T(8,128)(2,1)} %bitcast.53, bf16[2048,768]{1,0:T(8,128)(2,1)} %pad_maximum_fusion), kind=kOutput, calls=%fused_computation | convolution fusion | flops 6444023808 | bytes 14680064 | tf_op jit(solution)/shard_map/gd,gc->dc/dot_general | solution.py:1476
  581.9 0.0 reduce-scatter.15.cloned.1.call-start
  581.9 0.5 reduce-scatter.15.cloned.1.call-update
  582.5 0.0 reduce-scatter.11.cloned.1.call-start
  582.6 0.9 copy-done.8
  583.4 1.8 add_convert_fusion
  585.3 1.0 copy-done.24
  586.2 0.3 convolution_convert_fusion.1
  586.6 0.7 copy.59
  587.3 88.3 %shard_map.325 = (f32[256,2048]{1,0:T(8,128)}, f32[1,2048]{1,0:T(1,128)}, f32[64,256]{1,0:T(8,128)}) custom-call(bf16[2048,256]{1,0:T(8,128)(2,1)} %get-tuple-element.84.dq, bf16[2048,256]{1,0:T(8,128)(2,1)} %get-tuple-element.85.dk, bf16[2048,256]{1,0:T(8,128)(2,1)} %get-tuple-element.86.dv, bf16[3,2048,256]{2,1,0:T(8,128)(2,1)} %copy-done.22, ...), custom_call_target="tpu_custom_call" | custom-call | flops 6442450944 | bytes 293601280 | tf_op jit(solution)/shard_map/pallas_call | solution.py:921
  675.6 1.4 multiply_reduce_fusion
  677.0 0.1 multiply_bitcast_fusion.1
  677.1 0.0 reduce-scatter.9.cloned.1.call-done
  677.1 2.3 reduce-scatter.15.cloned.1.call-done
  679.5 0.6 broadcast_in_dim.28
  680.1 1.6 concatenate.7.x
  681.7 19.6 %shard_map.326 = f32[8,2048]{1,0:T(8,128)} custom-call(f32[8,2048]{1,0:T(8,128)} %concatenate.7.x), custom_call_target="tpu_custom_call" | custom-call | bytes 37748736 | tf_op jit(solution)/shard_map/pallas_call | solution.py:982
  701.3 1.2 slice.24
  703.1 1.5 multiply_reduce_fusion.2
  705.3 0.8 multiply_bitcast_fusion
  706.1 0.7 copy.55
  706.8 1.4 copy.52
  708.2 1.0 copy.53
  709.2 1.4 copy.54.g_ref
  710.6 1.4 copy-done.11
  712.0 6.8 shard_map.327
  718.9 0.2 slice_bitcast_fusion
  719.1 1.4 copy-done.2
  720.5 0.6 copy-done.9
  721.1 8.5 %shard_map.329 = (f32[512,1024]{1,0:T(8,128)}, f32[1,4,512,512]{3,2,1,0:T(8,128)}, f32[1,4,256,256]{3,2,1,0:T(8,128)}, f32[512,1024]{1,0:T(8,128)}) custom-call(f32[512,1024]{1,0:T(8,128)S(1)} %copy-done.2, bf16[512,1024]{1,0:T(8,128)(2,1)S(1)} %get-tuple-element.189.g_ref, f32[2,1,4,512,512]{4,3,2,1,0:T(8,128)} %l_ref.6, f32[2,1,4,256,256]{4,3,2,1,0:T(8,128)S(1)} %copy-done.9), custom_call_target="tpu_custom_call" | custom-call | flops 1610612736 | bytes 23068672 | tf_op jit(solution)/shard_map/pallas_call | solution.py:1374
  729.7 8.1 %shard_map.330 = (f32[1024,512]{1,0:T(8,128)}, f32[4,1,256,256]{3,2,1,0:T(8,128)}, f32[4,1,512,512]{3,2,1,0:T(8,128)}, f32[1024,512]{1,0:T(8,128)}) custom-call(f32[1024,512]{1,0:T(8,128)S(1)} %copy-done.4, bf16[512,1024]{1,0:T(8,128)(2,1)S(1)} %get-tuple-element.188.g_ref, f32[2,4,1,256,256]{4,3,2,1,0:T(8,128)S(1)} %copy-done.10, f32[2,4,1,512,512]{4,3,2,1,0:T(8,128)} %r_ref.7), custom_call_target="tpu_custom_call" | custom-call | flops 1610612736 | bytes 23068672 | tf_op jit(solution)/shard_map/pallas_call | solution.py:1374
  737.8 1.0 multiply_reduce_fusion.1
  738.8 0.7 multiply_subtract_fusion
  739.5 0.9 copy-done.14
  740.4 6.1 shard_map.328
  746.6 1.3 copy.62
  (66 shorter events, 0.3 us)
Async XLA Ops:
  7.2 3.0 copy-start.3
  7.2 239.2 %all-gather.3.cloned.1.call-start = ((), (), s32[]{:S(2)}) async-start(), calls=%async_computation.4 | async-start | bytes 5242880 | tf_op jit(solution)/shard_map/all_gather | solution.py:1446
  10.1 236.3 %all-gather.5.cloned.1.call-start = ((), (), s32[]{:S(2)}) async-start(), calls=%async_computation.5 | async-start | bytes 5242880 | tf_op jit(solution)/shard_map/all_gather | solution.py:1447
  11.3 4.9 copy-start.6
  11.3 559.1 %reduce-scatter.13.cloned.1.call-start = ((), (), s32[]{:S(2)}) async-start(), calls=%async_computation.8 | async-start | bytes 10485760
  12.1 4.2 copy-start
  14.8 4.5 slice-start
  109.4 1.7 copy-start.22
  111.1 121.9 %copy-start.18 = (bf16[2048,256]{1,0:T(8,128)(2,1)}, bf16[2048,256]{1,0:T(8,128)(2,1)S(1)}, u32[]{:S(2)}) copy-start(bf16[2048,256]{1,0:T(8,128)(2,1)S(1)} %get-tuple-element.70.q_ref) | copy-start | bytes 3145732
  111.1 121.9 %copy-start.19 = (bf16[2048,256]{1,0:T(8,128)(2,1)}, bf16[2048,256]{1,0:T(8,128)(2,1)S(1)}, u32[]{:S(2)}) copy-start(bf16[2048,256]{1,0:T(8,128)(2,1)S(1)} %get-tuple-element.71.k_ref) | copy-start | bytes 3145732
  111.1 121.9 %copy-start.20 = (bf16[2048,256]{1,0:T(8,128)(2,1)}, bf16[2048,256]{1,0:T(8,128)(2,1)S(1)}, u32[]{:S(2)}) copy-start(bf16[2048,256]{1,0:T(8,128)(2,1)S(1)} %get-tuple-element.72.v_ref) | copy-start | bytes 3145732
  111.1 123.6 %copy-start.15 = (f32[2,2048]{1,0:T(2,128)S(1)}, f32[2,2048]{1,0:T(2,128)}, u32[]{:S(2)}) copy-start(f32[2,2048]{1,0:T(2,128)} %gain.5) | copy-start | bytes 49156
  233.0 1.0 copy-start.21
  234.0 0.7 copy-start.23
  234.7 9.4 %copy-start.12 = (bf16[8,256,256]{2,1,0:T(8,128)(2,1)}, bf16[8,256,256]{2,1,0:T(8,128)(2,1)S(1)}, u32[]{:S(2)}) copy-start(bf16[8,256,256]{2,1,0:T(8,128)(2,1)S(1)} %get-tuple-element.73.ctx) | copy-start | bytes 3145732
  234.7 3.8 copy-start.1
  244.1 1.3 copy-start.7
  245.4 1.0 copy-start.17
  428.5 248.6 %reduce-scatter.9.cloned.1.call-start = ((), (), s32[]{:S(2)}) async-start(), calls=%async_computation.6 | async-start | bytes 3932160 | tf_op jit(solution)/shard_map/reduce_scatter | solution.py:1477
  581.8 1.6 copy-start.8
  581.9 97.6 %reduce-scatter.15.cloned.1.call-start = ((), (), s32[]{:S(2)}) async-start(), calls=%async_computation.9 | async-start | bytes 5242880
  582.5 157.0 %reduce-scatter.11.cloned.1.call-start = ((), (), s32[]{:S(2)}) async-start(), calls=%async_computation.7 | async-start | bytes 1310720 | tf_op jit(solution)/shard_map/reduce_scatter | solution.py:1494
  585.3 1.0 copy-start.24
  587.3 92.8 %copy-start.28 = (f32[1,2048]{1,0:T(1,128)S(1)}, f32[1,2048]{1,0:T(1,128)}, u32[]{:S(2)}) copy-start(f32[1,2048]{1,0:T(1,128)} %get-tuple-element.99) | copy-start | bytes 24580
  680.1 30.5 %copy-start.5 = (f32[512,768]{1,0:T(8,128)S(1)}, f32[512,768]{1,0:T(8,128)}, u32[]{:S(2)}) copy-start(f32[512,768]{1,0:T(8,128)} %w_ref.4) | copy-start | bytes 4718596
  710.6 1.4 copy-start.11
  712.0 6.8 copy-start.25
  718.9 1.6 copy-start.2
  718.9 2.2 copy-start.9
  721.1 8.5 %copy-start.4 = (f32[1024,512]{1,0:T(8,128)S(1)}, f32[1024,512]{1,0:T(8,128)}, u32[]{:S(2)}) copy-start(f32[1024,512]{1,0:T(8,128)} %w_ref.7) | copy-start | bytes 6291460
  721.1 8.5 %copy-start.10 = (f32[2,4,1,256,256]{4,3,2,1,0:T(8,128)S(1)}, f32[2,4,1,256,256]{4,3,2,1,0:T(8,128)}, u32[]{:S(2)}) copy-start(f32[2,4,1,256,256]{4,3,2,1,0:T(8,128)} %l_ref.7) | copy-start | bytes 6291460
  729.6 9.1 %copy-start.16 = (f32[2,2048]{1,0:T(2,128)S(1)}, f32[2,2048]{1,0:T(2,128)}, u32[]{:S(2)}) copy-start(f32[2,2048]{1,0:T(2,128)} %gain.5) | copy-start | bytes 49156
  729.7 9.8 %copy-start.13 = (f32[2,1,4,64,64]{4,3,2,1,0:T(8,128)S(1)}, f32[2,1,4,64,64]{4,3,2,1,0:T(8,128)}, u32[]{:S(2)}) copy-start(f32[2,1,4,64,64]{4,3,2,1,0:T(8,128)} %r_ref.5) | copy-start | bytes 393220
  738.8 7.8 %copy-start.27 = (f32[2,2048]{1,0:T(2,128)}, f32[2,2048]{1,0:T(2,128)S(1)}, u32[]{:S(2)}) copy-start(f32[2,2048]{1,0:T(2,128)S(1)} %get-tuple-element.214) | copy-start | bytes 49156
  739.5 1.0 copy-start.14
  740.4 6.1 copy-start.26
Sparse Core Ops, SparseCore 0:
  10.5 82.0 all-gather.2
  95.0 52.5 all-gather.4
  428.6 100.2 reduce-scatter.12
  582.0 41.6 reduce-scatter.8
  626.7 52.6 reduce-scatter.14
  702.6 29.2 reduce-scatter.10

commit v4 on v3

--- a/solution.py
+++ b/solution.py
@@ -188,34 +188,45 @@
             sends,
             sem,
         )
-
-    def copy(self, src, block, way, k):
+        self.pieces = recv.shape[1]
+
+    def copy(self, src, block, way, k, piece):
         line = self.line
         device = (line.right, line.left, line.twin)[way]
+        size = self.own.shape[0] // self.pieces
+        at = pl.ds(piece * size, size)
         return remote(
-            src, self.full(block), self.sends.at[way, k], self.recv.at[block], device
+            src.at[at, :],
+            self.full(block).at[at, :],
+            self.sends.at[way, k, piece],
+            self.recv.at[block, piece],
+            device,
         )
 
     def start(self):
         line = self.line
-        mine = self.copy
-        pl.when(line.has_right)(lambda: mine(self.own, line.me, 0, 0).start())
-        pl.when(line.has_left)(lambda: mine(self.own, line.me, 1, 0).start())
-        mine(self.own, line.me, 2, line.chip).start()
+        for piece in range(self.pieces):
+            mine = lambda way, k: self.copy(self.own, line.me, way, k, piece).start()
+            pl.when(line.has_right)(lambda: mine(0, 0))
+            pl.when(line.has_left)(lambda: mine(1, 0))
+            mine(2, line.chip)
         self.mine = local(self.own, self.full(line.me), self.sem)
 
     def arrived(self, block):
-        self.copy(self.own, block, 2, 0).wait_recv()
+        for piece in range(self.pieces):
+            self.copy(self.own, block, 2, 0, piece).wait_recv()
 
     def forward(self, away, only=None):
         line = self.line
 
         def take(chip, way, onward):
             block = 2 * chip + line.core
-            self.arrived(block)
             got = self.full(block)
-            pl.when(onward)(lambda: self.copy(got, block, way, away).start())
-            self.copy(got, block, 2, chip).start()
+            for piece in range(self.pieces):
+                move = lambda to, k: self.copy(got, block, to, k, piece)
+                move(2, 0).wait_recv()
+                pl.when(onward)(lambda: move(way, away).start())
+                move(2, chip).start()
 
         from_left, from_right = line.chip >= away, line.chip + away < line.n
         if only is not None:
@@ -233,7 +244,10 @@
         line = self.line
 
         def sent(away, _):
-            wait = lambda way, k: self.copy(self.own, line.me, way, k).wait_send()
+            def wait(way, k):
+                for piece in range(self.pieces):
+                    self.copy(self.own, line.me, way, k, piece).wait_send()
+
             pl.when(line.has_right & (line.chip >= away))(lambda: wait(0, away))
             pl.when(line.has_left & (line.chip + away < line.n))(lambda: wait(1, away))
             wait(2, away)
@@ -242,8 +256,8 @@
         lax.fori_loop(0, line.n, sent, 0)
 
 
-def gather_sems(mp_count):
-    return [DMA((mp_count,)), DMA((3, mp_count // 2)), DMA(())]
+def gather_sems(mp_count, pieces=1):
+    return [DMA((mp_count, pieces)), DMA((3, mp_count // 2, pieces)), DMA(())]
 
 
 def qkv_kernel(
@@ -857,6 +871,12 @@
         self.last(out)
 
 
+class Pairs(Scatter):
+    def make(self, chip, both):
+        both(chip, self.both.at[chip], self.tmp)
+        self.add(chip, lambda at: self.tmp[at, :].astype(F32))
+
+
 def scatter_scratch(mp_count, rows, width):
     n = mp_count // 2
     return [
@@ -875,22 +895,36 @@
 
 
 def d_normed_kernel(
-    mp_count, dq, dk, dv, w, tokens, gain, d_resid, picked, out, d_gain, owned,
-    total, land, p_send, p_recv, *scratch
+    dp_count, mp_count, dq, dk, dv, w, tokens, gain, d_resid, picked, d_gain_two,
+    out, owned, stats,
+    total, land, p_send, p_recv, x, mid, by_mp, by_dp, m_send, m_recv, d_send, d_recv, *scratch
 ):
     line = Line(mp_count)
+    me, dp = line.me, lax.axis_index("dp")
     rows, width = out.shape
-    peers = others("mp", mp_count)
-    greet_all([on_mp(peer) for peer in peers])
+    peers, dp_peers = others("mp", mp_count), others("dp", dp_count)
+    greet_all([on_mp(peer) for peer in peers] + [on_dp(peer) for peer in dp_peers])
 
     def pick(device, source):
         return remote(
             picked.at[device], land.at[source], p_send.at[device], p_recv.at[source], on_mp(device)
         )
 
+    def over_mp(device, source):
+        return remote(x, by_mp.at[source], m_send.at[device], m_recv.at[source], on_mp(device))
+
+    def over_dp(device, source):
+        return remote(mid, by_dp.at[source], d_send.at[device], d_recv.at[source], on_dp(device))
+
+    def added(ref, count):
+        sum_of = ref[0]
+        for k in range(1, count):
+            sum_of = sum_of + ref[k]
+        return sum_of
+
     for peer in peers:
-        pick(peer, line.me).start()
-    land[line.me] = picked[line.me]
+        pick(peer, me).start()
+    land[me] = picked[me]
 
     def block_sum(block, ref):
         at = pl.ds(pl.multiple_of(block * rows, rows), rows)
@@ -900,70 +934,33 @@
             part += dg(dv[at, :], w[2, cols, :], NT)
             ref[:, cols] = part.astype(BF)
 
-    Scatter(line, *scratch).run(block_sum, total)
+    def summaries():
+        for peer in peers:
+            pick(peer, peer).wait_recv()
+        vectors = lax.fori_loop(
+            0, mp_count, lambda p, s: s + land[p].astype(F32), jnp.zeros(owned.shape, F32)
+        )
+        owned[...] = vectors
+        sums = jnp.sum(vectors, axis=0, keepdims=True)
+        each = owned.shape[1]
+        for p in range(mp_count):
+            x[2:3, p * each : (p + 1) * each] = jnp.where(me == p, sums, 0.0)
+        x[1:2, :] = d_gain_two[...]
+        squares = jnp.sum(jnp.sum(vectors * vectors, axis=0, keepdims=True), axis=1, keepdims=True)
+        x[3:4, :] = jnp.broadcast_to(squares, (1, width))
+
+    Scatter(line, *scratch).run(block_sum, total, summaries)
 
     def back(at, carry):
         d_value, d_g = norm_back(tokens[at, :].astype(F32), gain[0:1, :], total[at, :])
         out[at, :] = d_resid[at, :] + d_value
         return carry + d_g
 
-    d_gain[...] = row_chunks(rows, back, jnp.zeros((1, width), F32))
+    x[0:1, :] = row_chunks(rows, back, jnp.zeros((1, width), F32))
     for peer in peers:
-        pick(peer, peer).wait_recv()
-        pick(peer, line.me).wait_send()
-    owned[...] = lax.fori_loop(
-        0, mp_count, lambda p, s: s + land[p].astype(F32), jnp.zeros(owned.shape, F32)
-    )
-
-
-def input_back(dq, dk, dv, w, tokens, gain, d_resid, picked, mp_count, cid):
-    rows, width = tokens.shape
-    return pl.pallas_call(
-        functools.partial(d_normed_kernel, mp_count),
-        in_specs=[VM] * 8,
-        out_specs=[VM, VM, VM],
-        out_shape=[
-            jax.ShapeDtypeStruct((rows, width), F32),
-            jax.ShapeDtypeStruct((1, width), F32),
-            jax.ShapeDtypeStruct(picked.shape[1:], F32),
-        ],
-        scratch_shapes=[
-            pltpu.VMEM((rows, width), F32),
-            pltpu.VMEM(picked.shape, BF),
-            DMA((mp_count,)),
-            DMA((mp_count,)),
-            *scatter_scratch(mp_count, rows, width),
-        ],
-        compiler_params=pltpu.CompilerParams(
-            collective_id=cid, has_side_effects=True, vmem_limit_bytes=60 << 20
-        ),
-        cost_estimate=pl.CostEstimate(
-            flops=6 * dq.size * width, bytes_accessed=280 << 20, transcendentals=0
-        ),
-    )(dq, dk, dv, w, tokens, gain, d_resid, picked)
-
-
-def total_kernel(dp_count, mp_count, x, out, mid, by_mp, by_dp, m_send, m_recv, d_send, d_recv):
-    me, dp = lax.axis_index("mp"), lax.axis_index("dp")
-    mp_peers, dp_peers = others("mp", mp_count), others("dp", dp_count)
-    greet_all([on_mp(peer) for peer in mp_peers] + [on_dp(peer) for peer in dp_peers])
-
-    def over_mp(device, source):
-        return remote(x, by_mp.at[source], m_send.at[device], m_recv.at[source], on_mp(device))
-
-    def over_dp(device, source):
-        return remote(mid, by_dp.at[source], d_send.at[device], d_recv.at[source], on_dp(device))
-
-    def added(ref, count):
-        total = ref[0]
-        for k in range(1, count):
-            total = total + ref[k]
-        return total
-
-    for peer in mp_peers:
         over_mp(peer, me).start()
     by_mp[me] = x[...]
-    for peer in mp_peers:
+    for peer in peers:
         over_mp(peer, peer).wait_recv()
     mid[...] = added(by_mp, mp_count)
     for peer in dp_peers:
@@ -971,31 +968,49 @@
     by_dp[dp] = mid[...]
     for peer in dp_peers:
         over_dp(peer, peer).wait_recv()
-    out[...] = added(by_dp, dp_count)
-    for peer in mp_peers:
+    stats[...] = added(by_dp, dp_count)
+    for peer in peers:
+        pick(peer, me).wait_send()
         over_mp(peer, me).wait_send()
     for peer in dp_peers:
         over_dp(peer, dp).wait_send()
 
 
-def total_everywhere(x, dp_count, mp_count, cid):
+def input_back(
+    dq, dk, dv, w, tokens, gain, d_resid, picked, d_gain_two, dp_count, mp_count, cid
+):
+    rows, width = tokens.shape
     return pl.pallas_call(
-        functools.partial(total_kernel, dp_count, mp_count),
-        in_specs=[VM],
-        out_specs=VM,
-        out_shape=jax.ShapeDtypeStruct(x.shape, F32),
+        functools.partial(d_normed_kernel, dp_count, mp_count),
+        in_specs=[VM] * 9,
+        out_specs=[VM, VM, VM],
+        out_shape=[
+            jax.ShapeDtypeStruct((rows, width), F32),
+            jax.ShapeDtypeStruct(picked.shape[1:], F32),
+            jax.ShapeDtypeStruct((4, width), F32),
+        ],
         scratch_shapes=[
-            pltpu.VMEM(x.shape, F32),
-            pltpu.VMEM((mp_count, *x.shape), F32),
-            pltpu.VMEM((dp_count, *x.shape), F32),
+            pltpu.VMEM((rows, width), F32),
+            pltpu.VMEM(picked.shape, BF),
+            DMA((mp_count,)),
+            DMA((mp_count,)),
+            pltpu.VMEM((4, width), F32),
+            pltpu.VMEM((4, width), F32),
+            pltpu.VMEM((mp_count, 4, width), F32),
+            pltpu.VMEM((dp_count, 4, width), F32),
             DMA((mp_count,)),
             DMA((mp_count,)),
             DMA((dp_count,)),
             DMA((dp_count,)),
-        ],
-        compiler_params=pltpu.CompilerParams(collective_id=cid, has_side_effects=True),
-        cost_estimate=pl.CostEstimate(flops=0, bytes_accessed=36 << 20, transcendentals=0),
-    )(x)
+            *scatter_scratch(mp_count, rows, width),
+        ],
+        compiler_params=pltpu.CompilerParams(
+            collective_id=cid, has_side_effects=True, vmem_limit_bytes=60 << 20
+        ),
+        cost_estimate=pl.CostEstimate(
+            flops=6 * dq.size * width, bytes_accessed=300 << 20, transcendentals=0
+        ),
+    )(dq, dk, dv, w, tokens, gain, d_resid, picked, d_gain_two)
 
 
 def attend_bwd_kernel(
@@ -1006,17 +1021,20 @@
 ):
     line = Line(mp_count)
     flat = flat_step()
-    scatter = Scatter(line, *scratch)
-
-    def block_sum(block, ref):
-        local(part.at[block], ref, io_sem).wait()
+    scatter = Pairs(line, *scratch)
+
+    def both(chip, ref, other):
+        first = local(part.at[0, chip], ref, io_sem.at[0])
+        second = local(part.at[1, chip], other, io_sem.at[1])
+        first.wait()
+        second.wait()
 
     @pl.when(flat == 0)
     def _():
         line.greet()
         for away in range(line.n - 1, 0, -1):
-            scatter.produce(away, block_sum)
-        scatter.make(line.chip, block_sum)
+            scatter.produce(away, both)
+        scatter.make(line.chip, both)
 
     bwd_block(
         hp, bq, len_ref, q_ref, k_ref, v_ref, o_ref, do_ref, lse_ref,
@@ -1036,7 +1054,7 @@
 
 def attend_bwd(seg_len, q, k, v, o, do, lse, part, mp_count, cid, bq=512):
     total, hw = q.shape
-    _, rows, features = part.shape
+    _, _, rows, features = part.shape
     heads = hw // HD
     hp = 2 if heads % 2 == 0 else 1
     width, nb, segs, pairs = hp * HD, SLOT // bq, total // SLOT, heads // hp
@@ -1066,7 +1084,7 @@
         scratch_shapes=[
             pltpu.VMEM((SLOT, width), F32),
             pltpu.VMEM((SLOT, width), F32),
-            DMA(()),
+            DMA((2,)),
             *scatter_scratch(mp_count, rows, features),
         ],
         compiler_params=pltpu.CompilerParams(
@@ -1122,7 +1140,7 @@
     def onward(self, chip, slot, way, away, piece):
         line = self.line
         device = (line.right, line.left)[way]
-        at = slice(piece * self.size, (piece + 1) * self.size)
+        at = pl.ds(pl.multiple_of(piece * self.size, self.size), self.size)
         return remote(
             self.both.at[chip, at, :], self.slots.at[slot, at, :],
             self.sends.at[way, away, piece], self.slot_recv.at[slot, piece], device,
@@ -1131,29 +1149,33 @@
     def arrived(self, slot, piece):
         self.onward(0, slot, 0, 0, piece).wait_recv()
 
-    def pass_on(self, chip, way, away, fed):
+    def pass_on(self, chip, way, away, piece, fed):
         last = jnp.where(away == 1, self.line.n, chip) if way == 1 else chip
-        for piece in range(self.pieces):
-            if fed:
-                self.arrived(chip, piece)
-                self.add(chip, lambda at: self.slots[chip, at, :].astype(F32), piece)
-            self.onward(chip, last, way, away, piece).start()
+        if fed:
+            self.arrived(chip, piece)
+            self.add(chip, lambda at: self.slots[chip, at, :].astype(F32), piece)
+        self.onward(chip, last, way, away, piece).start()
 
     def pass_unfed(self, away):
         line = self.line
+
+        def all_pieces(chip, way):
+            for piece in range(self.pieces):
+                self.pass_on(chip, way, away, piece, False)
+
         right = (line.chip + away < line.n) & jnp.logical_not(line.has_left)
         left = (line.chip >= away) & jnp.logical_not(line.has_right)
-        pl.when(right)(lambda: self.pass_on(line.chip + away, 0, away, False))
-        pl.when(left)(lambda: self.pass_on(line.chip - away, 1, away, False))
-
-    def pass_fed(self, turn):
+        pl.when(right)(lambda: all_pieces(line.chip + away, 0))
+        pl.when(left)(lambda: all_pieces(line.chip - away, 1))
+
+    def pass_fed(self, turn, piece):
         line = self.line
         right = turn - 2 * line.chip
         left = turn - 2 * (line.n - 1 - line.chip)
         to_right = line.has_left & (right >= 1) & (line.chip + right < line.n)
         to_left = line.has_right & (left >= 1) & (line.chip >= left)
-        pl.when(to_right)(lambda: self.pass_on(line.chip + right, 0, right, True))
-        pl.when(to_left)(lambda: self.pass_on(line.chip - left, 1, left, True))
+        pl.when(to_right)(lambda: self.pass_on(line.chip + right, 0, right, piece, True))
+        pl.when(to_left)(lambda: self.pass_on(line.chip - left, 1, left, piece, True))
 
     def last(self, out):
         line = self.line
@@ -1184,7 +1206,7 @@
 
 def ffn_kernel(
     mp_count, own, u_all, up, down, out, x_all, part_out, kept, g_out,
-    x, u, hid, pre, part, tile, g_tile, io_sem, recv, sends, sem, *scratch
+    x, u, hid, pre, part, tile, g_tile, io_sem, p_send, p_recv, recv, sends, sem, *scratch
 ):
     line = Line(mp_count)
     line.greet()
@@ -1197,9 +1219,13 @@
     gather.start()
 
     def saved(block):
-        return pltpu.make_async_copy(part, part_out.at[block], io_sem.at[2])
-
-    def terms(block, ref, first=False):
+        return pltpu.make_async_copy(part.at[0], part_out.at[0, block // 2], io_sem.at[2])
+
+    def given(block):
+        chip = block // 2
+        return remote(part.at[1], part_out.at[1, chip], p_send, p_recv.at[chip], line.twin)
+
+    def terms(block, ref, side, done):
         at = pl.ds(pl.multiple_of(block * rows, rows), rows)
         one = local(x_all.at[block], x, io_sem.at[0])
         two = local(u_all.at[block], u, io_sem.at[1])
@@ -1216,23 +1242,29 @@
                 GELU_C * (1.0 + 3.0 * 0.044715 * square)
             )
             pre[at, cols] = (d_hidden * slope).astype(BF)
-        if not first:
-            saved(block).wait()
+        done()
         for cols in tiled(width):
             ref[:, cols] = dg(pre[at, :], up[cols, :], NT).astype(BF)
-            part[:, cols] = dg(hid[at, :], down[:, cols], NN).astype(BF)
+            part[side, :, cols] = dg(hid[at, :], down[:, cols], NN).astype(BF)
+
+    def nothing():
+        return None
+
+    def mine(block, first=False):
+        terms(block, scatter.tmp, 0, nothing if first else lambda: saved(block).wait())
         saved(block).start()
-
-    def mine(block, first=False):
-        terms(block, scatter.tmp, first)
         scatter.keep(block)
 
     def other(block, first=False):
         gather.arrived(block)
-        if not first:
+
+        def sent():
             scatter.across(0).wait_send()
-        terms(block, scatter.stage)
+            given(block).wait_send()
+
+        terms(block, scatter.stage, 1, nothing if first else sent)
         scatter.across(block // 2).start()
+        given(block).start()
 
     gather.mine.wait()
     mine(line.me, True)
@@ -1251,6 +1283,7 @@
     lax.fori_loop(1, line.n, step, 0)
     saved(0).wait()
     scatter.across(0).wait_send()
+    given(0).wait_send()
 
     def fetch(i, which):
         source = (x_all, u_all)[which]
@@ -1278,23 +1311,27 @@
 
     turns = 2 * line.n - 3
     early = tiles // 2
-    share = -(-early // max(turns - 3, 1))
+    first, second = max(turns - 3, 1) * PIECES, (turns - 2) * PIECES
     fetch(0, 0).start()
 
-    def turn(k, _):
-        scatter.pass_fed(k + 1)
-        lax.fori_loop(
-            jnp.minimum(k * share, early), jnp.minimum((k + 1) * share, early), weigh, 0
-        )
+    def done(slot):
+        before = lax.div(early * jnp.minimum(slot, first), first)
+        after = jnp.minimum(jnp.maximum(slot - second, 0), PIECES)
+        return before + lax.div((tiles - early) * after, PIECES)
+
+    def turn(slot, _):
+        scatter.pass_fed(lax.div(slot, PIECES) + 1, lax.rem(slot, PIECES))
+        lax.fori_loop(done(slot), done(slot + 1), weigh, 0)
         return 0
 
-    lax.fori_loop(0, turns, turn, 0)
-    lax.fori_loop(early, tiles, weigh, 0)
+    lax.fori_loop(0, turns * PIECES, turn, 0)
     store(0, 0).wait()
     store(0, 1).wait()
     scatter.join(line.chip)
     scatter.last(out)
     gather.finish()
+    for chip in range(mp_count // 2):
+        given(2 * chip).wait_recv()
 
 
 def ffn(own, u_all, up, down, dp_count, mp_count, cid):
@@ -1310,7 +1347,7 @@
         out_shape=[
             jax.ShapeDtypeStruct((rows, width), F32),
             jax.ShapeDtypeStruct((mp_count, rows, width), BF),
-            jax.ShapeDtypeStruct((mp_count, rows, width), BF),
+            jax.ShapeDtypeStruct((2, chips, rows, width), BF),
             jax.ShapeDtypeStruct((chips, rows, width), BF),
             jax.ShapeDtypeStruct((dp_count, 2, width // dp_count, units), BF),
         ],
@@ -1319,11 +1356,13 @@
             pltpu.VMEM((rows, width), BF),
             pltpu.VMEM((total, units), BF),
             pltpu.VMEM((total, units), BF),
-            pltpu.VMEM((rows, width), BF),
+            pltpu.VMEM((2, rows, width), BF),
             pltpu.VMEM((2, mp_count, rows, span), BF),
             pltpu.VMEM((2, span, units), BF),
             DMA((4,)),
-            *gather_sems(mp_count),
+            DMA(()),
+            DMA((chips,)),
+            *gather_sems(mp_count, 2),
             pltpu.VMEM((chips, rows, width), BF),
             pltpu.VMEM((chips + 1, rows, width), BF),
             pltpu.VMEM((rows, width), BF),
@@ -1484,11 +1523,22 @@
     selector = (slot_index[:, None] == positions[None, :]).astype(BF)
     picked = jnp.dot(selector, block_out, preferred_element_type=F32).astype(BF)
     picked = picked.reshape(padded, mp_count, features // mp_count).transpose(1, 0, 2)
-    input_grad, d_gain_one, owned_vectors = input_back(
-        d_queries, d_keys, d_values, qkv_full, tokens, ln_gain, d_resid, picked, mp_count, 7
-    )
-    d_gain_one, grad_ffn, grad_qkv, grad_out = lax.optimization_barrier(
-        (d_gain_one, grad_ffn, grad_qkv, grad_out)
+    input_grad, owned_vectors, stats = input_back(
+        d_queries,
+        d_keys,
+        d_values,
+        qkv_full,
+        tokens,
+        ln_gain,
+        d_resid,
+        picked,
+        d_gain_two,
+        dp_count,
+        mp_count,
+        7,
+    )
+    stats, grad_ffn, grad_qkv, grad_out = lax.optimization_barrier(
+        (stats, grad_ffn, grad_qkv, grad_out)
     )
     grad_up, grad_down = grad_ffn[0], grad_ffn[1]
     grad_out = lax.psum_scatter(
@@ -1501,13 +1551,6 @@
     )
     owned_vectors = owned_vectors[:picks].reshape(seg_count, NSUM, features // mp_count)
     owned_width = owned_vectors.shape[2]
-    col_sums = jnp.sum(owned_vectors, axis=(0, 1))
-    spread_sums = (
-        (jnp.arange(mp_count) == mp_index).astype(F32)[:, None] * col_sums[None, :]
-    ).reshape(1, features)
-    squares = jnp.full((1, features), jnp.sum(owned_vectors * owned_vectors))
-    stats = jnp.concatenate([d_gain_one, d_gain_two, spread_sums, squares] * 2)
-    stats = total_everywhere(stats, dp_count, mp_count, 8)
     gain_grads, total_cols, total_squares = stats[:2], stats[2], stats[3, 0]
     vector_count = seg_count * dp_count * NSUM
     centre_all = total_cols / vector_count

time: 760 us -> 726 us (0.955)
  Pallas kernels: 675 us -> 649 us
    pallas_call x2 -> x1, Pallas kernels: 108 us -> 95.7 us  [input_back(): pl.pallas_call(functools.partial(d_normed_kernel, dp_count, mp_count), in...]
    pallas_call x1, Pallas kernels: 95.5 us -> 87.5 us  [attend_bwd(): pl.pallas_call(functools.partial(attend_bwd_kernel, hp, bq, segs * pairs...]
    unnamed x62 -> x61, local copies, waits for them, and re-layouts: 19.5 us -> 19.5 us
  transfers between devices with their start and end apart: 6 -> 6, of which waited for: 1 -> 0; matrix products, arithmetic and copies ran while one was open for 3% -> 3% of each run, Pallas kernels for 62% -> 64%
where the time goes in v4:
time: 726 us; the launch traced here: 722 us
  Pallas kernels  649 us (89%)
  local copies, waits for them, and re-layouts  28 us (4%)
  between operations  16.8 us (2%)
  other arithmetic  15.4 us (2%)
  matrix products  11.7 us (2%)
    pallas_call x1, Pallas kernels, ffn(): pl.pallas_call(functools.partial(ffn_kernel, mp_count), in_specs=[HBM, HB...  182 us
    pallas_call x1, Pallas kernels, attend_fwd(): pl.pallas_call(functools.partial(attend_fwd_kernel, hp, bq, segs * pairs...  122 us
    pallas_call x1, Pallas kernels, input_back(): pl.pallas_call(functools.partial(d_normed_kernel, dp_count, mp_count), in...  95.7 us
    pallas_call x1, Pallas kernels, gather_qkv(): pl.pallas_call(functools.partial(qkv_kernel, dp_count, mp_count), in_spec...  89.7 us
    pallas_call x1, Pallas kernels, attend_bwd(): pl.pallas_call(functools.partial(attend_bwd_kernel, hp, bq, segs * pairs...  87.5 us
    pallas_call x1, Pallas kernels, resid_back(): pl.pallas_call(functools.partial(resid_back_kernel, dp_count, mp_count),...  36.4 us
    pallas_call x4, Pallas kernels, shampoo(): pl.pallas_call(functools.partial(shampoo_kernel, group, tc, flipped), gri...  29.6 us
    unnamed x61, local copies, waits for them, and re-layouts  19.5 us
  transfers between devices with their start and end apart: 6, of which 0 were waited for; matrix products, arithmetic and copies ran while one was open for 3% of the time, Pallas kernels for 64%

profile of v4, /device:TPU:0, one launch (start us, length us, event | category | flops | bytes accessed | tf_op | source)
XLA Modules:
  0.0 721.5 jit_solution(9587792570885142013)
XLA Ops:
  7.2 0.0 all-gather.3.cloned.1.call-start
  7.2 2.9 convert_element_type.32
  10.1 0.0 all-gather.3.cloned.1.call-update
  10.1 0.0 all-gather.5.cloned.1.call-start
  10.2 1.1 convert_element_type.33
  11.3 0.0 all-gather.5.cloned.1.call-update
  11.3 0.0 reduce-scatter.13.cloned.1.call-start
  12.1 0.0 copy-start
  12.1 1.8 copy.48
  13.9 1.0 copy.49
  14.8 1.4 copy.50.w_own
  16.3 0.2 convert_reduce_fusion
  16.6 0.4 fusion.2
  17.0 2.3 broadcast_select_fusion.up_own
  19.3 0.4 fusion.4.own
  19.7 89.7 %shard_map.319 = (bf16[8,256,2048]{2,1,0:T(8,128)(2,1)}, bf16[2048,256]{1,0:T(8,128)(2,1)S(1)}, bf16[2048,256]{1,0:T(8,128)(2,1)S(1)}, bf16[2048,256]{1,0:T(8,128)(2,1)S(1)}, bf16[3,2048,256]{2,1,0:T(8,128)(2,1)S(1)}) custom-call(bf16[256,2048]{1,0:T(8,128)(2,1)S(1)} %fusion.4.own, bf16[3,512,256]{2,1,0:T(8,128)(2,1)S(1)} %copy.50.w_own), custom_call_target="tpu_custom_call" | custom-call | flops 6442450944 | bytes 293601280 | tf_op jit(solution)/shard_map/pallas_call | solution.py:332
  109.4 0.0 copy-start.22
  109.5 1.7 copy-done.22
  111.1 121.8 %shard_map.320 = (bf16[2048,256]{1,0:T(8,128)(2,1)S(1)}, f32[1,4,8,2048]{3,2,1,0:T(8,128)S(1)}, bf16[8,256,256]{2,1,0:T(8,128)(2,1)S(1)}, bf16[8,256,2048]{2,1,0:T(8,128)(2,1)}, bf16[2,4,2048,256]{3,2,1,0:T(8,128)(2,1)}) custom-call(s32[1]{0:T(128)} %copy.60.len_ref, bf16[2048,256]{1,0:T(8,128)(2,1)S(1)} %get-tuple-element.70.q_ref, ...), custom_call_target="tpu_custom_call" | custom-call | flops 2147483648 | bytes 398458880 | tf_op jit(solution)/shard_map/pallas_call | solution.py:507
  233.0 1.0 copy-done.21
  234.0 0.7 copy-done.23
  234.7 3.8 copy-done.1
  238.4 5.6 shard_map.321
  244.1 1.3 copy-done.7
  245.4 1.0 copy-done.17
  246.4 182.4 %shard_map.322 = (f32[256,2048]{1,0:T(8,128)}, bf16[8,256,2048]{2,1,0:T(8,128)(2,1)}, bf16[2,4,256,2048]{3,2,1,0:T(8,128)(2,1)}, bf16[4,256,2048]{2,1,0:T(8,128)(2,1)}, bf16[4,2,512,1024]{3,2,1,0:T(8,128)(2,1)}) custom-call(bf16[256,2048]{1,0:T(8,128)(2,1)} %copy-done.17, bf16[8,256,2048]{2,1,0:T(8,128)(2,1)} %get-tuple-element.78.u_all, ...), custom_call_target="tpu_custom_call" | custom-call | flops 51539607552 | bytes 555745280 | tf_op jit(solution)/shard_map/pallas_call | solution.py:1343
  428.8 0.0 reduce-scatter.13.cloned.1.call-update
  428.9 0.0 reduce-scatter.9.cloned.1.call-start
  428.9 36.4 %shard_map.323 = (f32[256,2048]{1,0:T(8,128)}, f32[1,2048]{1,0:T(1,128)}, bf16[8,256,256]{2,1,0:T(8,128)(2,1)}, bf16[4,4,512,256]{3,2,1,0:T(8,128)(2,1)}) custom-call(f32[256,2048]{1,0:T(8,128)} %get-tuple-element.79.dn, f32[256,2048]{1,0:T(8,128)} %copy-done.7, bf16[256,2048]{1,0:T(8,128)(2,1)} %broadcast_select_fusion.up_own, f32[2,2048]{1,0:T(2,128)} %gain.5, ...), custom_call_target="tpu_custom_call" | custom-call | flops 4294967296 | bytes 115343360 | tf_op jit(solution)/shard_map/pallas_call | solution.py:730
  465.3 87.5 %shard_map.324 = (bf16[2048,256]{1,0:T(8,128)(2,1)}, bf16[2048,256]{1,0:T(8,128)(2,1)}, bf16[2048,256]{1,0:T(8,128)(2,1)}, f32[256,2048]{1,0:T(8,128)}) custom-call(s32[1]{0:T(128)} %copy.60.len_ref, bf16[2048,256]{1,0:T(8,128)(2,1)} %copy-done.18, bf16[2048,256]{1,0:T(8,128)(2,1)} %copy-done.19, bf16[2048,256]{1,0:T(8,128)(2,1)} %copy-done.20, ...), custom_call_target="tpu_custom_call" | custom-call | flops 5368709120 | bytes 304087040 | tf_op jit(solution)/shard_map/pallas_call | solution.py:1064
  552.8 3.1 pad_maximum_fusion
  556.0 11.4 %convolution_convert_fusion = bf16[2048,768]{1,0:T(8,128)(2,1)} fusion(bf16[2048,2048]{1,0:T(8,128)(2,1)} %bitcast.47, bf16[2048,768]{1,0:T(8,128)(2,1)} %pad_maximum_fusion), kind=kOutput, calls=%fused_computation | convolution fusion | flops 6444023808 | bytes 14680064 | tf_op jit(solution)/shard_map/gd,gc->dc/dot_general | solution.py:1515
  567.3 0.0 reduce-scatter.9.cloned.1.call-update
  567.4 0.0 reduce-scatter.15.cloned.1.call-start
  567.4 0.5 reduce-scatter.15.cloned.1.call-update
  567.9 0.0 reduce-scatter.11.cloned.1.call-start
  568.0 0.9 copy-done.8
  568.9 1.8 add_convert_fusion
  570.8 1.0 copy-done.24
  571.7 0.3 convolution_convert_fusion.1
  572.1 0.7 copy.58
  572.8 95.7 %shard_map.325 = (f32[256,2048]{1,0:T(8,128)}, f32[64,256]{1,0:T(8,128)}, f32[4,2048]{1,0:T(4,128)}) custom-call(bf16[2048,256]{1,0:T(8,128)(2,1)} %get-tuple-element.84.dq, bf16[2048,256]{1,0:T(8,128)(2,1)} %get-tuple-element.85.dk, bf16[2048,256]{1,0:T(8,128)(2,1)} %get-tuple-element.86.dv, bf16[3,2048,256]{2,1,0:T(8,128)(2,1)} %copy-done.22, ...), custom_call_target="tpu_custom_call" | custom-call | flops 6442450944 | bytes 314572800 | tf_op jit(solution)/shard_map/pallas_call | solution.py:983
  668.5 0.0 reduce-scatter.9.cloned.1.call-done
  668.6 0.0 reduce-scatter.15.cloned.1.call-done
  668.6 1.3 slice.24
  669.9 0.0 reduce-scatter.11.cloned.1.call-update
  670.6 1.4 multiply_reduce_fusion.1
  672.7 0.8 multiply_bitcast_fusion
  673.5 0.7 copy.55
  674.2 1.4 copy.52
  675.6 1.0 copy.53
  676.5 1.5 copy.54.g_ref
  678.1 1.4 copy-done.11
  679.5 6.8 shard_map.326
  686.3 0.2 slice_bitcast_fusion
  686.5 1.4 copy-done.2
  687.9 0.7 copy-done.9
  688.6 8.5 %shard_map.328 = (f32[512,1024]{1,0:T(8,128)}, f32[1,4,512,512]{3,2,1,0:T(8,128)}, f32[1,4,256,256]{3,2,1,0:T(8,128)}, f32[512,1024]{1,0:T(8,128)}) custom-call(f32[512,1024]{1,0:T(8,128)S(1)} %copy-done.2, bf16[512,1024]{1,0:T(8,128)(2,1)S(1)} %get-tuple-element.187.g_ref, f32[2,1,4,512,512]{4,3,2,1,0:T(8,128)} %l_ref.6, f32[2,1,4,256,256]{4,3,2,1,0:T(8,128)S(1)} %copy-done.9), custom_call_target="tpu_custom_call" | custom-call | flops 1610612736 | bytes 23068672 | tf_op jit(solution)/shard_map/pallas_call | solution.py:1413
  697.1 8.1 %shard_map.329 = (f32[1024,512]{1,0:T(8,128)}, f32[4,1,256,256]{3,2,1,0:T(8,128)}, f32[4,1,512,512]{3,2,1,0:T(8,128)}, f32[1024,512]{1,0:T(8,128)}) custom-call(f32[1024,512]{1,0:T(8,128)S(1)} %copy-done.4, bf16[512,1024]{1,0:T(8,128)(2,1)S(1)} %get-tuple-element.186.g_ref, f32[2,4,1,256,256]{4,3,2,1,0:T(8,128)S(1)} %copy-done.10, f32[2,4,1,512,512]{4,3,2,1,0:T(8,128)} %r_ref.7), custom_call_target="tpu_custom_call" | custom-call | flops 1610612736 | bytes 23068672 | tf_op jit(solution)/shard_map/pallas_call | solution.py:1413
  705.2 0.1 multiply_reduce_fusion
  705.4 0.7 multiply_subtract_fusion
  706.1 0.9 copy-done.14
  707.0 6.1 shard_map.327
  713.2 1.3 copy.61
  (59 shorter events, 0.2 us)
Async XLA Ops:
  7.2 3.0 copy-start.3
  7.2 239.2 %all-gather.3.cloned.1.call-start = ((), (), s32[]{:S(2)}) async-start(), calls=%async_computation.4 | async-start | bytes 5242880 | tf_op jit(solution)/shard_map/all_gather | solution.py:1485
  10.1 236.3 %all-gather.5.cloned.1.call-start = ((), (), s32[]{:S(2)}) async-start(), calls=%async_computation.5 | async-start | bytes 5242880 | tf_op jit(solution)/shard_map/all_gather | solution.py:1486
  11.3 4.9 copy-start.6
  11.3 544.6 %reduce-scatter.13.cloned.1.call-start = ((), (), s32[]{:S(2)}) async-start(), calls=%async_computation.8 | async-start | bytes 10485760
  12.1 4.2 copy-start
  14.8 4.5 slice-start
  109.4 1.7 copy-start.22
  111.1 121.9 %copy-start.18 = (bf16[2048,256]{1,0:T(8,128)(2,1)}, bf16[2048,256]{1,0:T(8,128)(2,1)S(1)}, u32[]{:S(2)}) copy-start(bf16[2048,256]{1,0:T(8,128)(2,1)S(1)} %get-tuple-element.70.q_ref) | copy-start | bytes 3145732
  111.1 121.9 %copy-start.19 = (bf16[2048,256]{1,0:T(8,128)(2,1)}, bf16[2048,256]{1,0:T(8,128)(2,1)S(1)}, u32[]{:S(2)}) copy-start(bf16[2048,256]{1,0:T(8,128)(2,1)S(1)} %get-tuple-element.71.k_ref) | copy-start | bytes 3145732
  111.1 121.9 %copy-start.20 = (bf16[2048,256]{1,0:T(8,128)(2,1)}, bf16[2048,256]{1,0:T(8,128)(2,1)S(1)}, u32[]{:S(2)}) copy-start(bf16[2048,256]{1,0:T(8,128)(2,1)S(1)} %get-tuple-element.72.v_ref) | copy-start | bytes 3145732
  111.1 123.6 %copy-start.15 = (f32[2,2048]{1,0:T(2,128)S(1)}, f32[2,2048]{1,0:T(2,128)}, u32[]{:S(2)}) copy-start(f32[2,2048]{1,0:T(2,128)} %gain.5) | copy-start | bytes 49156
  233.0 1.0 copy-start.21
  234.0 0.7 copy-start.23
  234.7 9.4 %copy-start.12 = (bf16[8,256,256]{2,1,0:T(8,128)(2,1)}, bf16[8,256,256]{2,1,0:T(8,128)(2,1)S(1)}, u32[]{:S(2)}) copy-start(bf16[8,256,256]{2,1,0:T(8,128)(2,1)S(1)} %get-tuple-element.73.ctx) | copy-start | bytes 3145732
  234.7 3.8 copy-start.1
  244.1 1.3 copy-start.7
  245.4 1.0 copy-start.17
  428.9 239.7 %reduce-scatter.9.cloned.1.call-start = ((), (), s32[]{:S(2)}) async-start(), calls=%async_computation.6 | async-start | bytes 3932160 | tf_op jit(solution)/shard_map/reduce_scatter | solution.py:1516
  567.3 1.6 copy-start.8
  567.4 101.2 %reduce-scatter.15.cloned.1.call-start = ((), (), s32[]{:S(2)}) async-start(), calls=%async_computation.9 | async-start | bytes 5242880
  567.9 138.1 %reduce-scatter.11.cloned.1.call-start = ((), (), s32[]{:S(2)}) async-start(), calls=%async_computation.7 | async-start | bytes 1310720 | tf_op jit(solution)/shard_map/reduce_scatter | solution.py:1544
  570.8 1.0 copy-start.24
  668.5 9.5 %copy-start.5 = (f32[512,768]{1,0:T(8,128)S(1)}, f32[512,768]{1,0:T(8,128)}, u32[]{:S(2)}) copy-start(f32[512,768]{1,0:T(8,128)} %w_ref.4) | copy-start | bytes 4718596
  678.1 1.4 copy-start.11
  679.5 6.8 copy-start.25
  686.3 1.6 copy-start.2
  686.3 2.2 copy-start.9
  688.6 8.5 %copy-start.4 = (f32[1024,512]{1,0:T(8,128)S(1)}, f32[1024,512]{1,0:T(8,128)}, u32[]{:S(2)}) copy-start(f32[1024,512]{1,0:T(8,128)} %w_ref.7) | copy-start | bytes 6291460
  688.6 8.5 %copy-start.10 = (f32[2,4,1,256,256]{4,3,2,1,0:T(8,128)S(1)}, f32[2,4,1,256,256]{4,3,2,1,0:T(8,128)}, u32[]{:S(2)}) copy-start(f32[2,4,1,256,256]{4,3,2,1,0:T(8,128)} %l_ref.7) | copy-start | bytes 6291460
  697.1 8.1 %copy-start.28 = (f32[4,2048]{1,0:T(4,128)S(1)}, f32[4,2048]{1,0:T(4,128)}, u32[]{:S(2)}) copy-start(f32[4,2048]{1,0:T(4,128)} %get-tuple-element.99) | copy-start | bytes 98308
  697.1 8.3 %copy-start.16 = (f32[2,2048]{1,0:T(2,128)S(1)}, f32[2,2048]{1,0:T(2,128)}, u32[]{:S(2)}) copy-start(f32[2,2048]{1,0:T(2,128)} %gain.5) | copy-start | bytes 49156
  697.1 9.0 %copy-start.13 = (f32[2,1,4,64,64]{4,3,2,1,0:T(8,128)S(1)}, f32[2,1,4,64,64]{4,3,2,1,0:T(8,128)}, u32[]{:S(2)}) copy-start(f32[2,1,4,64,64]{4,3,2,1,0:T(8,128)} %r_ref.5) | copy-start | bytes 393220
  705.4 7.8 %copy-start.27 = (f32[2,2048]{1,0:T(2,128)}, f32[2,2048]{1,0:T(2,128)S(1)}, u32[]{:S(2)}) copy-start(f32[2,2048]{1,0:T(2,128)S(1)} %get-tuple-element.212) | copy-start | bytes 49156
  706.1 1.0 copy-start.14
  707.0 6.1 copy-start.26
Sparse Core Ops, SparseCore 0:
  10.5 82.0 all-gather.2
  95.0 52.5 all-gather.4
  429.0 93.5 reduce-scatter.12
  567.5 41.0 reduce-scatter.8
  611.7 52.6 reduce-scatter.14
  670.0 28.4 reduce-scatter.10

commit v5 on v4

--- a/solution.py
+++ b/solution.py
@@ -830,7 +830,7 @@
         pl.when(line.chip + away < line.n)(lambda: self.make(line.chip + away, block_sum))
         pl.when(line.chip >= away)(lambda: self.make(line.chip - away, block_sum))
 
-    def last(self, out):
+    def last(self, out, far=None):
         line = self.line
 
         def join():
@@ -848,7 +848,7 @@
             pl.when(line.chip >= away)(lambda: wait(1))
             return 0
 
-        lax.fori_loop(1, line.n, sent, 0)
+        lax.fori_loop(1, far or line.n, sent, 0)
 
     def produce(self, away, block_sum):
         self.each(away, block_sum)
@@ -1015,13 +1015,19 @@
 
 def attend_bwd_kernel(
     hp, bq, steps, mp_count,
-    len_ref, q_ref, k_ref, v_ref, o_ref, do_ref, lse_ref, part,
-    dq_ref, dk_ref, dv_ref, out,
-    dka, dva, io_sem, *scratch
+    len_ref, q_ref, k_ref, v_ref, o_ref, do_ref, lse_ref, part, far_in, x_all,
+    dq_ref, dk_ref, dv_ref, out, g_out,
+    dka, dva, d_all, tile, g_tile, io_sem, w_sem, *scratch
 ):
     line = Line(mp_count)
     flat = flat_step()
     scatter = Pairs(line, *scratch)
+    far = line.n - 1
+    rows, features = out.shape
+    width = q_ref.shape[1]
+    span = tile.shape[3]
+    per = g_out.shape[2] // span
+    tiles = features // span
 
     def both(chip, ref, other):
         first = local(part.at[0, chip], ref, io_sem.at[0])
@@ -1029,19 +1035,56 @@
         first.wait()
         second.wait()
 
+    def from_far(chip, way):
+        local(far_in.at[way], scatter.slots.at[chip], io_sem.at[0]).wait()
+        scatter.add(chip, lambda at: scatter.slots[chip, at, :].astype(F32))
+        slot = line.n if way == 1 and far == 2 else chip
+        scatter.onward(chip, slot, way, far - 1).start()
+
+    def fetch(i):
+        at = pl.ds(pl.multiple_of(i * span, span), span)
+        slot = lax.rem(i, 2)
+        return pltpu.make_async_copy(x_all.at[:, :, at], tile.at[slot], w_sem.at[slot])
+
+    def store(i):
+        at = pl.ds(pl.multiple_of(lax.rem(i, per) * span, span), span)
+        return pltpu.make_async_copy(g_tile, g_out.at[lax.div(i, per), :, at, :], w_sem.at[2])
+
     @pl.when(flat == 0)
     def _():
         line.greet()
-        for away in range(line.n - 1, 0, -1):
+        for away in range(far - 1, 0, -1):
             scatter.produce(away, both)
+            if away == far - 1:
+                pl.when(line.chip == 1)(lambda: from_far(far, 0))
+                pl.when(line.chip == far - 1)(lambda: from_far(0, 1))
         scatter.make(line.chip, both)
+
+    @pl.when(flat == steps - 1)
+    def _():
+        fetch(0).start()
 
     bwd_block(
         hp, bq, len_ref, q_ref, k_ref, v_ref, o_ref, do_ref, lse_ref,
         dq_ref, dk_ref, dv_ref, dka, dva,
     )
-    for away in range(line.n - 2, 0, -1):
-        turn = min(steps - 1, (line.n - 1 - away) * steps // (line.n - 2))
+    pair = pl.program_id(1)
+    if width == d_all.shape[2]:
+        lanes = slice(None)
+    else:
+        lanes = pl.ds(pl.multiple_of(pair * width, width), width)
+    segment = pl.program_id(0) * SLOT
+    at = pl.ds(pl.multiple_of(segment + pl.program_id(2) * bq, bq), bq)
+    d_all[0, at, lanes] = dq_ref[...]
+
+    @pl.when(pl.program_id(2) == pl.num_programs(2) - 1)
+    def _():
+        every = pl.ds(pl.multiple_of(segment, SLOT), SLOT)
+        d_all[1, every, lanes] = dk_ref[...]
+        d_all[2, every, lanes] = dv_ref[...]
+
+    for away in range(far - 2, 0, -1):
+        turn = min(steps - 1, (far - 1 - away) * steps // (far - 1))
 
         @pl.when(flat == turn)
         def _(away=away):
@@ -1049,15 +1092,30 @@
 
     @pl.when(flat == steps - 1)
     def _():
-        scatter.last(out)
-
-
-def attend_bwd(seg_len, q, k, v, o, do, lse, part, mp_count, cid, bq=512):
+        def weigh(i, _):
+            pl.when(i + 1 < tiles)(lambda: fetch(i + 1).start())
+            fetch(i).wait()
+            value = tile[lax.rem(i, 2)].reshape(mp_count * rows, span)
+            pl.when(i > 0)(lambda: store(0).wait())
+            for j in range(3):
+                g_tile[j] = dg(value, d_all[j], TN).astype(BF)
+            store(i).start()
+            return 0
+
+        lax.fori_loop(0, tiles, weigh, 0)
+        store(0).wait()
+        scatter.last(out, far)
+
+
+def attend_bwd(
+    seg_len, q, k, v, o, do, lse, part, far_in, x_all, dp_count, mp_count, cid, bq=512
+):
     total, hw = q.shape
     _, _, rows, features = part.shape
     heads = hw // HD
     hp = 2 if heads % 2 == 0 else 1
     width, nb, segs, pairs = hp * HD, SLOT // bq, total // SLOT, heads // hp
+    span = 256 if mp_count <= 8 else 128
     blk = pl.BlockSpec((bq, width), lambda s, p, i: (s * nb + i, p))
     full = pl.BlockSpec((SLOT, width), lambda s, p, i: (s, p))
     sh = jax.ShapeDtypeStruct((total, hw), BF)
@@ -1073,29 +1131,42 @@
             blk,
             pl.BlockSpec((1, hp, 8, bq), lambda s, p, i: (s, p, 0, i)),
             HBM,
+            HBM,
+            HBM,
         ],
         out_specs=[
             blk,
             full,
             full,
             pl.BlockSpec((rows, features), lambda s, p, i: (0, 0)),
-        ],
-        out_shape=[sh, sh, sh, jax.ShapeDtypeStruct((rows, features), F32)],
+            HBM,
+        ],
+        out_shape=[
+            sh,
+            sh,
+            sh,
+            jax.ShapeDtypeStruct((rows, features), F32),
+            jax.ShapeDtypeStruct((dp_count, 3, features // dp_count, hw), BF),
+        ],
         scratch_shapes=[
             pltpu.VMEM((SLOT, width), F32),
             pltpu.VMEM((SLOT, width), F32),
+            pltpu.VMEM((3, total, hw), BF),
+            pltpu.VMEM((2, mp_count, rows, span), BF),
+            pltpu.VMEM((3, span, hw), BF),
             DMA((2,)),
+            DMA((3,)),
             *scatter_scratch(mp_count, rows, features),
         ],
         compiler_params=pltpu.CompilerParams(
-            collective_id=cid, has_side_effects=True, vmem_limit_bytes=60 << 20
+            collective_id=cid, has_side_effects=True, vmem_limit_bytes=62 << 20
         ),
         cost_estimate=pl.CostEstimate(
             flops=segs * heads * SLOT * SLOT * 320,
-            bytes_accessed=290 << 20,
+            bytes_accessed=260 << 20,
             transcendentals=segs * heads * SLOT * SLOT // 2,
         ),
-    )(seg_len, q, k, v, o, do, lse, part)
+    )(seg_len, q, k, v, o, do, lse, part, far_in, x_all)
 
 
 GELU_C = math.sqrt(2.0 / math.pi)
@@ -1205,8 +1276,8 @@
 
 
 def ffn_kernel(
-    mp_count, own, u_all, up, down, out, x_all, part_out, kept, g_out,
-    x, u, hid, pre, part, tile, g_tile, io_sem, p_send, p_recv, recv, sends, sem, *scratch
+    mp_count, own, u_all, up, down, out, x_all, part_out, kept, g_out, far_in,
+    x, u, hid, pre, part, tile, g_tile, io_sem, p_send, p_recv, f_send, f_recv, recv, sends, sem, *scratch
 ):
     line = Line(mp_count)
     line.greet()
@@ -1284,6 +1355,28 @@
     saved(0).wait()
     scatter.across(0).wait_send()
     given(0).wait_send()
+    at_start, at_end = line.chip == 0, line.chip == line.n - 1
+    farthest = jnp.where(at_start, line.n - 1, jnp.where(at_end, 0, -1))
+
+    def far_copy(way):
+        device = (line.right, line.left)[way]
+        return remote(x, far_in.at[way], f_send, f_recv.at[way], device)
+
+    @pl.when(at_start | at_end)
+    def _():
+        given(2 * farthest).wait_recv()
+        one = local(part_out.at[0, farthest], x, io_sem.at[0])
+        two = local(part_out.at[1, farthest], u, io_sem.at[1])
+        one.wait()
+        two.wait()
+
+        def add(at, carry):
+            x[at, :] = (x[at, :].astype(F32) + u[at, :].astype(F32)).astype(BF)
+            return carry
+
+        row_chunks(rows, add)
+        pl.when(at_start)(lambda: far_copy(0).start())
+        pl.when(at_end)(lambda: far_copy(1).start())
 
     def fetch(i, which):
         source = (x_all, u_all)[which]
@@ -1331,7 +1424,10 @@
     scatter.last(out)
     gather.finish()
     for chip in range(mp_count // 2):
-        given(2 * chip).wait_recv()
+        pl.when(farthest != chip)(lambda chip=chip: given(2 * chip).wait_recv())
+    pl.when(line.chip == 1)(lambda: far_copy(0).wait_recv())
+    pl.when(line.chip == line.n - 2)(lambda: far_copy(1).wait_recv())
+    pl.when(at_start | at_end)(lambda: far_copy(0).wait_send())
 
 
 def ffn(own, u_all, up, down, dp_count, mp_count, cid):
@@ -1343,13 +1439,14 @@
     return pl.pallas_call(
         functools.partial(ffn_kernel, mp_count),
         in_specs=[HBM, HBM, VM, VM],
-        out_specs=[VM, HBM, HBM, HBM, HBM],
+        out_specs=[VM, HBM, HBM, HBM, HBM, HBM],
         out_shape=[
             jax.ShapeDtypeStruct((rows, width), F32),
             jax.ShapeDtypeStruct((mp_count, rows, width), BF),
             jax.ShapeDtypeStruct((2, chips, rows, width), BF),
             jax.ShapeDtypeStruct((chips, rows, width), BF),
             jax.ShapeDtypeStruct((dp_count, 2, width // dp_count, units), BF),
+            jax.ShapeDtypeStruct((2, rows, width), BF),
         ],
         scratch_shapes=[
             pltpu.VMEM((rows, width), BF),
@@ -1362,6 +1459,8 @@
             DMA((4,)),
             DMA(()),
             DMA((chips,)),
+            DMA(()),
+            DMA((2,)),
             *gather_sems(mp_count, 2),
             pltpu.VMEM((chips, rows, width), BF),
             pltpu.VMEM((chips + 1, rows, width), BF),
@@ -1384,10 +1483,15 @@
     )(own, u_all, up, down)
 
 
-def shampoo_kernel(group, tc, flipped, w_ref, g_ref, l_ref, r_ref, nw_ref, nl_ref, nr_ref, gf_ref):
+def shampoo_kernel(group, tc, form, w_ref, g_ref, l_ref, r_ref, nw_ref, nl_ref, nr_ref, gf_ref):
     for h in range(group):
         cols = slice(h * tc, (h + 1) * tc)
-        g = g_ref[...].T if flipped else g_ref[:, cols]
+        if form == "flipped":
+            g = g_ref[...].T
+        elif form == "heads":
+            g = jnp.concatenate([g_ref[j, :, h * HD : (h + 1) * HD] for j in range(3)], axis=1)
+        else:
+            g = g_ref[:, cols]
         gf_ref[:, cols] = g.astype(F32)
         nl_ref[0, h] = DECAY * l_ref[0, 0, h] + (1.0 - DECAY) * dg(g, g, NT)
         nr_ref[0, h] = DECAY * r_ref[0, 0, h] + (1.0 - DECAY) * dg(g, g, TN)
@@ -1396,13 +1500,17 @@
         nw_ref[:, cols] = w_ref[:, cols] - SHAMPOO_RATE * step
 
 
-def shampoo(weight, grad, left, right, tr, tc, flipped=False):
+def shampoo(weight, grad, left, right, tr, tc, form="plain"):
     rows, cols = weight.shape
     tiles_c = cols // tc
     group = 1 if tc % 128 == 0 or tiles_c == 1 else 2
     width = group * tc
     wide = pl.BlockSpec((tr, width), lambda i, j: (i, j))
-    grad_block = pl.BlockSpec((width, tr), lambda i, j: (j, i)) if flipped else wide
+    grad_block = wide
+    if form == "flipped":
+        grad_block = pl.BlockSpec((width, tr), lambda i, j: (j, i))
+    elif form == "heads":
+        grad_block = pl.BlockSpec((3, tr, group * HD), lambda i, j: (0, i, j))
 
     def stat(size):
         return pl.BlockSpec((2, 1, group, size, size), lambda i, j: (0, i, j, 0, 0))
@@ -1411,7 +1519,7 @@
         return pl.BlockSpec((1, group, size, size), lambda i, j: (i, j, 0, 0))
 
     return pl.pallas_call(
-        functools.partial(shampoo_kernel, group, tc, flipped),
+        functools.partial(shampoo_kernel, group, tc, form),
         grid=(rows // tr, tiles_c // group),
         in_specs=[wide, grad_block, stat(tr), stat(tc)],
         out_specs=[wide, new(tr), new(tc), wide],
@@ -1488,14 +1596,14 @@
         seg_len, queries, keys, values, upstream, out_weight.astype(BF), dp_count, mp_count, 2
     )
     resid, normed_two = out_and_norm(ctx_rows, out_full, tokens, ln_gain, mp_count)
-    d_normed_two, _, ffn_part, _, grad_ffn = ffn(
+    d_normed_two, _, ffn_part, _, grad_ffn, far_in = ffn(
         normed_two, upstream_all, up_part, down_part, dp_count, mp_count, 4
     )
     d_resid, d_gain_two, d_context, grad_out = resid_back(
         d_normed_two, resid, upstream, ln_gain, out_full, ctx_rows, dp_count, mp_count, 5
     )
     grad_ffn = lax.psum_scatter(grad_ffn, "dp", scatter_dimension=0, tiled=False)
-    d_queries, d_keys, d_values, ffn_out = attend_bwd(
+    d_queries, d_keys, d_values, ffn_out, grad_qkv = attend_bwd(
         seg_len,
         queries,
         keys,
@@ -1504,18 +1612,16 @@
         d_context.reshape(mp_count * row_count, head_width),
         log_sums,
         ffn_part,
+        far_in,
+        gathered,
+        dp_count,
         mp_count,
         6,
     )
     block_out = (resid + ffn_out).astype(BF)
-    d_qkv = jnp.concatenate([d_queries, d_keys, d_values], axis=1)
-    d_qkv, grad_out, grad_ffn = lax.optimization_barrier((d_qkv, grad_out, grad_ffn))
+    grad_qkv, grad_out, grad_ffn = lax.optimization_barrier((grad_qkv, grad_out, grad_ffn))
+    grad_qkv = lax.psum_scatter(grad_qkv, "dp", scatter_dimension=0, tiled=False)
     grad_out = lax.psum_scatter(grad_out, "dp", scatter_dimension=0, tiled=False)
-    gathered = gathered.reshape(mp_count * row_count, features)
-    grad_qkv_part = jnp.einsum("gd,gc->dc", gathered, d_qkv, preferred_element_type=F32)
-    grad_qkv = lax.psum_scatter(
-        grad_qkv_part.astype(BF), "dp", scatter_dimension=0, tiled=True
-    )
     picks = seg_count * NSUM
     padded = -(-picks // 16) * 16
     slot_index = (jnp.arange(seg_count) * SLOT + seg_len)[:, None] + jnp.arange(NSUM)[None, :]
@@ -1544,11 +1650,6 @@
     grad_out = lax.psum_scatter(
         grad_out, "mp", scatter_dimension=0, tiled=False, axis_index_groups=lines
     )
-    grad_qkv = (
-        grad_qkv.reshape(own_rows, 3, head_count, HD)
-        .transpose(0, 2, 1, 3)
-        .reshape(own_rows, own_cols)
-    )
     owned_vectors = owned_vectors[:picks].reshape(seg_count, NSUM, features // mp_count)
     owned_width = owned_vectors.shape[2]
     gain_grads, total_cols, total_squares = stats[:2], stats[2], stats[3, 0]
@@ -1561,7 +1662,7 @@
         jnp.mean(gain_grads * gain_grads, axis=-1, keepdims=True) + 1e-06
     )
     new_qkv, new_left_qkv, new_right_qkv, grad_qkv = shampoo(
-        qkv_weight, grad_qkv, left_qkv, right_qkv, BLOCK, 3 * HD
+        qkv_weight, grad_qkv, left_qkv, right_qkv, BLOCK, 3 * HD, "heads"
     )
     new_out, new_left_out, new_right_out, grad_out = shampoo(
         out_weight, grad_out, left_out, right_out, BLOCK, HD
@@ -1570,7 +1671,7 @@
         up_weight, grad_up, left_up, right_up, BLOCK, FBLK
     )
     new_down, new_left_down, new_right_down, grad_down = shampoo(
-        down_weight, grad_down, left_down, right_down, FBLK, BLOCK, True
+        down_weight, grad_down, left_down, right_down, FBLK, BLOCK, "flipped"
     )
     return (
         block_out,

time: 726 us -> 695 us (0.957)
  Pallas kernels: 649 us -> 634 us
  matrix products: 11.7 us -> 0.33 us
    pallas_call x1, Pallas kernels: 87.5 us -> 65.1 us  [attend_bwd(): pl.pallas_call(functools.partial(attend_bwd_kernel, hp, bq, segs * pairs...]
    dot_general x1 -> x0, matrix products: 11.4 us -> none  [body(): jnp.einsum('gd,gc->dc', gathered, d_qkv, preferred_element_type=F32)]
    pallas_call x1, Pallas kernels: 95.7 us -> 103 us  [input_back(): pl.pallas_call(functools.partial(d_normed_kernel, dp_count, mp_count), in...]
    unnamed x61 -> x65, local copies, waits for them, and re-layouts: 19.5 us -> 20.3 us
  transfers between devices with their start and end apart: 6 -> 6, of which waited for: 0 -> 0; matrix products, arithmetic and copies ran while one was open for 3% -> 2% of each run, Pallas kernels for 64% -> 65%
where the time goes in v5:
time: 695 us; the launch traced here: 686 us
  Pallas kernels  634 us (91%)
  local copies, waits for them, and re-layouts  22.7 us (3%)
  between operations  16.7 us (2%)
  other arithmetic  11 us (2%)
    pallas_call x1, Pallas kernels, ffn(): pl.pallas_call(functools.partial(ffn_kernel, mp_count), in_specs=[HBM, HB...  182 us
    pallas_call x1, Pallas kernels, attend_fwd(): pl.pallas_call(functools.partial(attend_fwd_kernel, hp, bq, segs * pairs...  122 us
    pallas_call x1, Pallas kernels, input_back(): pl.pallas_call(functools.partial(d_normed_kernel, dp_count, mp_count), in...  103 us
    pallas_call x1, Pallas kernels, gather_qkv(): pl.pallas_call(functools.partial(qkv_kernel, dp_count, mp_count), in_spec...  89.7 us
    pallas_call x1, Pallas kernels, attend_bwd(): pl.pallas_call(functools.partial(attend_bwd_kernel, hp, bq, segs * pairs...  65.1 us
    pallas_call x1, Pallas kernels, resid_back(): pl.pallas_call(functools.partial(resid_back_kernel, dp_count, mp_count),...  36.4 us
    pallas_call x4, Pallas kernels, shampoo(): pl.pallas_call(functools.partial(shampoo_kernel, group, tc, form), grid=(...  29.7 us
    unnamed x65, local copies, waits for them, and re-layouts  20.3 us
  transfers between devices with their start and end apart: 6, of which 0 were waited for; matrix products, arithmetic and copies ran while one was open for 2% of the time, Pallas kernels for 65%

profile of v5, /device:TPU:0, one launch (start us, length us, event | category | flops | bytes accessed | tf_op | source)
XLA Modules:
  0.0 686.1 jit_solution(353636426776184156)
XLA Ops:
  7.2 0.0 copy-start.3
  7.2 0.0 all-gather.3.cloned.1.call-start
  7.2 2.9 convert_element_type.29
  10.1 0.0 all-gather.3.cloned.1.call-update
  10.1 0.0 all-gather.5.cloned.1.call-start
  10.2 1.1 convert_element_type.30
  11.3 0.0 all-gather.5.cloned.1.call-update
  11.3 0.0 reduce-scatter.13.cloned.1.call-start
  12.0 1.7 copy.44
  13.7 0.0 copy-start
  13.7 0.1 copy.45
  13.8 0.3 copy.46.w_own
  14.1 0.7 copy-done.6
  14.8 0.0 copy-start.28
  14.8 0.3 copy-done
  15.1 0.2 convert_reduce_fusion
  15.3 0.4 fusion.2
  15.8 0.3 copy-done.28
  16.1 1.1 broadcast_select_fusion.up_own
  17.2 0.4 fusion.4.own
  17.6 89.7 %shard_map.319 = (bf16[8,256,2048]{2,1,0:T(8,128)(2,1)}, bf16[2048,256]{1,0:T(8,128)(2,1)S(1)}, bf16[2048,256]{1,0:T(8,128)(2,1)S(1)}, bf16[2048,256]{1,0:T(8,128)(2,1)S(1)}, bf16[3,2048,256]{2,1,0:T(8,128)(2,1)S(1)}) custom-call(bf16[256,2048]{1,0:T(8,128)(2,1)S(1)} %fusion.4.own, bf16[3,512,256]{2,1,0:T(8,128)(2,1)S(1)} %copy.46.w_own), custom_call_target="tpu_custom_call" | custom-call | flops 6442450944 | bytes 293601280 | tf_op jit(solution)/shard_map/pallas_call | solution.py:332
  107.3 1.7 copy-done.24
  109.0 122.1 %shard_map.320 = (bf16[2048,256]{1,0:T(8,128)(2,1)S(1)}, f32[1,4,8,2048]{3,2,1,0:T(8,128)S(1)}, bf16[8,256,256]{2,1,0:T(8,128)(2,1)S(1)}, bf16[8,256,2048]{2,1,0:T(8,128)(2,1)}, bf16[2,4,2048,256]{3,2,1,0:T(8,128)(2,1)}) custom-call(s32[1]{0:T(128)} %copy.53.len_ref, bf16[2048,256]{1,0:T(8,128)(2,1)S(1)} %get-tuple-element.72.q_ref, ...), custom_call_target="tpu_custom_call" | custom-call | flops 2147483648 | bytes 398458880 | tf_op jit(solution)/shard_map/pallas_call | solution.py:507
  231.2 1.0 copy-done.16
  232.1 3.9 copy-done.1
  236.0 5.6 shard_map.321
  241.7 0.0 copy-start.7
  241.7 1.3 copy-done.7
  243.0 1.0 copy-done.23
  244.0 182.5 %shard_map.322 = (f32[256,2048]{1,0:T(8,128)}, bf16[8,256,2048]{2,1,0:T(8,128)(2,1)}, bf16[2,4,256,2048]{3,2,1,0:T(8,128)(2,1)}, bf16[4,256,2048]{2,1,0:T(8,128)...) custom-call(bf16[256,2048]{1,0:T(8,128)(2,1)} %copy-done.23, ...), custom_call_target="tpu_custom_call" | custom-call | flops 51539607552 | bytes 555745280 | tf_op jit(solution)/shard_map/pallas_call | solution.py:1439
  426.4 0.0 reduce-scatter.13.cloned.1.call-update
  426.4 0.0 reduce-scatter.15.cloned.1.call-start
  426.5 36.4 %shard_map.323 = (f32[256,2048]{1,0:T(8,128)}, f32[1,2048]{1,0:T(1,128)}, bf16[8,256,256]{2,1,0:T(8,128)(2,1)}, bf16[4,4,512,256]{3,2,1,0:T(8,128)(2,1)}) custom-call(f32[256,2048]{1,0:T(8,128)} %get-tuple-element.81.dn, f32[256,2048]{1,0:T(8,128)} %copy-done.7, bf16[256,2048]{1,0:T(8,128)(2,1)} %broadcast_select_fusion.up_own, f32[2,2048]{1,0:T(2,128)} %gain.5, ...), custom_call_target="tpu_custom_call" | custom-call | flops 4294967296 | bytes 115343360 | tf_op jit(solution)/shard_map/pallas_call | solution.py:730
  462.9 65.1 %shard_map.324 = (bf16[2048,256]{1,0:T(8,128)(2,1)}, bf16[2048,256]{1,0:T(8,128)(2,1)}, bf16[2048,256]{1,0:T(8,128)(2,1)}, f32[256,2048]{1,0:T(8,128)}, bf16[4,3,512,256]{3,2,1,0:T(8,128)(2,1)}) custom-call(s32[1]{0:T(128)} %copy.53.len_ref, bf16[2048,256]{1,0:T(8,128)(2,1)} %copy-done.13, bf16[2048,256]{1,0:T(8,128)(2,1)} %copy-done.14, ...), custom_call_target="tpu_custom_call" | custom-call | flops 5368709120 | bytes 272629760 | tf_op jit(solution)/shard_map/pallas_call | solution.py:1122
  528.0 0.0 reduce-scatter.13.cloned.1.call-done
  528.0 0.0 reduce-scatter.15.cloned.1.call-update
  528.1 0.0 reduce-scatter.17.cloned.1.call-start
  528.1 0.5 reduce-scatter.17.cloned.1.call-update
  528.7 0.0 reduce-scatter.11.cloned.1.call-start
  528.7 0.9 copy-done.8
  529.6 1.8 add_convert_fusion
  531.5 0.3 convolution_convert_fusion
  531.8 0.7 copy.51
  532.6 103.3 %shard_map.325 = (f32[256,2048]{1,0:T(8,128)}, f32[64,256]{1,0:T(8,128)}, f32[4,2048]{1,0:T(4,128)}) custom-call(bf16[2048,256]{1,0:T(8,128)(2,1)} %get-tuple-element.88.dq, bf16[2048,256]{1,0:T(8,128)(2,1)} %get-tuple-element.89.dk, bf16[2048,256]{1,0:T(8,128)(2,1)} %get-tuple-element.90.dv, bf16[3,2048,256]{2,1,0:T(8,128)(2,1)} %copy-done.24, ...), custom_call_target="tpu_custom_call" | custom-call | flops 6442450944 | bytes 314572800 | tf_op jit(solution)/shard_map/pallas_call | solution.py:983
  635.9 0.0 reduce-scatter.15.cloned.1.call-done
  635.9 0.0 reduce-scatter.17.cloned.1.call-done
  635.9 1.2 slice.24
  637.1 0.0 reduce-scatter.11.cloned.1.call-update
  637.8 1.4 multiply_reduce_fusion.1
  639.9 0.8 multiply_bitcast_fusion
  640.7 0.7 copy.48
  641.4 1.4 copy-done.11
  642.8 1.1 copy-done.17
  644.0 6.9 %shard_map.326 = (f32[512,768]{1,0:T(8,128)}, f32[1,4,512,512]{3,2,1,0:T(8,128)}, f32[1,4,192,192]{3,2,1,0:T(8,128)}, f32[512,768]{1,0:T(8,128)}) custom-call(f32[512,768]{1,0:T(8,128)S(1)} %copy-done.5, bf16[3,512,256]{2,1,0:T(8,128)(2,1)S(1)} %bitcast.30, f32[2,1,4,512,512]{4,3,2,1,0:T(8,128)} %l_ref.4, f32[2,1,4,192,192]{4,3,2,1,0:T(8,128)S(1)} %copy-done.11), custom_call_target="tpu_custom_call" | custom-call | flops 1107296256 | bytes 19857408 | tf_op jit(solution)/shard_map/pallas_call | solution.py:1521
  650.9 0.2 slice_bitcast_fusion
  651.1 1.4 copy-done.2
  652.5 0.6 copy-done.9
  653.1 8.5 %shard_map.328 = (f32[512,1024]{1,0:T(8,128)}, f32[1,4,512,512]{3,2,1,0:T(8,128)}, f32[1,4,256,256]{3,2,1,0:T(8,128)}, f32[512,1024]{1,0:T(8,128)}) custom-call(f32[512,1024]{1,0:T(8,128)S(1)} %copy-done.2, bf16[512,1024]{1,0:T(8,128)(2,1)S(1)} %get-tuple-element.191.g_ref, f32[2,1,4,512,512]{4,3,2,1,0:T(8,128)} %l_ref.6, f32[2,1,4,256,256]{4,3,2,1,0:T(8,128)S(1)} %copy-done.9), custom_call_target="tpu_custom_call" | custom-call | flops 1610612736 | bytes 23068672 | tf_op jit(solution)/shard_map/pallas_call | solution.py:1521
  661.7 8.1 %shard_map.329 = (f32[1024,512]{1,0:T(8,128)}, f32[4,1,256,256]{3,2,1,0:T(8,128)}, f32[4,1,512,512]{3,2,1,0:T(8,128)}, f32[1024,512]{1,0:T(8,128)}) custom-call(f32[1024,512]{1,0:T(8,128)S(1)} %copy-done.4, bf16[512,1024]{1,0:T(8,128)(2,1)S(1)} %get-tuple-element.190.g_ref, f32[2,4,1,256,256]{4,3,2,1,0:T(8,128)S(1)} %copy-done.10, f32[2,4,1,512,512]{4,3,2,1,0:T(8,128)} %r_ref.7), custom_call_target="tpu_custom_call" | custom-call | flops 1610612736 | bytes 23068672 | tf_op jit(solution)/shard_map/pallas_call | solution.py:1521
  669.8 0.1 multiply_reduce_fusion
  670.0 0.7 multiply_subtract_fusion
  670.7 0.9 copy-done.20
  671.6 6.1 shard_map.327
  677.8 1.3 copy.54
  (58 shorter events, 0.2 us)
Async XLA Ops:
  7.2 3.0 copy-start.3
  7.2 236.7 %all-gather.3.cloned.1.call-start = ((), (), s32[]{:S(2)}) async-start(), calls=%async_computation.4 | async-start | bytes 5242880 | tf_op jit(solution)/shard_map/all_gather | solution.py:1593
  10.1 233.8 %all-gather.5.cloned.1.call-start = ((), (), s32[]{:S(2)}) async-start(), calls=%async_computation.5 | async-start | bytes 5242880 | tf_op jit(solution)/shard_map/all_gather | solution.py:1594
  11.3 516.7 %reduce-scatter.13.cloned.1.call-start = ((), (), s32[]{:S(2)}) async-start(), calls=%async_computation.7 | async-start | bytes 10485760
  13.7 1.0 copy-start.6
  13.7 1.4 copy-start
  14.8 1.3 copy-start.28
  15.1 2.1 slice-start
  107.3 1.7 copy-start.24
  109.0 122.1 %copy-start.13 = (bf16[2048,256]{1,0:T(8,128)(2,1)}, bf16[2048,256]{1,0:T(8,128)(2,1)S(1)}, u32[]{:S(2)}) copy-start(bf16[2048,256]{1,0:T(8,128)(2,1)S(1)} %get-tuple-element.72.q_ref) | copy-start | bytes 3145732
  109.0 122.2 %copy-start.14 = (bf16[2048,256]{1,0:T(8,128)(2,1)}, bf16[2048,256]{1,0:T(8,128)(2,1)S(1)}, u32[]{:S(2)}) copy-start(bf16[2048,256]{1,0:T(8,128)(2,1)S(1)} %get-tuple-element.73.k_ref) | copy-start | bytes 3145732
  109.0 122.2 %copy-start.15 = (bf16[2048,256]{1,0:T(8,128)(2,1)}, bf16[2048,256]{1,0:T(8,128)(2,1)S(1)}, u32[]{:S(2)}) copy-start(bf16[2048,256]{1,0:T(8,128)(2,1)S(1)} %get-tuple-element.74.v_ref) | copy-start | bytes 3145732
  109.0 123.1 %copy-start.21 = (f32[2,2048]{1,0:T(2,128)S(1)}, f32[2,2048]{1,0:T(2,128)}, u32[]{:S(2)}) copy-start(f32[2,2048]{1,0:T(2,128)} %gain.5) | copy-start | bytes 49156
  231.2 1.0 copy-start.16
  232.1 9.5 %copy-start.12 = (bf16[8,256,256]{2,1,0:T(8,128)(2,1)}, bf16[8,256,256]{2,1,0:T(8,128)(2,1)S(1)}, u32[]{:S(2)}) copy-start(bf16[8,256,256]{2,1,0:T(8,128)(2,1)S(1)} %get-tuple-element.75.ctx) | copy-start | bytes 3145732
  232.1 9.5 %copy-start.18 = (f32[1,4,8,2048]{3,2,1,0:T(8,128)}, f32[1,4,8,2048]{3,2,1,0:T(8,128)S(1)}, u32[]{:S(2)}) copy-start(f32[1,4,8,2048]{3,2,1,0:T(8,128)S(1)} %get-tuple-element.83.lse_ref) | copy-start | bytes 786436
  232.1 3.9 copy-start.1
  241.7 1.3 copy-start.7
  243.0 1.0 copy-start.23
  426.4 209.5 %reduce-scatter.15.cloned.1.call-start = ((), (), s32[]{:S(2)}) async-start(), calls=%async_computation.8 | async-start | bytes 3932160
  528.1 1.6 copy-start.8
  528.1 107.9 %reduce-scatter.17.cloned.1.call-start = ((), (), s32[]{:S(2)}) async-start(), calls=%async_computation.9 | async-start | bytes 5242880
  528.7 142.0 %reduce-scatter.11.cloned.1.call-start = ((), (), s32[]{:S(2)}) async-start(), calls=%async_computation.6 | async-start | bytes 1310720 | tf_op jit(solution)/shard_map/reduce_scatter | solution.py:1650
  531.5 1.1 copy-start.25
  532.6 108.8 %copy-start.5 = (f32[512,768]{1,0:T(8,128)S(1)}, f32[512,768]{1,0:T(8,128)}, u32[]{:S(2)}) copy-start(f32[512,768]{1,0:T(8,128)} %w_ref.4) | copy-start | bytes 4718596
  641.4 1.4 copy-start.11
  642.8 1.2 copy-start.17
  644.0 6.9 %copy-start.26 = (bf16[1,2,512,1024]{3,2,1,0:T(8,128)(2,1)S(1)}, bf16[1,2,512,1024]{3,2,1,0:T(8,128)(2,1)}, u32[]{:S(2)}) copy-start(bf16[1,2,512,1024]{3,2,1,0:T(8,128)(2,1)} %reduce-scatter.13.cloned.1.call-done) | copy-start | bytes 6291460
  650.9 1.6 copy-start.2
  650.9 2.2 copy-start.9
  653.1 8.5 %copy-start.4 = (f32[1024,512]{1,0:T(8,128)S(1)}, f32[1024,512]{1,0:T(8,128)}, u32[]{:S(2)}) copy-start(f32[1024,512]{1,0:T(8,128)} %w_ref.7) | copy-start | bytes 6291460
  653.1 8.5 %copy-start.10 = (f32[2,4,1,256,256]{4,3,2,1,0:T(8,128)S(1)}, f32[2,4,1,256,256]{4,3,2,1,0:T(8,128)}, u32[]{:S(2)}) copy-start(f32[2,4,1,256,256]{4,3,2,1,0:T(8,128)} %l_ref.7) | copy-start | bytes 6291460
  661.7 8.2 %copy-start.30 = (f32[4,2048]{1,0:T(4,128)S(1)}, f32[4,2048]{1,0:T(4,128)}, u32[]{:S(2)}) copy-start(f32[4,2048]{1,0:T(4,128)} %get-tuple-element.103) | copy-start | bytes 98308
  661.7 8.3 %copy-start.22 = (f32[2,2048]{1,0:T(2,128)S(1)}, f32[2,2048]{1,0:T(2,128)}, u32[]{:S(2)}) copy-start(f32[2,2048]{1,0:T(2,128)} %gain.5) | copy-start | bytes 49156
  661.7 9.0 %copy-start.19 = (f32[2,1,4,64,64]{4,3,2,1,0:T(8,128)S(1)}, f32[2,1,4,64,64]{4,3,2,1,0:T(8,128)}, u32[]{:S(2)}) copy-start(f32[2,1,4,64,64]{4,3,2,1,0:T(8,128)} %r_ref.5) | copy-start | bytes 393220
  670.0 7.8 %copy-start.29 = (f32[2,2048]{1,0:T(2,128)}, f32[2,2048]{1,0:T(2,128)S(1)}, u32[]{:S(2)}) copy-start(f32[2,2048]{1,0:T(2,128)S(1)} %get-tuple-element.216) | copy-start | bytes 49156
  670.7 1.0 copy-start.20
  671.6 6.1 copy-start.27
Sparse Core Ops, SparseCore 0:
  10.5 82.1 all-gather.2
  95.1 52.5 all-gather.4
  426.6 95.3 reduce-scatter.12
  528.2 49.1 reduce-scatter.14
  580.5 52.6 reduce-scatter.16
  637.3 27.8 reduce-scatter.10

commit v6 on v5

--- a/solution.py
+++ b/solution.py
@@ -537,7 +537,7 @@
             DMA((pairs, mp_count)),
             DMA((pairs, mp_count)),
             DMA((pairs,)),
-            *gather_sems(mp_count),
+            *gather_sems(mp_count, 2),
             *gather_sems(mp_count),
             DMA((dp_count,)),
             DMA((dp_count,)),
@@ -895,8 +895,8 @@
 
 
 def d_normed_kernel(
-    dp_count, mp_count, dq, dk, dv, w, tokens, gain, d_resid, picked, d_gain_two,
-    out, owned, stats,
+    dp_count, mp_count, vector_count, dq, dk, dv, w, tokens, gain, d_resid, picked, d_gain_two,
+    out, summed, gain_grads, new_gains,
     total, land, p_send, p_recv, x, mid, by_mp, by_dp, m_send, m_recv, d_send, d_recv, *scratch
 ):
     line = Line(mp_count)
@@ -922,6 +922,7 @@
             sum_of = sum_of + ref[k]
         return sum_of
 
+    each = summed.shape[1]
     for peer in peers:
         pick(peer, me).start()
     land[me] = picked[me]
@@ -938,11 +939,10 @@
         for peer in peers:
             pick(peer, peer).wait_recv()
         vectors = lax.fori_loop(
-            0, mp_count, lambda p, s: s + land[p].astype(F32), jnp.zeros(owned.shape, F32)
+            0, mp_count, lambda p, s: s + land[p].astype(F32), jnp.zeros(summed.shape, F32)
         )
-        owned[...] = vectors
+        summed[...] = vectors
         sums = jnp.sum(vectors, axis=0, keepdims=True)
-        each = owned.shape[1]
         for p in range(mp_count):
             x[2:3, p * each : (p + 1) * each] = jnp.where(me == p, sums, 0.0)
         x[1:2, :] = d_gain_two[...]
@@ -968,7 +968,20 @@
     by_dp[dp] = mid[...]
     for peer in dp_peers:
         over_dp(peer, peer).wait_recv()
-    stats[...] = added(by_dp, dp_count)
+    stats = added(by_dp, dp_count)
+    grads = stats[0:2, :]
+    gain_grads[...] = grads
+    new_gains[...] = gain[...] - GAIN_RATE * grads * lax.rsqrt(
+        jnp.mean(grads * grads, axis=-1, keepdims=True) + 1e-06
+    )
+    centres = stats[2:3, :] * (1.0 / vector_count)
+    centre = jnp.zeros((1, each), F32)
+    for p in range(mp_count):
+        centre += jnp.where(me == p, centres[:, p * each : (p + 1) * each], 0.0)
+    variance = stats[3:4, 0:1] * (1.0 / (vector_count * width)) - jnp.mean(
+        centres * centres, axis=-1, keepdims=True
+    )
+    summed[...] = (summed[...] - centre) * lax.rsqrt(variance + NORM_EPSILON)
     for peer in peers:
         pick(peer, me).wait_send()
         over_mp(peer, me).wait_send()
@@ -977,17 +990,18 @@
 
 
 def input_back(
-    dq, dk, dv, w, tokens, gain, d_resid, picked, d_gain_two, dp_count, mp_count, cid
+    dq, dk, dv, w, tokens, gain, d_resid, picked, d_gain_two, vectors, dp_count, mp_count, cid
 ):
     rows, width = tokens.shape
     return pl.pallas_call(
-        functools.partial(d_normed_kernel, dp_count, mp_count),
+        functools.partial(d_normed_kernel, dp_count, mp_count, vectors),
         in_specs=[VM] * 9,
-        out_specs=[VM, VM, VM],
+        out_specs=[VM, VM, VM, VM],
         out_shape=[
             jax.ShapeDtypeStruct((rows, width), F32),
             jax.ShapeDtypeStruct(picked.shape[1:], F32),
-            jax.ShapeDtypeStruct((4, width), F32),
+            jax.ShapeDtypeStruct((2, width), F32),
+            jax.ShapeDtypeStruct((2, width), F32),
         ],
         scratch_shapes=[
             pltpu.VMEM((rows, width), F32),
@@ -1603,6 +1617,7 @@
         d_normed_two, resid, upstream, ln_gain, out_full, ctx_rows, dp_count, mp_count, 5
     )
     grad_ffn = lax.psum_scatter(grad_ffn, "dp", scatter_dimension=0, tiled=False)
+    grad_out = lax.psum_scatter(grad_out, "dp", scatter_dimension=0, tiled=False)
     d_queries, d_keys, d_values, ffn_out, grad_qkv = attend_bwd(
         seg_len,
         queries,
@@ -1619,9 +1634,8 @@
         6,
     )
     block_out = (resid + ffn_out).astype(BF)
-    grad_qkv, grad_out, grad_ffn = lax.optimization_barrier((grad_qkv, grad_out, grad_ffn))
+    grad_qkv, grad_ffn = lax.optimization_barrier((grad_qkv, grad_ffn))
     grad_qkv = lax.psum_scatter(grad_qkv, "dp", scatter_dimension=0, tiled=False)
-    grad_out = lax.psum_scatter(grad_out, "dp", scatter_dimension=0, tiled=False)
     picks = seg_count * NSUM
     padded = -(-picks // 16) * 16
     slot_index = (jnp.arange(seg_count) * SLOT + seg_len)[:, None] + jnp.arange(NSUM)[None, :]
@@ -1629,7 +1643,7 @@
     selector = (slot_index[:, None] == positions[None, :]).astype(BF)
     picked = jnp.dot(selector, block_out, preferred_element_type=F32).astype(BF)
     picked = picked.reshape(padded, mp_count, features // mp_count).transpose(1, 0, 2)
-    input_grad, owned_vectors, stats = input_back(
+    input_grad, summaries, gain_grads, new_gains = input_back(
         d_queries,
         d_keys,
         d_values,
@@ -1639,28 +1653,19 @@
         d_resid,
         picked,
         d_gain_two,
+        dp_count * picks,
         dp_count,
         mp_count,
         7,
     )
-    stats, grad_ffn, grad_qkv, grad_out = lax.optimization_barrier(
-        (stats, grad_ffn, grad_qkv, grad_out)
+    gain_grads, grad_ffn, grad_qkv, grad_out = lax.optimization_barrier(
+        (gain_grads, grad_ffn, grad_qkv, grad_out)
     )
     grad_up, grad_down = grad_ffn[0], grad_ffn[1]
     grad_out = lax.psum_scatter(
         grad_out, "mp", scatter_dimension=0, tiled=False, axis_index_groups=lines
     )
-    owned_vectors = owned_vectors[:picks].reshape(seg_count, NSUM, features // mp_count)
-    owned_width = owned_vectors.shape[2]
-    gain_grads, total_cols, total_squares = stats[:2], stats[2], stats[3, 0]
-    vector_count = seg_count * dp_count * NSUM
-    centre_all = total_cols / vector_count
-    centre = lax.dynamic_slice_in_dim(centre_all, mp_index * owned_width, owned_width, 0)
-    variance = total_squares / (vector_count * features) - jnp.mean(centre_all * centre_all)
-    summaries = (owned_vectors - centre) * lax.rsqrt(variance + NORM_EPSILON)
-    new_gains = ln_gain - GAIN_RATE * gain_grads * lax.rsqrt(
-        jnp.mean(gain_grads * gain_grads, axis=-1, keepdims=True) + 1e-06
-    )
+    summaries = summaries[:picks].reshape(seg_count, NSUM, features // mp_count)
     new_qkv, new_left_qkv, new_right_qkv, grad_qkv = shampoo(
         qkv_weight, grad_qkv, left_qkv, right_qkv, BLOCK, 3 * HD, "heads"
     )

time: 695 us -> 685 us (0.986)
  transfers between devices with their start and end apart: 6 -> 6, of which waited for: 0 -> 0; matrix products, arithmetic and copies ran while one was open for 2% -> 1% of each run, Pallas kernels for 65% -> 65%
where the time goes in v6:
time: 685 us; the launch traced here: 676 us
  Pallas kernels  628 us (92%)
  local copies, waits for them, and re-layouts  24.1 us (4%)
  between operations  15.4 us (2%)
  other arithmetic  8.01 us (1%)
    pallas_call x1, Pallas kernels, ffn(): pl.pallas_call(functools.partial(ffn_kernel, mp_count), in_specs=[HBM, HB...  182 us
    pallas_call x1, Pallas kernels, attend_fwd(): pl.pallas_call(functools.partial(attend_fwd_kernel, hp, bq, segs * pairs...  122 us
    pallas_call x1, Pallas kernels, input_back(): pl.pallas_call(functools.partial(d_normed_kernel, dp_count, mp_count, vec...  103 us
    pallas_call x1, Pallas kernels, gather_qkv(): pl.pallas_call(functools.partial(qkv_kernel, dp_count, mp_count), in_spec...  89.7 us
    pallas_call x1, Pallas kernels, attend_bwd(): pl.pallas_call(functools.partial(attend_bwd_kernel, hp, bq, segs * pairs...  65.1 us
    pallas_call x1, Pallas kernels, resid_back(): pl.pallas_call(functools.partial(resid_back_kernel, dp_count, mp_count),...  30.4 us
    pallas_call x4, Pallas kernels, shampoo(): pl.pallas_call(functools.partial(shampoo_kernel, group, tc, form), grid=(...  29.8 us
    unnamed x65, local copies, waits for them, and re-layouts  22 us
  transfers between devices with their start and end apart: 6, of which 0 were waited for; matrix products, arithmetic and copies ran while one was open for 1% of the time, Pallas kernels for 65%

profile of v6, /device:TPU:0, one launch (start us, length us, event | category | flops | bytes accessed | tf_op | source)
XLA Modules:
  0.0 676.0 jit_solution(5377656569489336941)
XLA Ops:
  7.2 0.0 copy-start.3
  7.2 0.0 all-gather.3.cloned.1.call-start
  7.2 2.9 convert_element_type.29
  10.1 0.0 all-gather.3.cloned.1.call-update
  10.1 0.0 all-gather.5.cloned.1.call-start
  10.2 1.1 convert_element_type.30
  11.3 0.0 all-gather.5.cloned.1.call-update
  11.3 0.0 reduce-scatter.13.cloned.1.call-start
  12.0 1.7 copy.44
  13.7 0.0 copy-start.6
  13.7 0.1 copy.45
  13.8 0.3 copy.46.w_own
  14.1 0.7 copy-done.6
  14.8 0.3 copy-done
  15.1 0.2 convert_reduce_fusion
  15.3 0.4 fusion.2
  15.8 0.3 copy-done.27
  16.1 1.1 broadcast_select_fusion.up_own
  17.2 0.4 fusion.4.own
  17.6 89.7 %shard_map.319 = (bf16[8,256,2048]{2,1,0:T(8,128)(2,1)}, bf16[2048,256]{1,0:T(8,128)(2,1)S(1)}, bf16[2048,256]{1,0:T(8,128)(2,1)S(1)}, bf16[2048,256]{1,0:T(8,128)(2,1)S(1)}, bf16[3,2048,256]{2,1,0:T(8,128)(2,1)S(1)}) custom-call(bf16[256,2048]{1,0:T(8,128)(2,1)S(1)} %fusion.4.own, bf16[3,512,256]{2,1,0:T(8,128)(2,1)S(1)} %copy.46.w_own), custom_call_target="tpu_custom_call" | custom-call | flops 6442450944 | bytes 293601280 | tf_op jit(solution)/shard_map/pallas_call | solution.py:332
  107.3 0.0 copy-start.23
  107.3 1.7 copy-done.23
  109.0 121.5 %shard_map.320 = (bf16[2048,256]{1,0:T(8,128)(2,1)S(1)}, f32[1,4,8,2048]{3,2,1,0:T(8,128)S(1)}, bf16[8,256,256]{2,1,0:T(8,128)(2,1)S(1)}, bf16[8,256,2048]{2,1,0:T(8,128)(2,1)}, bf16[2,4,2048,256]{3,2,1,0:T(8,128)(2,1)}) custom-call(s32[1]{0:T(128)} %copy.55.len_ref, bf16[2048,256]{1,0:T(8,128)(2,1)S(1)} %get-tuple-element.72.q_ref, ...), custom_call_target="tpu_custom_call" | custom-call | flops 2147483648 | bytes 398458880 | tf_op jit(solution)/shard_map/pallas_call | solution.py:507
  230.6 1.0 copy-done.16
  231.6 3.9 copy-done.1
  235.4 5.6 shard_map.321
  241.1 1.3 copy-done.7
  242.4 1.0 copy-done.22
  243.4 182.5 %shard_map.322 = (f32[256,2048]{1,0:T(8,128)}, bf16[8,256,2048]{2,1,0:T(8,128)(2,1)}, bf16[2,4,256,2048]{3,2,1,0:T(8,128)(2,1)}, bf16[4,256,2048]{2,1,0:T(8,128)...) custom-call(bf16[256,2048]{1,0:T(8,128)(2,1)} %copy-done.22, ...), custom_call_target="tpu_custom_call" | custom-call | flops 51539607552 | bytes 555745280 | tf_op jit(solution)/shard_map/pallas_call | solution.py:1453
  425.8 0.0 reduce-scatter.13.cloned.1.call-update
  425.9 0.0 reduce-scatter.17.cloned.1.call-start
  425.9 30.4 %shard_map.323 = (f32[256,2048]{1,0:T(8,128)}, f32[1,2048]{1,0:T(1,128)}, bf16[8,256,256]{2,1,0:T(8,128)(2,1)}, bf16[4,4,512,256]{3,2,1,0:T(8,128)(2,1)}) custom-call(f32[256,2048]{1,0:T(8,128)} %get-tuple-element.81.dn, f32[256,2048]{1,0:T(8,128)} %copy-done.7, bf16[256,2048]{1,0:T(8,128)(2,1)} %broadcast_select_fusion.up_own, f32[2,2048]{1,0:T(2,128)} %gain.5, ...), custom_call_target="tpu_custom_call" | custom-call | flops 4294967296 | bytes 115343360 | tf_op jit(solution)/shard_map/pallas_call | solution.py:730
  456.3 0.0 reduce-scatter.17.cloned.1.call-update
  456.3 0.0 reduce-scatter.15.cloned.1.call-start
  456.3 65.1 %shard_map.324 = (bf16[2048,256]{1,0:T(8,128)(2,1)}, bf16[2048,256]{1,0:T(8,128)(2,1)}, bf16[2048,256]{1,0:T(8,128)(2,1)}, f32[256,2048]{1,0:T(8,128)}, bf16[4,3,512,256]{3,2,1,0:T(8,128)(2,1)}) custom-call(s32[1]{0:T(128)} %copy.55.len_ref, bf16[2048,256]{1,0:T(8,128)(2,1)} %copy-done.13, bf16[2048,256]{1,0:T(8,128)(2,1)} %copy-done.14, ...), custom_call_target="tpu_custom_call" | custom-call | flops 5368709120 | bytes 272629760 | tf_op jit(solution)/shard_map/pallas_call | solution.py:1136
  521.5 0.0 reduce-scatter.13.cloned.1.call-done
  521.5 0.0 reduce-scatter.15.cloned.1.call-update
  521.5 0.0 reduce-scatter.11.cloned.1.call-start
  521.6 1.4 copy-done.8
  523.1 1.8 add_convert_fusion
  524.9 0.3 convolution_convert_fusion
  525.2 0.7 copy.51
  526.0 103.2 %shard_map.325 = (f32[256,2048]{1,0:T(8,128)}, f32[64,256]{1,0:T(8,128)}, f32[2,2048]{1,0:T(2,128)}, f32[2,2048]{1,0:T(2,128)}) custom-call(bf16[2048,256]{1,0:T(8,128)(2,1)} %get-tuple-element.88.dq, bf16[2048,256]{1,0:T(8,128)(2,1)} %get-tuple-element.89.dk, bf16[2048,256]{1,0:T(8,128)(2,1)} %get-tuple-element.90.dv, bf16[3,2048,256]{2,1,0:T(8,128)(2,1)} %copy-done.23, ...), custom_call_target="tpu_custom_call" | custom-call | flops 6442450944 | bytes 314572800 | tf_op jit(solution)/shard_map/pallas_call | solution.py:996
  629.2 0.0 reduce-scatter.17.cloned.1.call-done
  629.2 0.0 reduce-scatter.15.cloned.1.call-done
  629.2 0.0 reduce-scatter.11.cloned.1.call-update
  629.2 0.8 slice_bitcast_fusion.2
  630.1 0.7 copy.48
  630.8 1.4 copy-done.11
  632.2 1.1 copy-done.17
  633.3 7.0 %shard_map.326 = (f32[512,768]{1,0:T(8,128)}, f32[1,4,512,512]{3,2,1,0:T(8,128)}, f32[1,4,192,192]{3,2,1,0:T(8,128)}, f32[512,768]{1,0:T(8,128)}) custom-call(f32[512,768]{1,0:T(8,128)S(1)} %copy-done.5, bf16[3,512,256]{2,1,0:T(8,128)(2,1)S(1)} %bitcast.28, f32[2,1,4,512,512]{4,3,2,1,0:T(8,128)} %l_ref.4, f32[2,1,4,192,192]{4,3,2,1,0:T(8,128)S(1)} %copy-done.11), custom_call_target="tpu_custom_call" | custom-call | flops 1107296256 | bytes 19857408 | tf_op jit(solution)/shard_map/pallas_call | solution.py:1535
  640.3 0.0 copy-start.2
  640.4 0.0 copy-start.9
  640.4 0.2 slice_bitcast_fusion
  640.5 1.4 copy-done.2
  641.9 0.6 copy-done.9
  642.6 8.5 %shard_map.328 = (f32[512,1024]{1,0:T(8,128)}, f32[1,4,512,512]{3,2,1,0:T(8,128)}, f32[1,4,256,256]{3,2,1,0:T(8,128)}, f32[512,1024]{1,0:T(8,128)}) custom-call(f32[512,1024]{1,0:T(8,128)S(1)} %copy-done.2, bf16[512,1024]{1,0:T(8,128)(2,1)S(1)} %get-tuple-element.187.g_ref, f32[2,1,4,512,512]{4,3,2,1,0:T(8,128)} %l_ref.6, f32[2,1,4,256,256]{4,3,2,1,0:T(8,128)S(1)} %copy-done.9), custom_call_target="tpu_custom_call" | custom-call | flops 1610612736 | bytes 23068672 | tf_op jit(solution)/shard_map/pallas_call | solution.py:1535
  651.1 8.1 %shard_map.329 = (f32[1024,512]{1,0:T(8,128)}, f32[4,1,256,256]{3,2,1,0:T(8,128)}, f32[4,1,512,512]{3,2,1,0:T(8,128)}, f32[1024,512]{1,0:T(8,128)}) custom-call(f32[1024,512]{1,0:T(8,128)S(1)} %copy-done.4, bf16[512,1024]{1,0:T(8,128)(2,1)S(1)} %get-tuple-element.186.g_ref, f32[2,4,1,256,256]{4,3,2,1,0:T(8,128)S(1)} %copy-done.10, f32[2,4,1,512,512]{4,3,2,1,0:T(8,128)} %r_ref.7), custom_call_target="tpu_custom_call" | custom-call | flops 1610612736 | bytes 23068672 | tf_op jit(solution)/shard_map/pallas_call | solution.py:1535
  659.3 0.0 reduce-scatter.11.cloned.1.call-done
  659.3 0.9 copy-done.20
  660.2 6.1 shard_map.327
  666.4 1.3 copy.56
  667.7 0.6 copy.57
  668.3 0.6 copy.58
  (52 shorter events, 0.2 us)
Async XLA Ops:
  7.2 3.0 copy-start.3
  7.2 236.2 %all-gather.3.cloned.1.call-start = ((), (), s32[]{:S(2)}) async-start(), calls=%async_computation.4 | async-start | bytes 5242880 | tf_op jit(solution)/shard_map/all_gather | solution.py:1607
  10.1 233.2 %all-gather.5.cloned.1.call-start = ((), (), s32[]{:S(2)}) async-start(), calls=%async_computation.5 | async-start | bytes 5242880 | tf_op jit(solution)/shard_map/all_gather | solution.py:1608
  11.3 510.2 %reduce-scatter.13.cloned.1.call-start = ((), (), s32[]{:S(2)}) async-start(), calls=%async_computation.7 | async-start | bytes 10485760
  13.7 1.0 copy-start.6
  13.7 1.4 copy-start
  14.8 1.3 copy-start.27
  15.1 2.1 slice-start
  107.3 1.7 copy-start.23
  109.0 121.5 %copy-start.13 = (bf16[2048,256]{1,0:T(8,128)(2,1)}, bf16[2048,256]{1,0:T(8,128)(2,1)S(1)}, u32[]{:S(2)}) copy-start(bf16[2048,256]{1,0:T(8,128)(2,1)S(1)} %get-tuple-element.72.q_ref) | copy-start | bytes 3145732
  109.0 121.6 %copy-start.14 = (bf16[2048,256]{1,0:T(8,128)(2,1)}, bf16[2048,256]{1,0:T(8,128)(2,1)S(1)}, u32[]{:S(2)}) copy-start(bf16[2048,256]{1,0:T(8,128)(2,1)S(1)} %get-tuple-element.73.k_ref) | copy-start | bytes 3145732
  109.0 121.6 %copy-start.15 = (bf16[2048,256]{1,0:T(8,128)(2,1)}, bf16[2048,256]{1,0:T(8,128)(2,1)S(1)}, u32[]{:S(2)}) copy-start(bf16[2048,256]{1,0:T(8,128)(2,1)S(1)} %get-tuple-element.74.v_ref) | copy-start | bytes 3145732
  109.0 122.6 %copy-start.21 = (f32[2,2048]{1,0:T(2,128)S(1)}, f32[2,2048]{1,0:T(2,128)}, u32[]{:S(2)}) copy-start(f32[2,2048]{1,0:T(2,128)} %gain.5) | copy-start | bytes 49156
  230.6 1.0 copy-start.16
  231.5 9.5 %copy-start.12 = (bf16[8,256,256]{2,1,0:T(8,128)(2,1)}, bf16[8,256,256]{2,1,0:T(8,128)(2,1)S(1)}, u32[]{:S(2)}) copy-start(bf16[8,256,256]{2,1,0:T(8,128)(2,1)S(1)} %get-tuple-element.75.ctx) | copy-start | bytes 3145732
  231.5 9.5 %copy-start.18 = (f32[1,4,8,2048]{3,2,1,0:T(8,128)}, f32[1,4,8,2048]{3,2,1,0:T(8,128)S(1)}, u32[]{:S(2)}) copy-start(f32[1,4,8,2048]{3,2,1,0:T(8,128)S(1)} %get-tuple-element.83.lse_ref) | copy-start | bytes 786436
  231.5 3.9 copy-start.1
  241.1 1.3 copy-start.7
  242.4 1.0 copy-start.22
  425.9 203.3 %reduce-scatter.17.cloned.1.call-start = ((), (), s32[]{:S(2)}) async-start(), calls=%async_computation.9 | async-start | bytes 5242880
  456.3 172.9 %reduce-scatter.15.cloned.1.call-start = ((), (), s32[]{:S(2)}) async-start(), calls=%async_computation.8 | async-start | bytes 3932160
  521.5 1.6 copy-start.8
  521.5 137.7 %reduce-scatter.11.cloned.1.call-start = ((), (), s32[]{:S(2)}) async-start(), calls=%async_computation.6 | async-start | bytes 1310720 | tf_op jit(solution)/shard_map/reduce_scatter | solution.py:1665
  524.9 1.1 copy-start.24
  526.0 104.8 %copy-start.5 = (f32[512,768]{1,0:T(8,128)S(1)}, f32[512,768]{1,0:T(8,128)}, u32[]{:S(2)}) copy-start(f32[512,768]{1,0:T(8,128)} %w_ref.4) | copy-start | bytes 4718596
  630.7 1.4 copy-start.11
  632.2 1.1 copy-start.17
  633.3 7.0 %copy-start.25 = (bf16[1,2,512,1024]{3,2,1,0:T(8,128)(2,1)S(1)}, bf16[1,2,512,1024]{3,2,1,0:T(8,128)(2,1)}, u32[]{:S(2)}) copy-start(bf16[1,2,512,1024]{3,2,1,0:T(8,128)(2,1)} %reduce-scatter.13.cloned.1.call-done) | copy-start | bytes 6291460
  640.3 1.6 copy-start.2
  640.4 2.2 copy-start.9
  642.6 8.5 %copy-start.4 = (f32[1024,512]{1,0:T(8,128)S(1)}, f32[1024,512]{1,0:T(8,128)}, u32[]{:S(2)}) copy-start(f32[1024,512]{1,0:T(8,128)} %w_ref.7) | copy-start | bytes 6291460
  642.6 8.5 %copy-start.10 = (f32[2,4,1,256,256]{4,3,2,1,0:T(8,128)S(1)}, f32[2,4,1,256,256]{4,3,2,1,0:T(8,128)}, u32[]{:S(2)}) copy-start(f32[2,4,1,256,256]{4,3,2,1,0:T(8,128)} %l_ref.7) | copy-start | bytes 6291460
  651.1 8.1 %copy-start.19 = (f32[2,1,4,64,64]{4,3,2,1,0:T(8,128)S(1)}, f32[2,1,4,64,64]{4,3,2,1,0:T(8,128)}, u32[]{:S(2)}) copy-start(f32[2,1,4,64,64]{4,3,2,1,0:T(8,128)} %r_ref.5) | copy-start | bytes 393220
  659.3 1.0 copy-start.20
  660.2 6.1 copy-start.26
  666.4 1.3 copy-start.29
  666.4 1.9 copy-start.28
Sparse Core Ops, SparseCore 0:
  10.5 82.1 all-gather.2
  95.1 52.5 all-gather.4
  426.0 89.3 reduce-scatter.12
  518.5 52.7 reduce-scatter.16
  574.1 43.9 reduce-scatter.14
  629.4 27.8 reduce-scatter.10

commit v7 on v6

--- a/solution.py
+++ b/solution.py
@@ -11,6 +11,7 @@
 HD = 64
 SLOT = 2048
 NSUM = 50
+MIN_LEN = 1024
 BLOCK = 512
 FBLK = 256
 
@@ -97,7 +98,7 @@
     ls = [lse_ref[0,h,0:1,:] for h in range(hp)]
     rowk = lax.broadcasted_iota(jnp.int32,(bq,bq),0)
     colq = lax.broadcasted_iota(jnp.int32,(bq,bq),1)
-    def step(j, dq, diag):
+    def step(j, dq, diag, open_keys=False):
         at = pl.ds(pl.multiple_of(j*bq,bq),bq)
         k = k_ref[at,:]; v=v_ref[at,:]
         ok = rowk < limit - j*bq
@@ -105,7 +106,9 @@
         dk=dka[at,:]; dv=dva[at,:]
         for h in range(hp):
             s = dg(k,qs[h],NT)
-            p = jnp.where(ok, jnp.exp(s-ls[h]), 0.0)
+            p = jnp.exp(s-ls[h])
+            if not open_keys:
+                p = jnp.where(ok, p, 0.0)
             dp = dg(v,dos[h],NT)
             ds = (p*(dp-dd[h])).astype(BF)
             dv = dv + dg(p.astype(BF),dos[h],NN)
@@ -113,7 +116,10 @@
             dq = dq + dg(ds, jnp.where(masks[h],k,jnp.zeros_like(k)), TN)
         dka[at,:]=dk; dva[at,:]=dv
         return dq
-    dq = lax.fori_loop(0,i,lambda j,c: step(j,c,False), jnp.zeros((bq,width),F32))
+    whole = jnp.minimum(i, MIN_LEN // bq)
+    dq = jnp.zeros((bq,width),F32)
+    dq = lax.fori_loop(0,whole,lambda j,c: step(j,c,False,True), dq)
+    dq = lax.fori_loop(whole,i,lambda j,c: step(j,c,False), dq)
     dq = step(i,dq,True)
     dq_ref[...] = (dq*0.125).astype(BF)
     @pl.when(i==nb-1)
@@ -1044,13 +1050,15 @@
     tiles = features // span
 
     def both(chip, ref, other):
-        first = local(part.at[0, chip], ref, io_sem.at[0])
-        second = local(part.at[1, chip], other, io_sem.at[1])
-        first.wait()
+        second = local(part.at[1, chip], other, io_sem.at[line.n])
+        own_terms(chip).wait()
         second.wait()
 
+    def own_terms(chip):
+        return pltpu.make_async_copy(part.at[0, chip], scatter.both.at[chip], io_sem.at[chip])
+
     def from_far(chip, way):
-        local(far_in.at[way], scatter.slots.at[chip], io_sem.at[0]).wait()
+        local(far_in.at[way], scatter.slots.at[chip], io_sem.at[line.n]).wait()
         scatter.add(chip, lambda at: scatter.slots[chip, at, :].astype(F32))
         slot = line.n if way == 1 and far == 2 else chip
         scatter.onward(chip, slot, way, far - 1).start()
@@ -1066,6 +1074,9 @@
 
     @pl.when(flat == 0)
     def _():
+        for chip in range(line.n):
+            near = (chip - line.chip < far) & (line.chip - chip < far)
+            pl.when(near)(lambda chip=chip: own_terms(chip).start())
         line.greet()
         for away in range(far - 1, 0, -1):
             scatter.produce(away, both)
@@ -1168,7 +1179,7 @@
             pltpu.VMEM((3, total, hw), BF),
             pltpu.VMEM((2, mp_count, rows, span), BF),
             pltpu.VMEM((3, span, hw), BF),
-            DMA((2,)),
+            DMA((mp_count // 2 + 1,)),
             DMA((3,)),
             *scatter_scratch(mp_count, rows, features),
         ],

time: 685 us -> 679 us (level)
  no operation moved by 1% of the time
where the time goes in v7:
time: 679 us; the launch traced here: 675 us
  Pallas kernels  627 us (92%)
  local copies, waits for them, and re-layouts  24 us (4%)
  between operations  15.4 us (2%)
  other arithmetic  8.01 us (1%)
    pallas_call x1, Pallas kernels, ffn(): pl.pallas_call(functools.partial(ffn_kernel, mp_count), in_specs=[HBM, HB...  182 us
    pallas_call x1, Pallas kernels, attend_fwd(): pl.pallas_call(functools.partial(attend_fwd_kernel, hp, bq, segs * pairs...  122 us
    pallas_call x1, Pallas kernels, input_back(): pl.pallas_call(functools.partial(d_normed_kernel, dp_count, mp_count, vec...  103 us
    pallas_call x1, Pallas kernels, gather_qkv(): pl.pallas_call(functools.partial(qkv_kernel, dp_count, mp_count), in_spec...  89.7 us
    pallas_call x1, Pallas kernels, attend_bwd(): pl.pallas_call(functools.partial(attend_bwd_kernel, hp, bq, segs * pairs...  64.1 us
    pallas_call x1, Pallas kernels, resid_back(): pl.pallas_call(functools.partial(resid_back_kernel, dp_count, mp_count),...  30.4 us
    pallas_call x4, Pallas kernels, shampoo(): pl.pallas_call(functools.partial(shampoo_kernel, group, tc, form), grid=(...  29.8 us
    unnamed x65, local copies, waits for them, and re-layouts  22 us
  transfers between devices with their start and end apart: 6, of which 0 were waited for; matrix products, arithmetic and copies ran while one was open for 1% of the time, Pallas kernels for 65%

profile of v7, /device:TPU:0, one launch (start us, length us, event | category | flops | bytes accessed | tf_op | source)
XLA Modules:
  0.0 674.7 jit_solution(13144496985438573155)
XLA Ops:
  7.2 0.0 copy-start.3
  7.2 0.0 all-gather.3.cloned.1.call-start
  7.2 2.9 convert_element_type.29
  10.1 0.0 all-gather.3.cloned.1.call-update
  10.1 0.0 all-gather.5.cloned.1.call-start
  10.2 1.1 convert_element_type.30
  11.3 0.0 all-gather.5.cloned.1.call-update
  11.3 0.0 reduce-scatter.13.cloned.1.call-start
  12.0 1.7 copy.44
  13.7 0.0 copy-start.6
  13.7 0.0 copy-start
  13.7 0.1 copy.45
  13.8 0.3 copy.46.w_own
  14.1 0.7 copy-done.6
  14.8 0.0 copy-start.27
  14.8 0.3 copy-done
  15.1 0.2 convert_reduce_fusion
  15.3 0.4 fusion.2
  15.8 0.3 copy-done.27
  16.1 1.1 broadcast_select_fusion.up_own
  17.2 0.4 fusion.4.own
  17.6 89.7 %shard_map.319 = (bf16[8,256,2048]{2,1,0:T(8,128)(2,1)}, bf16[2048,256]{1,0:T(8,128)(2,1)S(1)}, bf16[2048,256]{1,0:T(8,128)(2,1)S(1)}, bf16[2048,256]{1,0:T(8,128)(2,1)S(1)}, bf16[3,2048,256]{2,1,0:T(8,128)(2,1)S(1)}) custom-call(bf16[256,2048]{1,0:T(8,128)(2,1)S(1)} %fusion.4.own, bf16[3,512,256]{2,1,0:T(8,128)(2,1)S(1)} %copy.46.w_own), custom_call_target="tpu_custom_call" | custom-call | flops 6442450944 | bytes 293601280 | tf_op jit(solution)/shard_map/pallas_call | solution.py:338
  107.3 0.0 copy-start.23
  107.3 1.7 copy-done.23
  109.0 121.5 %shard_map.320 = (bf16[2048,256]{1,0:T(8,128)(2,1)S(1)}, f32[1,4,8,2048]{3,2,1,0:T(8,128)S(1)}, bf16[8,256,256]{2,1,0:T(8,128)(2,1)S(1)}, bf16[8,256,2048]{2,1,0:T(8,128)(2,1)}, bf16[2,4,2048,256]{3,2,1,0:T(8,128)(2,1)}) custom-call(s32[1]{0:T(128)} %copy.55.len_ref, bf16[2048,256]{1,0:T(8,128)(2,1)S(1)} %get-tuple-element.72.q_ref, ...), custom_call_target="tpu_custom_call" | custom-call | flops 2147483648 | bytes 398458880 | tf_op jit(solution)/shard_map/pallas_call | solution.py:513
  230.6 1.0 copy-done.16
  231.6 3.9 copy-done.1
  235.4 5.6 shard_map.321
  241.1 1.3 copy-done.7
  242.4 1.0 copy-done.22
  243.4 182.5 %shard_map.322 = (f32[256,2048]{1,0:T(8,128)}, bf16[8,256,2048]{2,1,0:T(8,128)(2,1)}, bf16[2,4,256,2048]{3,2,1,0:T(8,128)(2,1)}, bf16[4,256,2048]{2,1,0:T(8,128)...) custom-call(bf16[256,2048]{1,0:T(8,128)(2,1)} %copy-done.22, ...), custom_call_target="tpu_custom_call" | custom-call | flops 51539607552 | bytes 555745280 | tf_op jit(solution)/shard_map/pallas_call | solution.py:1464
  425.8 0.0 reduce-scatter.13.cloned.1.call-update
  425.9 0.0 reduce-scatter.17.cloned.1.call-start
  425.9 30.4 %shard_map.323 = (f32[256,2048]{1,0:T(8,128)}, f32[1,2048]{1,0:T(1,128)}, bf16[8,256,256]{2,1,0:T(8,128)(2,1)}, bf16[4,4,512,256]{3,2,1,0:T(8,128)(2,1)}) custom-call(f32[256,2048]{1,0:T(8,128)} %get-tuple-element.81.dn, f32[256,2048]{1,0:T(8,128)} %copy-done.7, bf16[256,2048]{1,0:T(8,128)(2,1)} %broadcast_select_fusion.up_own, f32[2,2048]{1,0:T(2,128)} %gain.5, ...), custom_call_target="tpu_custom_call" | custom-call | flops 4294967296 | bytes 115343360 | tf_op jit(solution)/shard_map/pallas_call | solution.py:736
  456.3 0.0 reduce-scatter.17.cloned.1.call-update
  456.3 0.0 reduce-scatter.15.cloned.1.call-start
  456.3 64.1 %shard_map.324 = (bf16[2048,256]{1,0:T(8,128)(2,1)}, bf16[2048,256]{1,0:T(8,128)(2,1)}, bf16[2048,256]{1,0:T(8,128)(2,1)}, f32[256,2048]{1,0:T(8,128)}, bf16[4,3,512,256]{3,2,1,0:T(8,128)(2,1)}) custom-call(s32[1]{0:T(128)} %copy.55.len_ref, bf16[2048,256]{1,0:T(8,128)(2,1)} %copy-done.13, bf16[2048,256]{1,0:T(8,128)(2,1)} %copy-done.14, ...), custom_call_target="tpu_custom_call" | custom-call | flops 5368709120 | bytes 272629760 | tf_op jit(solution)/shard_map/pallas_call | solution.py:1147
  520.4 0.0 reduce-scatter.13.cloned.1.call-done
  520.4 0.0 reduce-scatter.15.cloned.1.call-update
  520.5 0.0 reduce-scatter.11.cloned.1.call-start
  520.6 1.4 copy-done.8
  522.0 1.8 add_convert_fusion
  523.8 0.3 convolution_convert_fusion
  524.2 0.7 copy.51
  524.9 103.0 %shard_map.325 = (f32[256,2048]{1,0:T(8,128)}, f32[64,256]{1,0:T(8,128)}, f32[2,2048]{1,0:T(2,128)}, f32[2,2048]{1,0:T(2,128)}) custom-call(bf16[2048,256]{1,0:T(8,128)(2,1)} %get-tuple-element.88.dq, bf16[2048,256]{1,0:T(8,128)(2,1)} %get-tuple-element.89.dk, bf16[2048,256]{1,0:T(8,128)(2,1)} %get-tuple-element.90.dv, bf16[3,2048,256]{2,1,0:T(8,128)(2,1)} %copy-done.23, ...), custom_call_target="tpu_custom_call" | custom-call | flops 6442450944 | bytes 314572800 | tf_op jit(solution)/shard_map/pallas_call | solution.py:1002
  627.9 0.0 reduce-scatter.17.cloned.1.call-done
  628.0 0.0 reduce-scatter.15.cloned.1.call-done
  628.0 0.0 reduce-scatter.11.cloned.1.call-update
  628.0 0.8 slice_bitcast_fusion.2
  628.9 0.7 copy.48
  629.5 1.4 copy-done.11
  630.9 1.1 copy-done.17
  632.1 7.0 %shard_map.326 = (f32[512,768]{1,0:T(8,128)}, f32[1,4,512,512]{3,2,1,0:T(8,128)}, f32[1,4,192,192]{3,2,1,0:T(8,128)}, f32[512,768]{1,0:T(8,128)}) custom-call(f32[512,768]{1,0:T(8,128)S(1)} %copy-done.5, bf16[3,512,256]{2,1,0:T(8,128)(2,1)S(1)} %bitcast.28, f32[2,1,4,512,512]{4,3,2,1,0:T(8,128)} %l_ref.4, f32[2,1,4,192,192]{4,3,2,1,0:T(8,128)S(1)} %copy-done.11), custom_call_target="tpu_custom_call" | custom-call | flops 1107296256 | bytes 19857408 | tf_op jit(solution)/shard_map/pallas_call | solution.py:1546
  639.1 0.2 slice_bitcast_fusion
  639.3 1.4 copy-done.2
  640.7 0.6 copy-done.9
  641.4 8.5 %shard_map.328 = (f32[512,1024]{1,0:T(8,128)}, f32[1,4,512,512]{3,2,1,0:T(8,128)}, f32[1,4,256,256]{3,2,1,0:T(8,128)}, f32[512,1024]{1,0:T(8,128)}) custom-call(f32[512,1024]{1,0:T(8,128)S(1)} %copy-done.2, bf16[512,1024]{1,0:T(8,128)(2,1)S(1)} %get-tuple-element.187.g_ref, f32[2,1,4,512,512]{4,3,2,1,0:T(8,128)} %l_ref.6, f32[2,1,4,256,256]{4,3,2,1,0:T(8,128)S(1)} %copy-done.9), custom_call_target="tpu_custom_call" | custom-call | flops 1610612736 | bytes 23068672 | tf_op jit(solution)/shard_map/pallas_call | solution.py:1546
  649.9 8.1 %shard_map.329 = (f32[1024,512]{1,0:T(8,128)}, f32[4,1,256,256]{3,2,1,0:T(8,128)}, f32[4,1,512,512]{3,2,1,0:T(8,128)}, f32[1024,512]{1,0:T(8,128)}) custom-call(f32[1024,512]{1,0:T(8,128)S(1)} %copy-done.4, bf16[512,1024]{1,0:T(8,128)(2,1)S(1)} %get-tuple-element.186.g_ref, f32[2,4,1,256,256]{4,3,2,1,0:T(8,128)S(1)} %copy-done.10, f32[2,4,1,512,512]{4,3,2,1,0:T(8,128)} %r_ref.7), custom_call_target="tpu_custom_call" | custom-call | flops 1610612736 | bytes 23068672 | tf_op jit(solution)/shard_map/pallas_call | solution.py:1546
  658.0 0.0 reduce-scatter.11.cloned.1.call-done
  658.1 0.9 copy-done.20
  659.0 6.1 shard_map.327
  665.2 1.3 copy.56
  666.5 0.6 copy.57
  667.1 0.6 copy.58
  (52 shorter events, 0.2 us)
Async XLA Ops:
  7.2 3.0 copy-start.3
  7.2 236.2 %all-gather.3.cloned.1.call-start = ((), (), s32[]{:S(2)}) async-start(), calls=%async_computation.4 | async-start | bytes 5242880 | tf_op jit(solution)/shard_map/all_gather | solution.py:1618
  10.1 233.2 %all-gather.5.cloned.1.call-start = ((), (), s32[]{:S(2)}) async-start(), calls=%async_computation.5 | async-start | bytes 5242880 | tf_op jit(solution)/shard_map/all_gather | solution.py:1619
  11.3 509.1 %reduce-scatter.13.cloned.1.call-start = ((), (), s32[]{:S(2)}) async-start(), calls=%async_computation.7 | async-start | bytes 10485760
  13.7 1.0 copy-start.6
  13.7 1.4 copy-start
  14.8 1.3 copy-start.27
  15.1 2.1 slice-start
  107.3 1.7 copy-start.23
  109.0 121.5 %copy-start.13 = (bf16[2048,256]{1,0:T(8,128)(2,1)}, bf16[2048,256]{1,0:T(8,128)(2,1)S(1)}, u32[]{:S(2)}) copy-start(bf16[2048,256]{1,0:T(8,128)(2,1)S(1)} %get-tuple-element.72.q_ref) | copy-start | bytes 3145732
  109.0 121.6 %copy-start.14 = (bf16[2048,256]{1,0:T(8,128)(2,1)}, bf16[2048,256]{1,0:T(8,128)(2,1)S(1)}, u32[]{:S(2)}) copy-start(bf16[2048,256]{1,0:T(8,128)(2,1)S(1)} %get-tuple-element.73.k_ref) | copy-start | bytes 3145732
  109.0 121.6 %copy-start.15 = (bf16[2048,256]{1,0:T(8,128)(2,1)}, bf16[2048,256]{1,0:T(8,128)(2,1)S(1)}, u32[]{:S(2)}) copy-start(bf16[2048,256]{1,0:T(8,128)(2,1)S(1)} %get-tuple-element.74.v_ref) | copy-start | bytes 3145732
  109.0 122.6 %copy-start.21 = (f32[2,2048]{1,0:T(2,128)S(1)}, f32[2,2048]{1,0:T(2,128)}, u32[]{:S(2)}) copy-start(f32[2,2048]{1,0:T(2,128)} %gain.5) | copy-start | bytes 49156
  230.6 1.0 copy-start.16
  231.5 9.5 %copy-start.12 = (bf16[8,256,256]{2,1,0:T(8,128)(2,1)}, bf16[8,256,256]{2,1,0:T(8,128)(2,1)S(1)}, u32[]{:S(2)}) copy-start(bf16[8,256,256]{2,1,0:T(8,128)(2,1)S(1)} %get-tuple-element.75.ctx) | copy-start | bytes 3145732
  231.5 9.5 %copy-start.18 = (f32[1,4,8,2048]{3,2,1,0:T(8,128)}, f32[1,4,8,2048]{3,2,1,0:T(8,128)S(1)}, u32[]{:S(2)}) copy-start(f32[1,4,8,2048]{3,2,1,0:T(8,128)S(1)} %get-tuple-element.83.lse_ref) | copy-start | bytes 786436
  231.5 3.9 copy-start.1
  241.1 1.3 copy-start.7
  242.4 1.0 copy-start.22
  425.9 202.1 %reduce-scatter.17.cloned.1.call-start = ((), (), s32[]{:S(2)}) async-start(), calls=%async_computation.9 | async-start | bytes 5242880
  456.3 171.7 %reduce-scatter.15.cloned.1.call-start = ((), (), s32[]{:S(2)}) async-start(), calls=%async_computation.8 | async-start | bytes 3932160
  520.4 1.6 copy-start.8
  520.5 137.6 %reduce-scatter.11.cloned.1.call-start = ((), (), s32[]{:S(2)}) async-start(), calls=%async_computation.6 | async-start | bytes 1310720 | tf_op jit(solution)/shard_map/reduce_scatter | solution.py:1676
  523.8 1.1 copy-start.24
  524.9 104.6 %copy-start.5 = (f32[512,768]{1,0:T(8,128)S(1)}, f32[512,768]{1,0:T(8,128)}, u32[]{:S(2)}) copy-start(f32[512,768]{1,0:T(8,128)} %w_ref.4) | copy-start | bytes 4718596
  629.5 1.4 copy-start.11
  630.9 1.1 copy-start.17
  632.1 7.0 %copy-start.25 = (bf16[1,2,512,1024]{3,2,1,0:T(8,128)(2,1)S(1)}, bf16[1,2,512,1024]{3,2,1,0:T(8,128)(2,1)}, u32[]{:S(2)}) copy-start(bf16[1,2,512,1024]{3,2,1,0:T(8,128)(2,1)} %reduce-scatter.13.cloned.1.call-done) | copy-start | bytes 6291460
  639.1 1.6 copy-start.2
  639.1 2.2 copy-start.9
  641.4 8.5 %copy-start.4 = (f32[1024,512]{1,0:T(8,128)S(1)}, f32[1024,512]{1,0:T(8,128)}, u32[]{:S(2)}) copy-start(f32[1024,512]{1,0:T(8,128)} %w_ref.7) | copy-start | bytes 6291460
  641.4 8.5 %copy-start.10 = (f32[2,4,1,256,256]{4,3,2,1,0:T(8,128)S(1)}, f32[2,4,1,256,256]{4,3,2,1,0:T(8,128)}, u32[]{:S(2)}) copy-start(f32[2,4,1,256,256]{4,3,2,1,0:T(8,128)} %l_ref.7) | copy-start | bytes 6291460
  649.9 8.1 %copy-start.19 = (f32[2,1,4,64,64]{4,3,2,1,0:T(8,128)S(1)}, f32[2,1,4,64,64]{4,3,2,1,0:T(8,128)}, u32[]{:S(2)}) copy-start(f32[2,1,4,64,64]{4,3,2,1,0:T(8,128)} %r_ref.5) | copy-start | bytes 393220
  658.1 1.0 copy-start.20
  659.0 6.1 copy-start.26
  665.1 1.3 copy-start.29
  665.1 1.9 copy-start.28
Sparse Core Ops, SparseCore 0:
  10.5 82.1 all-gather.2
  95.1 52.5 all-gather.4
  426.0 89.3 reduce-scatter.12
  518.5 52.6 reduce-scatter.16
  574.0 43.9 reduce-scatter.14
  628.1 27.9 reduce-scatter.10
